TPU v7x, 32 devices: a whole 2x2x4 slice. The times are simulated.
32 devices in a mesh: tile: 16 (over z, y, core), freq: 2 (over x).
Axes of the slice: x: 2, y: 2, z: 4, core: 2. Of those that a mesh axis runs over, the one named last changes fastest.
Arguments:
- visibilities: float32 [2, 2048, 2, 128], P('freq', 'tile'), may hold values from -6 to 6
- uv_cell: int32 [2, 2048, 2, 128], P('freq', 'tile'), may hold values from 0 to 120
- sub_pixel: int32 [2, 2048, 2, 128], P('freq', 'tile'), may hold values from 0 to 7
- w_plane: int32 [2, 2048], P('freq', 'tile'), may hold values from 0 to 15
- block_tile: int32 [2, 2048], P('freq', 'tile'), may hold values from 0 to 31, as said below
- model_grid: bfloat16 [2, 32, 128, 256], P('freq', 'tile'), may hold values from -3 to 3
- kernel_table: bfloat16 [16, 8, 8], replicated, may hold values from 0.049804688 to 1
- coupling: float32 [2, 2], replicated, may hold values from -4 to 4
Outputs:
- residuals: float32 [2, 2048, 2, 128], P('freq', 'tile')
- coupled_grid: float32 [2, 32, 128, 256], P('freq', 'tile')
Inputs may be any that keep to these rules, and one draw needn't show every extreme that they name: `block_tile`: among the 128 blocks of one plane on one device (aligned blocks), at most 24 have tiles of one owner, the owner of tile k being k // 2; in every plane some owner gets exactly 24 blocks from every device.
All inputs are finite; a program needn't handle non-finite values.
Results may differ from a plain program's by a relative error of at most 0.0034.
Values may be sent and summed in bfloat16 or wider, within the bound.
No kernel may reach another device: no remote copies, remote signals or barrier semaphores. Data moves between devices by JAX's collectives and lax.ppermute only.
A program may use at most 64 MiB of HBM per device.

v0:
```python
import jax
import jax.numpy as jnp
from jax import lax
from jax.experimental import pallas as pl
from jax.experimental.pallas import tpu as pltpu
from jax.sharding import PartitionSpec as P

UNROLL = 4
VMEM = pl.BlockSpec(memory_space=pltpu.VMEM)
SMEM = pl.BlockSpec(memory_space=pltpu.SMEM)
ANY = pl.BlockSpec(memory_space=pl.ANY)
PARAMS = pltpu.CompilerParams(vmem_limit_bytes=32 * 1024 * 1024)
TILE_CODE = 4096
PLANE_CODE = 65536


def pack_kernel(pairs, capacity, tiles_here, planes, plane_ref, tile_ref, vis_hbm, cell_hbm, sub_hbm,
                sent_ref, slot_ref, vis_ref, cell_ref, sub_ref, about_ref, count_ref, load_sem, about_sem):
    blocks = tile_ref.shape[0]
    loads = [
        pltpu.make_async_copy(source, target, load_sem.at[i])
        for i, (source, target) in enumerate(
            [(vis_hbm, vis_ref), (cell_hbm, cell_ref), (sub_hbm, sub_ref)]
        )
    ]
    for copy in loads:
        copy.start()
    part = lax.broadcasted_iota(jnp.int32, (4, 128), 0)
    empty = jnp.where(part == 0, float(planes * PLANE_CODE), 0.0)
    abouts = [d * (capacity + 1) + capacity for d in range(pairs)]
    for d in range(pairs):
        sent_ref[d * (capacity + 1)] = jnp.zeros((4, 128), jnp.float32)
        sent_ref[abouts[d]] = empty
        count_ref[d] = 0
    fills = [
        pltpu.make_async_copy(sent_ref.at[abouts[d]], about_ref.at[d], about_sem.at[d])
        for d in range(pairs)
    ]
    for copy in fills:
        copy.start()
    for copy in fills + loads:
        copy.wait()

    def one_block(b):
        tile = tile_ref[b]
        owner = lax.div(tile, tiles_here)
        high = (owner >= pairs).astype(jnp.int32)
        pair = owner - high * pairs
        local = tile - (owner - high) * tiles_here
        place = count_ref[pair]
        count_ref[pair] = place + 1
        slot_ref[b] = pair * capacity + place
        code = (plane_ref[b] * PLANE_CODE + local * TILE_CODE).astype(jnp.float32)
        about_ref[pair, 0, place] = code
        position = (cell_ref[b] * 8 + sub_ref[b]).astype(jnp.float32)
        sent_ref[pair * (capacity + 1) + place] = jnp.concatenate([vis_ref[b], position], axis=0)

    def step(turn, carry):
        for which in range(8):
            one_block(turn * 8 + which)
        return carry

    lax.fori_loop(0, blocks // 8, step, 0)
    for d in range(pairs):
        about_ref[d, 1, 0] = count_ref[d].astype(jnp.float32)
    returns = [
        pltpu.make_async_copy(about_ref.at[d], sent_ref.at[abouts[d]], about_sem.at[d])
        for d in range(pairs)
    ]
    for copy in returns:
        copy.start()
    for copy in returns:
        copy.wait()


def spread_parts(position, table_row):
    position = jnp.broadcast_to(position, (16, 128))
    delta = lax.broadcasted_iota(jnp.int32, (16, 128), 0) - (position >> 3)
    index = (delta & 15) + ((position & 7) << 4)
    table = jnp.broadcast_to(table_row, (8, 128))
    taps = jnp.concatenate(
        [
            jnp.take_along_axis(table, index[:8], axis=1, mode="promise_in_bounds"),
            jnp.take_along_axis(table, index[8:], axis=1, mode="promise_in_bounds"),
        ],
        axis=0,
    )
    return taps, (15 - delta) >> 4


def grid_kernel(pairs, capacity, member_ref, got_ref, table_ref, model_ref, residual_ref, own_ref,
                other_ref, turned_ref, grid_ref, row_ref, partial_ref, code_ref, about_ref, list_ref, sem):
    tiles, side, wide = model_ref.shape
    groups = side // 16
    zero_row = table_ref.shape[0] - 8
    lane = lax.broadcasted_iota(jnp.int32, (1, 128), 1)
    for s in range(pairs):
        about = got_ref[s * (capacity + 1) + capacity].astype(jnp.int32)
        code_ref[s, 0:1, :] = about[0:1] + (lane + s * capacity)
        code_ref[s, 1:2, :] = about[1:2]
    fill = pltpu.make_async_copy(code_ref, about_ref, sem)
    fill.start()
    for t in range(tiles):
        turned_ref[t] = model_ref[t].T
    grid_ref[...] = jnp.zeros_like(grid_ref)
    fill.wait()

    total = jnp.int32(0)
    for s in range(pairs):
        total = total + about_ref[s, 1, 0]
    spare = jnp.where(total == 0, UNROLL, lax.rem(UNROLL - lax.rem(total, UNROLL), UNROLL))
    for u in range(UNROLL):
        list_ref[u] = zero_row * PLANE_CODE

    def enlist(s, filled):
        for k in range(capacity):
            list_ref[filled + k] = about_ref[s, 0, k]
        return filled + about_ref[s, 1, 0]

    lax.fori_loop(0, pairs, enlist, spare)
    chunks = lax.div(total + spare, UNROLL)
    zero = jnp.zeros((16, 128), jnp.bfloat16)

    def read(which):
        entry = list_ref[which]
        slot = entry & (TILE_CODE - 1)
        tile = lax.div(entry, TILE_CODE) & 15
        table_row = table_ref[pl.ds(lax.div(entry, PLANE_CODE), 1), :]
        return slot, tile, table_row, got_ref[slot + lax.div(slot, capacity)]

    def front(which, u):
        _, tile, table_row, data = read(which)
        taps, group = spread_parts(data[2:3].astype(jnp.int32), table_row)
        taps = taps.astype(jnp.bfloat16)
        group = group.astype(jnp.float32).astype(jnp.bfloat16)
        row_matrix = jnp.concatenate(
            [jnp.where(group == k, taps, zero) for k in range(groups)], axis=0
        )
        row_ref[u] = row_matrix
        partial_ref[u] = jnp.dot(turned_ref[tile], row_matrix, preferred_element_type=jnp.float32)

    def back(which, u):
        slot, tile, table_row, data = read(which)
        taps, group = spread_parts(data[3:4].astype(jnp.int32), table_row)
        residuals, samples = [], []
        for part in range(2):
            picked = jnp.zeros((16, 128), jnp.float32)
            for k in range(groups):
                low = part * side + 16 * k
                picked = jnp.where(group == k, partial_ref[u, low : low + 16], picked)
            model = jnp.sum(picked * taps, axis=0, keepdims=True)
            residual = data[part : part + 1] - model
            residuals.append(residual)
            samples.append((residual * taps).astype(jnp.bfloat16))
        residual_ref[slot] = jnp.concatenate(residuals, axis=0).astype(jnp.bfloat16)
        group = group.astype(jnp.float32).astype(jnp.bfloat16)
        weighted = jnp.concatenate(
            [
                jnp.where(group == k, samples[part], zero)
                for part in range(2)
                for k in range(groups)
            ],
            axis=0,
        )
        grid_ref[tile] += lax.dot_general(
            row_ref[u],
            weighted,
            (((1,), (1,)), ((), ())),
            preferred_element_type=jnp.float32,
        )

    def step(turn, carry):
        for u in range(UNROLL):
            back((turn - 1) * UNROLL + u, u)
        for u in range(UNROLL):
            front(turn * UNROLL + u, u)
        return carry

    for u in range(UNROLL):
        front(u, u)
    lax.fori_loop(1, chunks, step, 0)
    for u in range(UNROLL):
        back((chunks - 1) * UNROLL + u, u)
    half = tiles // 2
    member = member_ref[0]
    for t in range(half):
        own_ref[t] = grid_ref[member * half + t]
        other_ref[t] = grid_ref[(1 - member) * half + t].astype(jnp.bfloat16)


def body(visibilities, uv_cell, sub_pixel, w_plane, block_tile, model_grid, kernel_table, coupling):
    owners = lax.axis_size("tile")
    pairs = owners // 2
    _, blocks, _, rows = visibilities.shape
    capacity = 2 * (3 * blocks // owners)
    _, tiles_here, side, wide = model_grid.shape
    planes, oversample, support = kernel_table.shape
    slots = pairs * capacity
    member = lax.axis_index("tile") // pairs
    swap = [(t, (t + pairs) % owners) for t in range(owners)]
    halves = [list(range(pairs)), list(range(pairs, owners))]

    model_own = model_grid[0]
    model_other = lax.ppermute(model_own, "tile", swap)
    sent, slot = pl.pallas_call(
        lambda *refs: pack_kernel(pairs, capacity, tiles_here, planes, *refs),
        out_shape=(
            jax.ShapeDtypeStruct((slots + pairs, 4, rows), jnp.float32),
            jax.ShapeDtypeStruct((blocks,), jnp.int32),
        ),
        in_specs=[SMEM, SMEM, ANY, ANY, ANY],
        out_specs=(VMEM, SMEM),
        scratch_shapes=[
            pltpu.VMEM((blocks, 2, rows), jnp.float32),
            pltpu.VMEM((blocks, 2, rows), jnp.int32),
            pltpu.VMEM((blocks, 2, rows), jnp.int32),
            pltpu.SMEM((pairs, 4, rows), jnp.float32),
            pltpu.SMEM((pairs,), jnp.int32),
            pltpu.SemaphoreType.DMA((3,)),
            pltpu.SemaphoreType.DMA((pairs,)),
        ],
        compiler_params=PARAMS,
        name="pack_blocks",
    )(w_plane[0], block_tile[0], visibilities[0], uv_cell[0], sub_pixel[0])
    sent, model_other = lax.optimization_barrier((sent, model_other))
    got = lax.all_to_all(
        sent, "tile", split_axis=0, concat_axis=0, tiled=True, axis_index_groups=halves
    )
    model = jnp.where(
        member == 0,
        jnp.concatenate([model_own, model_other]),
        jnp.concatenate([model_other, model_own]),
    )
    table = jnp.pad(
        kernel_table.astype(jnp.float32), ((0, 8), (0, 0), (0, 16 - support))
    ).reshape(planes + 8, 16 * oversample)
    residual, own, other = pl.pallas_call(
        lambda *refs: grid_kernel(pairs, capacity, *refs),
        out_shape=(
            jax.ShapeDtypeStruct((slots, 2, rows), jnp.bfloat16),
            jax.ShapeDtypeStruct((tiles_here, side, wide), jnp.float32),
            jax.ShapeDtypeStruct((tiles_here, side, wide), jnp.bfloat16),
        ),
        in_specs=[SMEM, VMEM, VMEM, VMEM],
        out_specs=(VMEM, VMEM, VMEM),
        scratch_shapes=[
            pltpu.VMEM((2 * tiles_here, wide, side), jnp.bfloat16),
            pltpu.VMEM((2 * tiles_here, side, wide), jnp.float32),
            pltpu.VMEM((UNROLL, side, rows), jnp.bfloat16),
            pltpu.VMEM((UNROLL, wide, rows), jnp.float32),
            pltpu.VMEM((pairs, 2, rows), jnp.int32),
            pltpu.SMEM((pairs, 2, rows), jnp.int32),
            pltpu.SMEM((slots + capacity + 2 * UNROLL,), jnp.int32),
            pltpu.SemaphoreType.DMA,
        ],
        compiler_params=PARAMS,
        name="grid_blocks",
    )(member[None], got, table, model)

    returned = lax.all_to_all(
        residual, "tile", split_axis=0, concat_axis=0, tiled=True, axis_index_groups=halves
    )
    residuals = jnp.take(returned, slot, axis=0, mode="clip").astype(jnp.float32)[None]
    grid_sum = own + lax.ppermute(other, "tile", swap).astype(jnp.float32)
    grid_rounded = grid_sum.astype(jnp.bfloat16)[None]
    own_row = lax.dynamic_index_in_dim(coupling, lax.axis_index("freq"), 0, keepdims=False)
    coupled_grid = jnp.sum(
        own_row[:, None, None, None]
        * lax.all_gather(grid_rounded, "freq", axis=0, tiled=True).astype(jnp.float32),
        axis=0,
    )[None]
    return (residuals, coupled_grid)


def solution(mesh):
    return jax.shard_map(
        body,
        mesh=mesh,
        in_specs=(
            P("freq", "tile", None, None),
            P("freq", "tile", None, None),
            P("freq", "tile", None, None),
            P("freq", "tile"),
            P("freq", "tile"),
            P("freq", "tile", None, None),
            P(),
            P(),
        ),
        out_specs=(P("freq", "tile", None, None), P("freq", "tile", None, None)),
        check_vma=False,
    )
```

profile of v0, /device:TPU:0, one launch (start us, length us, event | category | flops | bytes accessed | tf_op | source)
XLA Modules:
  0.0 67.1 jit_solution(5322489103640085724)
XLA Ops:
  0.6 0.0 copy-start
  0.6 4.1 %collective-permute-start = (bf16[2,128,256]{2,1,0:T(8,128)(2,1)}, bf16[2,128,256]{2,1,0:T(8,128)(2,1)S(1)}, u32[]{:S(2)}, u32[]{:S(2)}) collective-permute-start(bf16[2,128,256]{2,1,0:T(8,128)(2,1)} %bitcast.25), channel_id=1, source_target_pairs={{0,16},{2,18},{4,20},{6,22},{8,24},{10,26},{12,28},{14,30},{16,0},... | collective-permute-start | bytes 393224 | tf_op jit(solution)/shard_map/ppermute | solution.py:204
  4.7 0.0 copy-start.4
  4.8 0.0 copy-start.5
  4.8 0.7 copy-done.4
  5.4 0.0 copy-done.5
  5.4 0.0 copy-start.1
  5.4 0.9 %copy-done.1 = f32[1,128,2,128]{3,2,1,0:T(2,128)S(1)} copy-done((f32[1,128,2,128]{3,2,1,0:T(2,128)S(1)}, f32[1,128,2,128]{3,2,1,0:T(2,128)}, u32[]{:S(2)}) %copy-start.1) | copy-done | bytes 131096
  6.3 0.0 copy-start.2
  6.3 0.9 %copy-done.2 = s32[1,128,2,128]{3,2,1,0:T(2,128)S(1)} copy-done((s32[1,128,2,128]{3,2,1,0:T(2,128)S(1)}, s32[1,128,2,128]{3,2,1,0:T(2,128)}, u32[]{:S(2)}) %copy-start.2) | copy-done | bytes 131096
  7.2 0.0 copy-start.3
  7.2 0.9 %copy-done.3 = s32[1,128,2,128]{3,2,1,0:T(2,128)S(1)} copy-done((s32[1,128,2,128]{3,2,1,0:T(2,128)S(1)}, s32[1,128,2,128]{3,2,1,0:T(2,128)}, u32[]{:S(2)}) %copy-start.3) | copy-done | bytes 131096
  8.1 5.2 %pack_blocks.1 = (f32[392,4,128]{2,1,0:T(4,128)}, s32[128]{0:T(128)S(1)}) custom-call(s32[128]{0:T(128)S(1)} %bitcast.21, s32[128]{0:T(128)S(1)} %bitcast.22, f32[128,2,128]{2,1,0:T(2,128)S(1)} %bitcast.18, s32[128,2,128]{2,1,0:T(2,128)S(1)} %bitcast.19, s32[128,2,128]{2,1,0:T(2,128)S(1)} %bitcast.20), custom_call_target="tpu_custom_call" | custom-call | tf_op jit(solution)/shard_map/pack_blocks/pallas_call | solution.py:205
  13.4 0.0 collective-permute-done
  13.4 3.8 %all-to-all-start = ((f32[392,4,128]{2,1,0:T(4,128)}), f32[392,4,128]{2,1,0:T(4,128)S(1)}, u32[]{:S(2)}, u32[]{:S(2)}) async-start(f32[392,4,128]{2,1,0:T(4,128)} %get-tuple-element.10), calls=%async_computation | async-start | bytes 1605632 | tf_op jit(solution)/shard_map/all_to_all | solution.py:226
  17.2 0.0 copy-start.7
  17.2 0.0 copy-start.6
  17.2 0.7 %copy-done.7 = bf16[16,8,8]{0,2,1:T(8,128)(2,1)S(1)} copy-done((bf16[16,8,8]{0,2,1:T(8,128)(2,1)S(1)}, bf16[16,8,8]{0,2,1:T(8,128)(2,1)}, u32[]{:S(2)}) %copy-start.7) | copy-done | bytes 2072
  18.0 0.1 copy.13.refs_2_
  18.0 0.1 copy-done.6
  18.2 10.9 %all-to-all-done.refs_1_ = f32[392,4,128]{2,1,0:T(4,128)S(1)} async-done(((f32[392,4,128]{2,1,0:T(4,128)}), f32[392,4,128]{2,1,0:T(4,128)S(1)}, u32[]{:S(2)}, u32[]{:S(2)}) %all-to-all-start) | async-done | bytes 802848 | tf_op jit(solution)/shard_map/all_to_all | solution.py:226
  29.0 22.0 %grid_blocks.1 = (bf16[384,2,128]{2,1,0:T(2,128)(2,1)}, f32[2,128,256]{2,1,0:T(8,128)S(1)}, bf16[2,128,256]{2,1,0:T(8,128)(2,1)S(1)}) custom-call(s32[1]{0:T(128)} %bitcast.refs_0_, f32[392,4,128]{2,1,0:T(4,128)S(1)} %all-to-all-done.refs_1_, f32[24,128]{1,0:T(8,128)S(1)} %copy.13.refs_2_, bf16[4,128,256]{2,1,0:T(8,128)(2,1)S(1)} %maximum_select_fusion.refs_3_), custom_call_target="tpu_custom_call" | custom-call | tf_op jit(solution)/shard_map/grid_blocks/pallas_call | solution.py:237
  51.1 0.4 collective-permute-start.1
  51.5 0.0 copy-done
  51.5 3.4 %all-to-all-start.1 = ((bf16[384,2,128]{2,1,0:T(2,128)(2,1)}), bf16[384,2,128]{2,1,0:T(2,128)(2,1)S(1)}, u32[]{:S(2)}, u32[]{:S(2)}) async-start(bf16[384,2,128]{2,1,0:T(2,128)(2,1)} %get-tuple-element.12), calls=%async_computation.1 | async-start | bytes 393216 | tf_op jit(solution)/shard_map/all_to_all | solution.py:260
  55.0 4.2 %collective-permute-done.1 = bf16[2,128,256]{2,1,0:T(8,128)(2,1)S(1)} collective-permute-done((bf16[2,128,256]{2,1,0:T(8,128)(2,1)S(1)}, bf16[2,128,256]{2,1,0:T(8,128)(2,1)S(1)}, u32[]{:S(2)}, u32[]{:S(2)}) %collective-permute-start.1) | collective-permute-done | bytes 131104 | tf_op jit(solution)/shard_map/ppermute | solution.py:264
  59.1 5.6 %all-gather = bf16[4,128,256]{2,1,0:T(8,128)(2,1)S(1)} all-gather(bf16[2,128,256]{2,1,0:T(8,128)(2,1)S(1)} %add_convert_fusion), channel_id=2, replica_groups=mesh['tile'=16,'freq'=2] {'freq'}, dimensions={0}, use_global_device_ids=true | all-gather | bytes 393216 | tf_op jit(solution)/shard_map/all_gather | solution.py:269
  64.8 0.8 %fusion = f32[2,128,256]{2,1,0:T(8,128)} fusion(bf16[2,2,128,256]{3,2,1,0:T(8,128)(2,1)S(1)} %bitcast.23, f32[2]{0:T(128)S(1)} %dynamic-slice_bitcast_fusion), kind=kLoop, calls=%fused_computation.2 | loop fusion | flops 327680 | bytes 524296 | tf_op jit(solution)/shard_map/reduce_sum | solution.py:267
  65.6 0.0 all-to-all-done.1
  65.6 0.7 %gather_fusion = bf16[128,2,128]{2,1,0:T(2,128)(2,1)S(1)} fusion(bf16[384,2,128]{2,1,0:T(2,128)(2,1)S(1)} %all-to-all-done.1, s32[1024]{0:T(1024)S(1)} %pad_clamp_fusion), kind=kCustom, calls=%fused_computation | custom fusion | bytes 131584 | tf_op jit(solution)/shard_map/jit(_take)/gather | solution.py:263
  66.4 0.7 %bitcast_convert_fusion = f32[1,128,2,128]{3,2,1,0:T(2,128)} fusion(bf16[128,2,128]{2,1,0:T(2,128)(2,1)S(1)} %gather_fusion), kind=kLoop, calls=%fused_computation.5 | loop fusion | flops 32768 | bytes 196608 | tf_op jit(solution)/shard_map/convert_element_type | solution.py:263
  (6 shorter events, 0.1 us)
Async XLA Ops:
  0.6 50.9 %copy-start = (f32[2,2]{1,0:T(2,128)S(1)}, f32[2,2]{1,0:T(2,128)}, u32[]{:S(2)}) copy-start(f32[2,2]{1,0:T(2,128)} %param.15) | copy-start | bytes 52
  0.6 12.7 %collective-permute-start = (bf16[2,128,256]{2,1,0:T(8,128)(2,1)}, bf16[2,128,256]{2,1,0:T(8,128)(2,1)S(1)}, u32[]{:S(2)}, u32[]{:S(2)}) collective-permute-start(bf16[2,128,256]{2,1,0:T(8,128)(2,1)} %bitcast.25), channel_id=1, source_target_pairs={{0,16},{2,18},{4,20},{6,22},{8,24},{10,26},{12,28},{14,30},{16,0},... | collective-permute-start | bytes 393224 | tf_op jit(solution)/shard_map/ppermute | solution.py:204
  4.7 0.7 copy-start.4
  4.8 0.7 copy-start.5
  5.4 0.9 %copy-start.1 = (f32[1,128,2,128]{3,2,1,0:T(2,128)S(1)}, f32[1,128,2,128]{3,2,1,0:T(2,128)}, u32[]{:S(2)}) copy-start(f32[1,128,2,128]{3,2,1,0:T(2,128)} %param.8) | copy-start | bytes 393220
  6.3 0.9 %copy-start.2 = (s32[1,128,2,128]{3,2,1,0:T(2,128)S(1)}, s32[1,128,2,128]{3,2,1,0:T(2,128)}, u32[]{:S(2)}) copy-start(s32[1,128,2,128]{3,2,1,0:T(2,128)} %param.9) | copy-start | bytes 393220
  7.2 0.9 %copy-start.3 = (s32[1,128,2,128]{3,2,1,0:T(2,128)S(1)}, s32[1,128,2,128]{3,2,1,0:T(2,128)}, u32[]{:S(2)}) copy-start(s32[1,128,2,128]{3,2,1,0:T(2,128)} %param.10) | copy-start | bytes 393220
  13.4 15.6 %all-to-all-start = ((f32[392,4,128]{2,1,0:T(4,128)}), f32[392,4,128]{2,1,0:T(4,128)S(1)}, u32[]{:S(2)}, u32[]{:S(2)}) async-start(f32[392,4,128]{2,1,0:T(4,128)} %get-tuple-element.10), calls=%async_computation | async-start | bytes 1605632 | tf_op jit(solution)/shard_map/all_to_all | solution.py:226
  17.2 0.7 %copy-start.7 = (bf16[16,8,8]{0,2,1:T(8,128)(2,1)S(1)}, bf16[16,8,8]{0,2,1:T(8,128)(2,1)}, u32[]{:S(2)}) copy-start(bf16[16,8,8]{0,2,1:T(8,128)(2,1)} %param.14) | copy-start | bytes 6148
  17.2 0.9 %copy-start.6 = (bf16[1,2,128,256]{3,2,1,0:T(8,128)(2,1)S(1)}, bf16[1,2,128,256]{3,2,1,0:T(8,128)(2,1)}, u32[]{:S(2)}) copy-start(bf16[1,2,128,256]{3,2,1,0:T(8,128)(2,1)} %param.13) | copy-start | bytes 393220
  51.1 8.0 %collective-permute-start.1 = (bf16[2,128,256]{2,1,0:T(8,128)(2,1)S(1)}, bf16[2,128,256]{2,1,0:T(8,128)(2,1)S(1)}, u32[]{:S(2)}, u32[]{:S(2)}) collective-permute-start(bf16[2,128,256]{2,1,0:T(8,128)(2,1)S(1)} %get-tuple-element.15), channel_id=1, source_target_pairs={{0,16},{2,18},{4,20},{6,22},{8,24},{10,26},{12,28},{14,30},{16,0},... | collective-permute-start | bytes 393224 | tf_op jit(solution)/shard_map/ppermute | solution.py:264
  51.5 14.1 %all-to-all-start.1 = ((bf16[384,2,128]{2,1,0:T(2,128)(2,1)}), bf16[384,2,128]{2,1,0:T(2,128)(2,1)S(1)}, u32[]{:S(2)}, u32[]{:S(2)}) async-start(bf16[384,2,128]{2,1,0:T(2,128)(2,1)} %get-tuple-element.12), calls=%async_computation.1 | async-start | bytes 393216 | tf_op jit(solution)/shard_map/all_to_all | solution.py:260
where the time goes:
time: 66.6 us; the launch traced here: 67.1 us
  Pallas kernels  27.3 us (41%)
  waiting for transfers between devices  15.1 us (23%)
  starting transfers between devices  11.8 us (18%)
  blocking collectives  5.64 us (8%)
  local copies, waits for them, and re-layouts  5.01 us (8%)
  other arithmetic  1.6 us (2%)
  between operations  0.73 us (1%)
    pallas_call x1, Pallas kernels, body(): pl.pallas_call(lambda *refs: grid_kernel(pairs, capacity, *refs), out_sha...  22 us
    all_to_all x1, waiting for transfers between devices, body(): lax.all_to_all(sent, 'tile', split_axis=0, concat_axis=0, tiled=True, axi...  10.9 us
    all_gather x1, blocking collectives, body(): lax.all_gather(grid_rounded, 'freq', axis=0, tiled=True).astype(jnp.float32)  5.64 us
    pallas_call x1, Pallas kernels, body(): pl.pallas_call(lambda *refs: pack_kernel(pairs, capacity, tiles_here, pla...  5.25 us
    unnamed x16, local copies, waits for them, and re-layouts  4.21 us
    ppermute x1, waiting for transfers between devices, body(): grid_sum = own + lax.ppermute(other, 'tile', swap).astype(jnp.float32)  4.17 us
    ppermute x1, starting transfers between devices, body(): model_other = lax.ppermute(model_own, 'tile', swap)  4.1 us
    all_to_all x1, starting transfers between devices, body(): lax.all_to_all(sent, 'tile', split_axis=0, concat_axis=0, tiled=True, axi...  3.82 us
  transfers between devices with their start and end apart: 4, of which 2 were waited for; matrix products, arithmetic and copies ran while one was open for 1% of the time, Pallas kernels for 8%

commit v1 on v0

--- a/solution.py
+++ b/solution.py
@@ -8,10 +8,16 @@
 UNROLL = 4
 VMEM = pl.BlockSpec(memory_space=pltpu.VMEM)
 SMEM = pl.BlockSpec(memory_space=pltpu.SMEM)
-ANY = pl.BlockSpec(memory_space=pl.ANY)
+HBM = pl.BlockSpec(memory_space=pltpu.HBM)
 PARAMS = pltpu.CompilerParams(vmem_limit_bytes=32 * 1024 * 1024)
-TILE_CODE = 4096
-PLANE_CODE = 65536
+WHOLE_PARAMS = pltpu.CompilerParams(vmem_limit_bytes=62 * 1024 * 1024)
+TILE_SHIFT = 12
+PLANE_SHIFT = 16
+
+
+def scalar_div(value, count):
+    shift = count.bit_length() - 1
+    return value >> shift if count == 1 << shift else lax.div(value, count)
 
 
 def pack_kernel(pairs, capacity, tiles_here, planes, plane_ref, tile_ref, vis_hbm, cell_hbm, sub_hbm,
@@ -26,7 +32,7 @@
     for copy in loads:
         copy.start()
     part = lax.broadcasted_iota(jnp.int32, (4, 128), 0)
-    empty = jnp.where(part == 0, float(planes * PLANE_CODE), 0.0)
+    empty = jnp.where(part == 0, float(planes << PLANE_SHIFT), 0.0)
     abouts = [d * (capacity + 1) + capacity for d in range(pairs)]
     for d in range(pairs):
         sent_ref[d * (capacity + 1)] = jnp.zeros((4, 128), jnp.float32)
@@ -41,23 +47,27 @@
     for copy in fills + loads:
         copy.wait()
 
-    def one_block(b):
+    def assign(b):
         tile = tile_ref[b]
-        owner = lax.div(tile, tiles_here)
+        owner = scalar_div(tile, tiles_here)
         high = (owner >= pairs).astype(jnp.int32)
         pair = owner - high * pairs
         local = tile - (owner - high) * tiles_here
         place = count_ref[pair]
         count_ref[pair] = place + 1
-        slot_ref[b] = pair * capacity + place
-        code = (plane_ref[b] * PLANE_CODE + local * TILE_CODE).astype(jnp.float32)
-        about_ref[pair, 0, place] = code
+        slot_ref[b] = pair * (capacity + 1) + place
+        code = (plane_ref[b] << PLANE_SHIFT) + (local << TILE_SHIFT)
+        about_ref[pair, 0, place] = code.astype(jnp.float32)
+
+    def move(b):
         position = (cell_ref[b] * 8 + sub_ref[b]).astype(jnp.float32)
-        sent_ref[pair * (capacity + 1) + place] = jnp.concatenate([vis_ref[b], position], axis=0)
+        sent_ref[slot_ref[b]] = jnp.concatenate([vis_ref[b], position], axis=0)
 
     def step(turn, carry):
         for which in range(8):
-            one_block(turn * 8 + which)
+            assign(turn * 8 + which)
+        for which in range(8):
+            move(turn * 8 + which)
         return carry
 
     lax.fori_loop(0, blocks // 8, step, 0)
@@ -96,7 +106,7 @@
     lane = lax.broadcasted_iota(jnp.int32, (1, 128), 1)
     for s in range(pairs):
         about = got_ref[s * (capacity + 1) + capacity].astype(jnp.int32)
-        code_ref[s, 0:1, :] = about[0:1] + (lane + s * capacity)
+        code_ref[s, 0:1, :] = about[0:1] + (lane + s * (capacity + 1))
         code_ref[s, 1:2, :] = about[1:2]
     fill = pltpu.make_async_copy(code_ref, about_ref, sem)
     fill.start()
@@ -108,9 +118,9 @@
     total = jnp.int32(0)
     for s in range(pairs):
         total = total + about_ref[s, 1, 0]
-    spare = jnp.where(total == 0, UNROLL, lax.rem(UNROLL - lax.rem(total, UNROLL), UNROLL))
+    spare = jnp.where(total == 0, UNROLL, -total & (UNROLL - 1))
     for u in range(UNROLL):
-        list_ref[u] = zero_row * PLANE_CODE
+        list_ref[u] = zero_row << PLANE_SHIFT
 
     def enlist(s, filled):
         for k in range(capacity):
@@ -118,15 +128,14 @@
         return filled + about_ref[s, 1, 0]
 
     lax.fori_loop(0, pairs, enlist, spare)
-    chunks = lax.div(total + spare, UNROLL)
+    chunks = scalar_div(total + spare, UNROLL)
     zero = jnp.zeros((16, 128), jnp.bfloat16)
 
     def read(which):
         entry = list_ref[which]
-        slot = entry & (TILE_CODE - 1)
-        tile = lax.div(entry, TILE_CODE) & 15
-        table_row = table_ref[pl.ds(lax.div(entry, PLANE_CODE), 1), :]
-        return slot, tile, table_row, got_ref[slot + lax.div(slot, capacity)]
+        slot = entry & ((1 << TILE_SHIFT) - 1)
+        tile = (entry >> TILE_SHIFT) & 15
+        return slot, tile, table_ref[pl.ds(entry >> PLANE_SHIFT, 1), :], got_ref[slot]
 
     def front(which, u):
         _, tile, table_row, data = read(which)
@@ -195,7 +204,7 @@
     capacity = 2 * (3 * blocks // owners)
     _, tiles_here, side, wide = model_grid.shape
     planes, oversample, support = kernel_table.shape
-    slots = pairs * capacity
+    slots = pairs * (capacity + 1)
     member = lax.axis_index("tile") // pairs
     swap = [(t, (t + pairs) % owners) for t in range(owners)]
     halves = [list(range(pairs)), list(range(pairs, owners))]
@@ -205,10 +214,10 @@
     sent, slot = pl.pallas_call(
         lambda *refs: pack_kernel(pairs, capacity, tiles_here, planes, *refs),
         out_shape=(
-            jax.ShapeDtypeStruct((slots + pairs, 4, rows), jnp.float32),
+            jax.ShapeDtypeStruct((slots, 4, rows), jnp.float32),
             jax.ShapeDtypeStruct((blocks,), jnp.int32),
         ),
-        in_specs=[SMEM, SMEM, ANY, ANY, ANY],
+        in_specs=[SMEM, SMEM, HBM, HBM, HBM],
         out_specs=(VMEM, SMEM),
         scratch_shapes=[
             pltpu.VMEM((blocks, 2, rows), jnp.float32),
@@ -219,7 +228,7 @@
             pltpu.SemaphoreType.DMA((3,)),
             pltpu.SemaphoreType.DMA((pairs,)),
         ],
-        compiler_params=PARAMS,
+        compiler_params=WHOLE_PARAMS,
         name="pack_blocks",
     )(w_plane[0], block_tile[0], visibilities[0], uv_cell[0], sub_pixel[0])
     sent, model_other = lax.optimization_barrier((sent, model_other))

time: 66.6 us -> 64.9 us (0.974); the launches traced: 67.1 us -> 64.5 us
  local copies, waits for them, and re-layouts: 5.01 us -> 2.28 us
  waiting for transfers between devices: 15.1 us -> 12.8 us
  starting transfers between devices: 11.8 us -> 13.9 us
    ppermute x1, waiting for transfers between devices: 4.17 us -> 0.43 us  [body(): grid_sum = own + lax.ppermute(other, 'tile', swap).astype(jnp.float32)]
    unnamed x16 -> x8, local copies, waits for them, and re-layouts: 4.21 us -> 1.48 us
    ppermute x1, starting transfers between devices: 0.45 us -> 2.86 us  [body(): grid_sum = own + lax.ppermute(other, 'tile', swap).astype(jnp.float32)]
    ppermute x1, waiting for transfers between devices: 0.01 us -> 1.62 us  [body(): model_other = lax.ppermute(model_own, 'tile', swap)]
  transfers between devices with their start and end apart: 4 -> 4, of which waited for: 2 -> 3; matrix products, arithmetic and copies ran while one was open for 1% -> 2% of each run, Pallas kernels for 8% -> 8%
where the time goes in v1:
time: 64.9 us; the launch traced here: 64.5 us
  Pallas kernels  27.1 us (42%)
  starting transfers between devices  13.9 us (21%)
  waiting for transfers between devices  12.8 us (20%)
  blocking collectives  6.06 us (9%)
  local copies, waits for them, and re-layouts  2.28 us (4%)
  other arithmetic  1.61 us (2%)
  between operations  0.73 us (1%)
    pallas_call x1, Pallas kernels, body(): pl.pallas_call(lambda *refs: grid_kernel(pairs, capacity, *refs), out_sha...  22.2 us
    all_to_all x1, waiting for transfers between devices, body(): lax.all_to_all(sent, 'tile', split_axis=0, concat_axis=0, tiled=True, axi...  10.8 us
    all_gather x1, blocking collectives, body(): lax.all_gather(grid_rounded, 'freq', axis=0, tiled=True).astype(jnp.float32)  6.06 us
    pallas_call x1, Pallas kernels, body(): pl.pallas_call(lambda *refs: pack_kernel(pairs, capacity, tiles_here, pla...  4.89 us
    ppermute x1, starting transfers between devices, body(): model_other = lax.ppermute(model_own, 'tile', swap)  4.1 us
    all_to_all x1, starting transfers between devices, body(): lax.all_to_all(sent, 'tile', split_axis=0, concat_axis=0, tiled=True, axi...  3.55 us
    all_to_all x1, starting transfers between devices, body(): lax.all_to_all(residual, 'tile', split_axis=0, concat_axis=0, tiled=True,...  3.39 us
    ppermute x1, starting transfers between devices, body(): grid_sum = own + lax.ppermute(other, 'tile', swap).astype(jnp.float32)  2.86 us
  transfers between devices with their start and end apart: 4, of which 3 were waited for; matrix products, arithmetic and copies ran while one was open for 2% of the time, Pallas kernels for 8%

profile of v1, /device:TPU:0, one launch (start us, length us, event | category | flops | bytes accessed | tf_op | source)
XLA Modules:
  0.0 64.5 jit_solution(3921691397818465189)
XLA Ops:
  0.6 0.0 copy-start
  0.6 4.1 %collective-permute-start = (bf16[2,128,256]{2,1,0:T(8,128)(2,1)}, bf16[2,128,256]{2,1,0:T(8,128)(2,1)S(1)}, u32[]{:S(2)}, u32[]{:S(2)}) collective-permute-start(bf16[2,128,256]{2,1,0:T(8,128)(2,1)} %bitcast.23), channel_id=1, source_target_pairs={{0,16},{2,18},{4,20},{6,22},{8,24},{10,26},{12,28},{14,30},{16,0},... | collective-permute-start | bytes 393224 | tf_op jit(solution)/shard_map/ppermute | solution.py:213
  4.7 4.9 %pack_blocks.1 = (f32[392,4,128]{2,1,0:T(4,128)}, s32[128]{0:T(128)}) custom-call(s32[128]{0:T(128)} %bitcast.25, s32[128]{0:T(128)} %bitcast.26, f32[128,2,128]{2,1,0:T(2,128)} %bitcast.20, s32[128,2,128]{2,1,0:T(2,128)} %bitcast.21, s32[128,2,128]{2,1,0:T(2,128)} %bitcast.22), custom_call_target="tpu_custom_call" | custom-call | tf_op jit(solution)/shard_map/pack_blocks/pallas_call | solution.py:214
  9.6 1.6 %collective-permute-done = bf16[2,128,256]{2,1,0:T(8,128)(2,1)S(1)} collective-permute-done((bf16[2,128,256]{2,1,0:T(8,128)(2,1)}, bf16[2,128,256]{2,1,0:T(8,128)(2,1)S(1)}, u32[]{:S(2)}, u32[]{:S(2)}) %collective-permute-start) | collective-permute-done | bytes 131104 | tf_op jit(solution)/shard_map/ppermute | solution.py:213
  11.3 3.5 %all-to-all-start = ((f32[392,4,128]{2,1,0:T(4,128)}), f32[392,4,128]{2,1,0:T(4,128)S(1)}, u32[]{:S(2)}, u32[]{:S(2)}) async-start(f32[392,4,128]{2,1,0:T(4,128)} %get-tuple-element.10), calls=%async_computation | async-start | bytes 1605632 | tf_op jit(solution)/shard_map/all_to_all | solution.py:235
  14.8 0.0 copy-start.2
  14.8 0.0 copy-start.1
  14.9 0.7 %copy-done.2 = bf16[16,8,8]{0,2,1:T(8,128)(2,1)S(1)} copy-done((bf16[16,8,8]{0,2,1:T(8,128)(2,1)S(1)}, bf16[16,8,8]{0,2,1:T(8,128)(2,1)}, u32[]{:S(2)}) %copy-start.2) | copy-done | bytes 2072
  15.6 0.1 copy.13.refs_2_
  15.6 0.1 copy-done.1
  15.8 10.8 %all-to-all-done.refs_1_ = f32[392,4,128]{2,1,0:T(4,128)S(1)} async-done(((f32[392,4,128]{2,1,0:T(4,128)}), f32[392,4,128]{2,1,0:T(4,128)S(1)}, u32[]{:S(2)}, u32[]{:S(2)}) %all-to-all-start) | async-done | bytes 802848 | tf_op jit(solution)/shard_map/all_to_all | solution.py:235
  26.6 22.2 %grid_blocks.1 = (bf16[392,2,128]{2,1,0:T(2,128)(2,1)}, f32[2,128,256]{2,1,0:T(8,128)S(1)}, bf16[2,128,256]{2,1,0:T(8,128)(2,1)S(1)}) custom-call(s32[1]{0:T(128)} %bitcast.refs_0_, f32[392,4,128]{2,1,0:T(4,128)S(1)} %all-to-all-done.refs_1_, f32[24,128]{1,0:T(8,128)S(1)} %copy.13.refs_2_, bf16[4,128,256]{2,1,0:T(8,128)(2,1)S(1)} %maximum_select_fusion.refs_3_), custom_call_target="tpu_custom_call" | custom-call | tf_op jit(solution)/shard_map/grid_blocks/pallas_call | solution.py:246
  48.8 2.9 %collective-permute-start.1 = (bf16[2,128,256]{2,1,0:T(8,128)(2,1)S(1)}, bf16[2,128,256]{2,1,0:T(8,128)(2,1)S(1)}, u32[]{:S(2)}, u32[]{:S(2)}) collective-permute-start(bf16[2,128,256]{2,1,0:T(8,128)(2,1)S(1)} %get-tuple-element.15), channel_id=1, source_target_pairs={{0,16},{2,18},{4,20},{6,22},{8,24},{10,26},{12,28},{14,30},{16,0},... | collective-permute-start | bytes 393224 | tf_op jit(solution)/shard_map/ppermute | solution.py:273
  51.6 0.0 copy-done
  51.6 0.0 copy-start.3
  51.6 0.6 %copy-done.3 = s32[128]{0:T(128)S(1)} copy-done((s32[128]{0:T(128)S(1)}, s32[128]{0:T(128)}, u32[]{:S(2)}) %copy-start.3) | copy-done | bytes 536
  52.3 3.4 %all-to-all-start.1 = ((bf16[392,2,128]{2,1,0:T(2,128)(2,1)}), bf16[392,2,128]{2,1,0:T(2,128)(2,1)S(1)}, u32[]{:S(2)}, u32[]{:S(2)}) async-start(bf16[392,2,128]{2,1,0:T(2,128)(2,1)} %get-tuple-element.12), calls=%async_computation.1 | async-start | bytes 401408 | tf_op jit(solution)/shard_map/all_to_all | solution.py:269
  55.7 0.4 collective-permute-done.1
  56.2 6.1 %all-gather = bf16[4,128,256]{2,1,0:T(8,128)(2,1)S(1)} all-gather(bf16[2,128,256]{2,1,0:T(8,128)(2,1)S(1)} %add_convert_fusion), channel_id=2, replica_groups=mesh['tile'=16,'freq'=2] {'freq'}, dimensions={0}, use_global_device_ids=true | all-gather | bytes 393216 | tf_op jit(solution)/shard_map/all_gather | solution.py:278
  62.2 0.8 %fusion = f32[2,128,256]{2,1,0:T(8,128)} fusion(bf16[2,2,128,256]{3,2,1,0:T(8,128)(2,1)S(1)} %bitcast.18, f32[2]{0:T(128)S(1)} %dynamic-slice_bitcast_fusion), kind=kLoop, calls=%fused_computation.2 | loop fusion | flops 327680 | bytes 524296 | tf_op jit(solution)/shard_map/reduce_sum | solution.py:276
  63.0 0.0 all-to-all-done.1
  63.0 0.7 %gather_fusion = bf16[128,2,128]{2,1,0:T(2,128)(2,1)S(1)} fusion(bf16[392,2,128]{2,1,0:T(2,128)(2,1)S(1)} %all-to-all-done.1, s32[1024]{0:T(1024)S(1)} %pad_clamp_fusion), kind=kCustom, calls=%fused_computation | custom fusion | bytes 131584 | tf_op jit(solution)/shard_map/jit(_take)/gather | solution.py:272
  63.8 0.7 %bitcast_convert_fusion = f32[1,128,2,128]{3,2,1,0:T(2,128)} fusion(bf16[128,2,128]{2,1,0:T(2,128)(2,1)S(1)} %gather_fusion), kind=kLoop, calls=%fused_computation.5 | loop fusion | flops 32768 | bytes 196608 | tf_op jit(solution)/shard_map/convert_element_type | solution.py:272
  (6 shorter events, 0.1 us)
Async XLA Ops:
  0.6 51.0 %copy-start = (f32[2,2]{1,0:T(2,128)S(1)}, f32[2,2]{1,0:T(2,128)}, u32[]{:S(2)}) copy-start(f32[2,2]{1,0:T(2,128)} %param.15) | copy-start | bytes 52
  0.6 10.6 %collective-permute-start = (bf16[2,128,256]{2,1,0:T(8,128)(2,1)}, bf16[2,128,256]{2,1,0:T(8,128)(2,1)S(1)}, u32[]{:S(2)}, u32[]{:S(2)}) collective-permute-start(bf16[2,128,256]{2,1,0:T(8,128)(2,1)} %bitcast.23), channel_id=1, source_target_pairs={{0,16},{2,18},{4,20},{6,22},{8,24},{10,26},{12,28},{14,30},{16,0},... | collective-permute-start | bytes 393224 | tf_op jit(solution)/shard_map/ppermute | solution.py:213
  11.3 15.3 %all-to-all-start = ((f32[392,4,128]{2,1,0:T(4,128)}), f32[392,4,128]{2,1,0:T(4,128)S(1)}, u32[]{:S(2)}, u32[]{:S(2)}) async-start(f32[392,4,128]{2,1,0:T(4,128)} %get-tuple-element.10), calls=%async_computation | async-start | bytes 1605632 | tf_op jit(solution)/shard_map/all_to_all | solution.py:235
  14.8 0.7 %copy-start.2 = (bf16[16,8,8]{0,2,1:T(8,128)(2,1)S(1)}, bf16[16,8,8]{0,2,1:T(8,128)(2,1)}, u32[]{:S(2)}) copy-start(bf16[16,8,8]{0,2,1:T(8,128)(2,1)} %param.14) | copy-start | bytes 6148
  14.8 0.9 %copy-start.1 = (bf16[1,2,128,256]{3,2,1,0:T(8,128)(2,1)S(1)}, bf16[1,2,128,256]{3,2,1,0:T(8,128)(2,1)}, u32[]{:S(2)}) copy-start(bf16[1,2,128,256]{3,2,1,0:T(8,128)(2,1)} %param.13) | copy-start | bytes 393220
  48.8 7.4 %collective-permute-start.1 = (bf16[2,128,256]{2,1,0:T(8,128)(2,1)S(1)}, bf16[2,128,256]{2,1,0:T(8,128)(2,1)S(1)}, u32[]{:S(2)}, u32[]{:S(2)}) collective-permute-start(bf16[2,128,256]{2,1,0:T(8,128)(2,1)S(1)} %get-tuple-element.15), channel_id=1, source_target_pairs={{0,16},{2,18},{4,20},{6,22},{8,24},{10,26},{12,28},{14,30},{16,0},... | collective-permute-start | bytes 393224 | tf_op jit(solution)/shard_map/ppermute | solution.py:273
  51.6 0.7 %copy-start.3 = (s32[128]{0:T(128)S(1)}, s32[128]{0:T(128)}, u32[]{:S(2)}) copy-start(s32[128]{0:T(128)} %get-tuple-element.13) | copy-start | bytes 1540
  52.3 10.8 %all-to-all-start.1 = ((bf16[392,2,128]{2,1,0:T(2,128)(2,1)}), bf16[392,2,128]{2,1,0:T(2,128)(2,1)S(1)}, u32[]{:S(2)}, u32[]{:S(2)}) async-start(bf16[392,2,128]{2,1,0:T(2,128)(2,1)} %get-tuple-element.12), calls=%async_computation.1 | async-start | bytes 401408 | tf_op jit(solution)/shard_map/all_to_all | solution.py:269

commit v2 on v1

--- a/solution.py
+++ b/solution.py
@@ -18,6 +18,11 @@
 def scalar_div(value, count):
     shift = count.bit_length() - 1
     return value >> shift if count == 1 << shift else lax.div(value, count)
+
+
+def first_slot(local, rank, capacity):
+    half = capacity // 2
+    return (local >> 1) * half + jnp.where((local & 1) == 0, rank, half - 1 - rank)
 
 
 def pack_kernel(pairs, capacity, tiles_here, planes, plane_ref, tile_ref, vis_hbm, cell_hbm, sub_hbm,
@@ -35,9 +40,9 @@
     empty = jnp.where(part == 0, float(planes << PLANE_SHIFT), 0.0)
     abouts = [d * (capacity + 1) + capacity for d in range(pairs)]
     for d in range(pairs):
-        sent_ref[d * (capacity + 1)] = jnp.zeros((4, 128), jnp.float32)
         sent_ref[abouts[d]] = empty
-        count_ref[d] = 0
+        for t in range(2 * tiles_here):
+            count_ref[d * 2 * tiles_here + t] = 0
     fills = [
         pltpu.make_async_copy(sent_ref.at[abouts[d]], about_ref.at[d], about_sem.at[d])
         for d in range(pairs)
@@ -53,8 +58,10 @@
         high = (owner >= pairs).astype(jnp.int32)
         pair = owner - high * pairs
         local = tile - (owner - high) * tiles_here
-        place = count_ref[pair]
-        count_ref[pair] = place + 1
+        key = pair * (2 * tiles_here) + local
+        rank = count_ref[key]
+        count_ref[key] = rank + 1
+        place = first_slot(local, rank, capacity)
         slot_ref[b] = pair * (capacity + 1) + place
         code = (plane_ref[b] << PLANE_SHIFT) + (local << TILE_SHIFT)
         about_ref[pair, 0, place] = code.astype(jnp.float32)
@@ -72,7 +79,8 @@
 
     lax.fori_loop(0, blocks // 8, step, 0)
     for d in range(pairs):
-        about_ref[d, 1, 0] = count_ref[d].astype(jnp.float32)
+        for t in range(2 * tiles_here):
+            about_ref[d, 1, t] = count_ref[d * 2 * tiles_here + t].astype(jnp.float32)
     returns = [
         pltpu.make_async_copy(about_ref.at[d], sent_ref.at[abouts[d]], about_sem.at[d])
         for d in range(pairs)
@@ -99,7 +107,7 @@
 
 
 def grid_kernel(pairs, capacity, member_ref, got_ref, table_ref, model_ref, residual_ref, own_ref,
-                other_ref, turned_ref, grid_ref, row_ref, partial_ref, code_ref, about_ref, list_ref, sem):
+                other_ref, turned_ref, grid_ref, row_ref, kept_ref, partial_ref, weighted_ref, code_ref, about_ref, list_ref, sem):
     tiles, side, wide = model_ref.shape
     groups = side // 16
     zero_row = table_ref.shape[0] - 8
@@ -115,81 +123,89 @@
     grid_ref[...] = jnp.zeros_like(grid_ref)
     fill.wait()
 
-    total = jnp.int32(0)
-    for s in range(pairs):
-        total = total + about_ref[s, 1, 0]
-    spare = jnp.where(total == 0, UNROLL, -total & (UNROLL - 1))
+    start = jnp.int32(0)
+    for t in range(tiles):
+        count = jnp.int32(0)
+        for s in range(pairs):
+            count = count + about_ref[s, 1, t]
+        spare = -count & (UNROLL - 1)
+        for u in range(UNROLL):
+            list_ref[start + u] = (zero_row << PLANE_SHIFT) + (t << TILE_SHIFT) + capacity
+
+        def enlist(s, filled, t=t):
+            for k in range(capacity // 2):
+                place = k if t % 2 == 0 else capacity // 2 - 1 - k
+                list_ref[filled + k] = about_ref[s, 0, t // 2 * (capacity // 2) + place]
+            return filled + about_ref[s, 1, t]
+
+        lax.fori_loop(0, pairs, enlist, start + spare)
+        start = start + count + spare
     for u in range(UNROLL):
-        list_ref[u] = zero_row << PLANE_SHIFT
-
-    def enlist(s, filled):
-        for k in range(capacity):
-            list_ref[filled + k] = about_ref[s, 0, k]
-        return filled + about_ref[s, 1, 0]
-
-    lax.fori_loop(0, pairs, enlist, spare)
-    chunks = scalar_div(total + spare, UNROLL)
+        list_ref[start + u] = (zero_row << PLANE_SHIFT) + capacity
+    chunks = jnp.maximum(start >> UNROLL.bit_length() - 1, 1)
     zero = jnp.zeros((16, 128), jnp.bfloat16)
 
     def read(which):
         entry = list_ref[which]
         slot = entry & ((1 << TILE_SHIFT) - 1)
-        tile = (entry >> TILE_SHIFT) & 15
-        return slot, tile, table_ref[pl.ds(entry >> PLANE_SHIFT, 1), :], got_ref[slot]
-
-    def front(which, u):
-        _, tile, table_row, data = read(which)
-        taps, group = spread_parts(data[2:3].astype(jnp.int32), table_row)
-        taps = taps.astype(jnp.bfloat16)
-        group = group.astype(jnp.float32).astype(jnp.bfloat16)
-        row_matrix = jnp.concatenate(
-            [jnp.where(group == k, taps, zero) for k in range(groups)], axis=0
+        return slot, table_ref[pl.ds(entry >> PLANE_SHIFT, 1), :], got_ref[slot]
+
+    def chunk_tile(turn):
+        return (list_ref[turn * UNROLL] >> TILE_SHIFT) & 15
+
+    def front(turn):
+        for u in range(UNROLL):
+            _, table_row, data = read(turn * UNROLL + u)
+            taps, group = spread_parts(data[2:3].astype(jnp.int32), table_row)
+            taps = taps.astype(jnp.bfloat16)
+            group = group.astype(jnp.float32).astype(jnp.bfloat16)
+            for k in range(groups):
+                row_ref[16 * k : 16 * k + 16, 128 * u : 128 * u + 128] = jnp.where(
+                    group == k, taps, zero
+                )
+        partial_ref[...] = jnp.dot(
+            turned_ref[chunk_tile(turn)], row_ref[...], preferred_element_type=jnp.float32
         )
-        row_ref[u] = row_matrix
-        partial_ref[u] = jnp.dot(turned_ref[tile], row_matrix, preferred_element_type=jnp.float32)
-
-    def back(which, u):
-        slot, tile, table_row, data = read(which)
-        taps, group = spread_parts(data[3:4].astype(jnp.int32), table_row)
-        residuals, samples = [], []
-        for part in range(2):
-            picked = jnp.zeros((16, 128), jnp.float32)
-            for k in range(groups):
-                low = part * side + 16 * k
-                picked = jnp.where(group == k, partial_ref[u, low : low + 16], picked)
-            model = jnp.sum(picked * taps, axis=0, keepdims=True)
-            residual = data[part : part + 1] - model
-            residuals.append(residual)
-            samples.append((residual * taps).astype(jnp.bfloat16))
-        residual_ref[slot] = jnp.concatenate(residuals, axis=0).astype(jnp.bfloat16)
-        group = group.astype(jnp.float32).astype(jnp.bfloat16)
-        weighted = jnp.concatenate(
-            [
-                jnp.where(group == k, samples[part], zero)
-                for part in range(2)
-                for k in range(groups)
-            ],
-            axis=0,
-        )
-        grid_ref[tile] += lax.dot_general(
-            row_ref[u],
-            weighted,
+
+    def back(turn):
+        kept_ref[...] = row_ref[...]
+        for u in range(UNROLL):
+            slot, table_row, data = read(turn * UNROLL + u)
+            columns = slice(128 * u, 128 * u + 128)
+            taps, group = spread_parts(data[3:4].astype(jnp.int32), table_row)
+            residuals, samples = [], []
+            for part in range(2):
+                picked = jnp.zeros((16, 128), jnp.float32)
+                for k in range(groups):
+                    low = part * side + 16 * k
+                    picked = jnp.where(group == k, partial_ref[low : low + 16, columns], picked)
+                model = jnp.sum(picked * taps, axis=0, keepdims=True)
+                residual = data[part : part + 1] - model
+                residuals.append(residual)
+                samples.append((residual * taps).astype(jnp.bfloat16))
+            residual_ref[slot] = jnp.concatenate(residuals, axis=0).astype(jnp.bfloat16)
+            group = group.astype(jnp.float32).astype(jnp.bfloat16)
+            for part in range(2):
+                for k in range(groups):
+                    low = part * side + 16 * k
+                    weighted_ref[low : low + 16, columns] = jnp.where(
+                        group == k, samples[part], zero
+                    )
+        grid_ref[chunk_tile(turn)] += lax.dot_general(
+            kept_ref[...],
+            weighted_ref[...],
             (((1,), (1,)), ((), ())),
             preferred_element_type=jnp.float32,
         )
 
     def step(turn, carry):
-        for u in range(UNROLL):
-            back((turn - 1) * UNROLL + u, u)
-        for u in range(UNROLL):
-            front(turn * UNROLL + u, u)
+        back(turn - 1)
+        front(turn)
         return carry
 
-    for u in range(UNROLL):
-        front(u, u)
+    front(0)
     lax.fori_loop(1, chunks, step, 0)
-    for u in range(UNROLL):
-        back((chunks - 1) * UNROLL + u, u)
+    back(chunks - 1)
     half = tiles // 2
     member = member_ref[0]
     for t in range(half):
@@ -224,7 +240,7 @@
             pltpu.VMEM((blocks, 2, rows), jnp.int32),
             pltpu.VMEM((blocks, 2, rows), jnp.int32),
             pltpu.SMEM((pairs, 4, rows), jnp.float32),
-            pltpu.SMEM((pairs,), jnp.int32),
+            pltpu.SMEM((pairs * 2 * tiles_here,), jnp.int32),
             pltpu.SemaphoreType.DMA((3,)),
             pltpu.SemaphoreType.DMA((pairs,)),
         ],
@@ -255,11 +271,13 @@
         scratch_shapes=[
             pltpu.VMEM((2 * tiles_here, wide, side), jnp.bfloat16),
             pltpu.VMEM((2 * tiles_here, side, wide), jnp.float32),
-            pltpu.VMEM((UNROLL, side, rows), jnp.bfloat16),
-            pltpu.VMEM((UNROLL, wide, rows), jnp.float32),
+            pltpu.VMEM((side, UNROLL * rows), jnp.bfloat16),
+            pltpu.VMEM((side, UNROLL * rows), jnp.bfloat16),
+            pltpu.VMEM((wide, UNROLL * rows), jnp.float32),
+            pltpu.VMEM((wide, UNROLL * rows), jnp.bfloat16),
             pltpu.VMEM((pairs, 2, rows), jnp.int32),
             pltpu.SMEM((pairs, 2, rows), jnp.int32),
-            pltpu.SMEM((slots + capacity + 2 * UNROLL,), jnp.int32),
+            pltpu.SMEM((slots + capacity + 2 * tiles_here * UNROLL + UNROLL,), jnp.int32),
             pltpu.SemaphoreType.DMA,
         ],
         compiler_params=PARAMS,

time: 64.9 us -> 66.1 us (1.018)
  starting transfers between devices: 13.9 us -> 32.8 us
  Pallas kernels: 27.1 us -> 8.82 us
  blocking collectives: 6.06 us -> 7.37 us
    pallas_call x1, Pallas kernels: 22.2 us -> 3.72 us  [body(): pl.pallas_call(lambda *refs: grid_kernel(pairs, capacity, *refs), out_sha...]
    all_to_all x1, starting transfers between devices: 3.39 us -> 21.8 us  [body(): lax.all_to_all(residual, 'tile', split_axis=0, concat_axis=0, tiled=True,...]
    all_gather x1, blocking collectives: 6.06 us -> 7.37 us  [body(): lax.all_gather(grid_rounded, 'freq', axis=0, tiled=True).astype(jnp.float32)]
  transfers between devices with their start and end apart: 4 -> 4, of which waited for: 3 -> 2; matrix products, arithmetic and copies ran while one was open for 2% -> 1% of each run, Pallas kernels for 8% -> 8%
where the time goes in v2:
time: 66.1 us; the launch traced here: 65.8 us
  starting transfers between devices  32.8 us (50%)
  waiting for transfers between devices  12.2 us (18%)
  Pallas kernels  8.82 us (13%)
  blocking collectives  7.37 us (11%)
  local copies, waits for them, and re-layouts  2.28 us (3%)
  other arithmetic  1.61 us (2%)
  between operations  0.72 us (1%)
    all_to_all x1, starting transfers between devices, body(): lax.all_to_all(residual, 'tile', split_axis=0, concat_axis=0, tiled=True,...  21.8 us
    all_to_all x1, waiting for transfers between devices, body(): lax.all_to_all(sent, 'tile', split_axis=0, concat_axis=0, tiled=True, axi...  10.8 us
    all_gather x1, blocking collectives, body(): lax.all_gather(grid_rounded, 'freq', axis=0, tiled=True).astype(jnp.float32)  7.37 us
    pallas_call x1, Pallas kernels, body(): pl.pallas_call(lambda *refs: pack_kernel(pairs, capacity, tiles_here, pla...  5.1 us
    ppermute x1, starting transfers between devices, body(): model_other = lax.ppermute(model_own, 'tile', swap)  4.1 us
    pallas_call x1, Pallas kernels, body(): pl.pallas_call(lambda *refs: grid_kernel(pairs, capacity, *refs), out_sha...  3.72 us
    all_to_all x1, starting transfers between devices, body(): lax.all_to_all(sent, 'tile', split_axis=0, concat_axis=0, tiled=True, axi...  3.55 us
    ppermute x1, starting transfers between devices, body(): grid_sum = own + lax.ppermute(other, 'tile', swap).astype(jnp.float32)  3.33 us
  transfers between devices with their start and end apart: 4, of which 2 were waited for; matrix products, arithmetic and copies ran while one was open for 1% of the time, Pallas kernels for 8%

profile of v2, /device:TPU:0, one launch (start us, length us, event | category | flops | bytes accessed | tf_op | source)
XLA Modules:
  0.0 65.8 jit_solution(4151881796088056204)
XLA Ops:
  0.6 0.0 copy-start
  0.6 4.1 %collective-permute-start = (bf16[2,128,256]{2,1,0:T(8,128)(2,1)}, bf16[2,128,256]{2,1,0:T(8,128)(2,1)S(1)}, u32[]{:S(2)}, u32[]{:S(2)}) collective-permute-start(bf16[2,128,256]{2,1,0:T(8,128)(2,1)} %bitcast.23), channel_id=1, source_target_pairs={{0,16},{2,18},{4,20},{6,22},{8,24},{10,26},{12,28},{14,30},{16,0},... | collective-permute-start | bytes 393224 | tf_op jit(solution)/shard_map/ppermute | solution.py:229
  4.7 5.1 %pack_blocks.1 = (f32[392,4,128]{2,1,0:T(4,128)}, s32[128]{0:T(128)}) custom-call(s32[128]{0:T(128)} %bitcast.25, s32[128]{0:T(128)} %bitcast.26, f32[128,2,128]{2,1,0:T(2,128)} %bitcast.20, s32[128,2,128]{2,1,0:T(2,128)} %bitcast.21, s32[128,2,128]{2,1,0:T(2,128)} %bitcast.22), custom_call_target="tpu_custom_call" | custom-call | tf_op jit(solution)/shard_map/pack_blocks/pallas_call | solution.py:230
  9.9 1.4 %collective-permute-done = bf16[2,128,256]{2,1,0:T(8,128)(2,1)S(1)} collective-permute-done((bf16[2,128,256]{2,1,0:T(8,128)(2,1)}, bf16[2,128,256]{2,1,0:T(8,128)(2,1)S(1)}, u32[]{:S(2)}, u32[]{:S(2)}) %collective-permute-start) | collective-permute-done | bytes 131104 | tf_op jit(solution)/shard_map/ppermute | solution.py:229
  11.3 3.5 %all-to-all-start = ((f32[392,4,128]{2,1,0:T(4,128)}), f32[392,4,128]{2,1,0:T(4,128)S(1)}, u32[]{:S(2)}, u32[]{:S(2)}) async-start(f32[392,4,128]{2,1,0:T(4,128)} %get-tuple-element.10), calls=%async_computation | async-start | bytes 1605632 | tf_op jit(solution)/shard_map/all_to_all | solution.py:251
  14.8 0.0 copy-start.2
  14.8 0.0 copy-start.1
  14.9 0.7 %copy-done.2 = bf16[16,8,8]{0,2,1:T(8,128)(2,1)S(1)} copy-done((bf16[16,8,8]{0,2,1:T(8,128)(2,1)S(1)}, bf16[16,8,8]{0,2,1:T(8,128)(2,1)}, u32[]{:S(2)}) %copy-start.2) | copy-done | bytes 2072
  15.6 0.1 copy.13.refs_2_
  15.6 0.1 copy-done.1
  15.8 10.8 %all-to-all-done.refs_1_ = f32[392,4,128]{2,1,0:T(4,128)S(1)} async-done(((f32[392,4,128]{2,1,0:T(4,128)}), f32[392,4,128]{2,1,0:T(4,128)S(1)}, u32[]{:S(2)}, u32[]{:S(2)}) %all-to-all-start) | async-done | bytes 802848 | tf_op jit(solution)/shard_map/all_to_all | solution.py:251
  26.6 3.7 %grid_blocks.1 = (bf16[392,2,128]{2,1,0:T(2,128)(2,1)}, f32[2,128,256]{2,1,0:T(8,128)S(1)}, bf16[2,128,256]{2,1,0:T(8,128)(2,1)S(1)}) custom-call(s32[1]{0:T(128)} %bitcast.refs_0_, f32[392,4,128]{2,1,0:T(4,128)S(1)} %all-to-all-done.refs_1_, f32[24,128]{1,0:T(8,128)S(1)} %copy.13.refs_2_, bf16[4,128,256]{2,1,0:T(8,128)(2,1)S(1)} %maximum_select_fusion.refs_3_), custom_call_target="tpu_custom_call" | custom-call | tf_op jit(solution)/shard_map/grid_blocks/pallas_call | solution.py:262
  30.3 3.3 %collective-permute-start.1 = (bf16[2,128,256]{2,1,0:T(8,128)(2,1)S(1)}, bf16[2,128,256]{2,1,0:T(8,128)(2,1)S(1)}, u32[]{:S(2)}, u32[]{:S(2)}) collective-permute-start(bf16[2,128,256]{2,1,0:T(8,128)(2,1)S(1)} %get-tuple-element.15), channel_id=1, source_target_pairs={{0,16},{2,18},{4,20},{6,22},{8,24},{10,26},{12,28},{14,30},{16,0},... | collective-permute-start | bytes 393224 | tf_op jit(solution)/shard_map/ppermute | solution.py:291
  33.6 0.0 copy-done
  33.6 0.0 copy-start.3
  33.6 0.6 copy-done.3
  34.3 21.8 %all-to-all-start.1 = ((bf16[392,2,128]{2,1,0:T(2,128)(2,1)}), bf16[392,2,128]{2,1,0:T(2,128)(2,1)S(1)}, u32[]{:S(2)}, u32[]{:S(2)}) async-start(bf16[392,2,128]{2,1,0:T(2,128)(2,1)} %get-tuple-element.12), calls=%async_computation.1 | async-start | bytes 401408 | tf_op jit(solution)/shard_map/all_to_all | solution.py:287
  56.1 0.0 collective-permute-done.1
  56.2 7.4 %all-gather = bf16[4,128,256]{2,1,0:T(8,128)(2,1)S(1)} all-gather(bf16[2,128,256]{2,1,0:T(8,128)(2,1)S(1)} %add_convert_fusion), channel_id=2, replica_groups=mesh['tile'=16,'freq'=2] {'freq'}, dimensions={0}, use_global_device_ids=true | all-gather | bytes 393216 | tf_op jit(solution)/shard_map/all_gather | solution.py:296
  63.5 0.8 %fusion = f32[2,128,256]{2,1,0:T(8,128)} fusion(bf16[2,2,128,256]{3,2,1,0:T(8,128)(2,1)S(1)} %bitcast.18, f32[2]{0:T(128)S(1)} %dynamic-slice_bitcast_fusion), kind=kLoop, calls=%fused_computation.2 | loop fusion | flops 327680 | bytes 524296 | tf_op jit(solution)/shard_map/reduce_sum | solution.py:294
  64.4 0.0 all-to-all-done.1
  64.4 0.7 %gather_fusion = bf16[128,2,128]{2,1,0:T(2,128)(2,1)S(1)} fusion(bf16[392,2,128]{2,1,0:T(2,128)(2,1)S(1)} %all-to-all-done.1, s32[1024]{0:T(1024)S(1)} %pad_clamp_fusion), kind=kCustom, calls=%fused_computation | custom fusion | bytes 131584 | tf_op jit(solution)/shard_map/jit(_take)/gather | solution.py:290
  65.1 0.7 %bitcast_convert_fusion = f32[1,128,2,128]{3,2,1,0:T(2,128)} fusion(bf16[128,2,128]{2,1,0:T(2,128)(2,1)S(1)} %gather_fusion), kind=kLoop, calls=%fused_computation.5 | loop fusion | flops 32768 | bytes 196608 | tf_op jit(solution)/shard_map/convert_element_type | solution.py:290
  (6 shorter events, 0.1 us)
Async XLA Ops:
  0.6 33.0 %copy-start = (f32[2,2]{1,0:T(2,128)S(1)}, f32[2,2]{1,0:T(2,128)}, u32[]{:S(2)}) copy-start(f32[2,2]{1,0:T(2,128)} %param.15) | copy-start | bytes 52
  0.6 10.6 %collective-permute-start = (bf16[2,128,256]{2,1,0:T(8,128)(2,1)}, bf16[2,128,256]{2,1,0:T(8,128)(2,1)S(1)}, u32[]{:S(2)}, u32[]{:S(2)}) collective-permute-start(bf16[2,128,256]{2,1,0:T(8,128)(2,1)} %bitcast.23), channel_id=1, source_target_pairs={{0,16},{2,18},{4,20},{6,22},{8,24},{10,26},{12,28},{14,30},{16,0},... | collective-permute-start | bytes 393224 | tf_op jit(solution)/shard_map/ppermute | solution.py:229
  11.3 15.3 %all-to-all-start = ((f32[392,4,128]{2,1,0:T(4,128)}), f32[392,4,128]{2,1,0:T(4,128)S(1)}, u32[]{:S(2)}, u32[]{:S(2)}) async-start(f32[392,4,128]{2,1,0:T(4,128)} %get-tuple-element.10), calls=%async_computation | async-start | bytes 1605632 | tf_op jit(solution)/shard_map/all_to_all | solution.py:251
  14.8 0.7 %copy-start.2 = (bf16[16,8,8]{0,2,1:T(8,128)(2,1)S(1)}, bf16[16,8,8]{0,2,1:T(8,128)(2,1)}, u32[]{:S(2)}) copy-start(bf16[16,8,8]{0,2,1:T(8,128)(2,1)} %param.14) | copy-start | bytes 6148
  14.8 0.9 %copy-start.1 = (bf16[1,2,128,256]{3,2,1,0:T(8,128)(2,1)S(1)}, bf16[1,2,128,256]{3,2,1,0:T(8,128)(2,1)}, u32[]{:S(2)}) copy-start(bf16[1,2,128,256]{3,2,1,0:T(8,128)(2,1)} %param.13) | copy-start | bytes 393220
  30.3 25.8 %collective-permute-start.1 = (bf16[2,128,256]{2,1,0:T(8,128)(2,1)S(1)}, bf16[2,128,256]{2,1,0:T(8,128)(2,1)S(1)}, u32[]{:S(2)}, u32[]{:S(2)}) collective-permute-start(bf16[2,128,256]{2,1,0:T(8,128)(2,1)S(1)} %get-tuple-element.15), channel_id=1, source_target_pairs={{0,16},{2,18},{4,20},{6,22},{8,24},{10,26},{12,28},{14,30},{16,0},... | collective-permute-start | bytes 393224 | tf_op jit(solution)/shard_map/ppermute | solution.py:291
  33.6 0.7 copy-start.3
  34.3 30.1 %all-to-all-start.1 = ((bf16[392,2,128]{2,1,0:T(2,128)(2,1)}), bf16[392,2,128]{2,1,0:T(2,128)(2,1)S(1)}, u32[]{:S(2)}, u32[]{:S(2)}) async-start(bf16[392,2,128]{2,1,0:T(2,128)(2,1)} %get-tuple-element.12), calls=%async_computation.1 | async-start | bytes 401408 | tf_op jit(solution)/shard_map/all_to_all | solution.py:287

commit v3 on v2

--- a/solution.py
+++ b/solution.py
@@ -192,8 +192,8 @@
                         group == k, samples[part], zero
                     )
         grid_ref[chunk_tile(turn)] += lax.dot_general(
+            weighted_ref[...],
             kept_ref[...],
-            weighted_ref[...],
             (((1,), (1,)), ((), ())),
             preferred_element_type=jnp.float32,
         )
@@ -209,8 +209,8 @@
     half = tiles // 2
     member = member_ref[0]
     for t in range(half):
-        own_ref[t] = grid_ref[member * half + t]
-        other_ref[t] = grid_ref[(1 - member) * half + t].astype(jnp.bfloat16)
+        own_ref[t] = grid_ref[member * half + t].T
+        other_ref[t] = grid_ref[(1 - member) * half + t].T.astype(jnp.bfloat16)
 
 
 def body(visibilities, uv_cell, sub_pixel, w_plane, block_tile, model_grid, kernel_table, coupling):
@@ -270,7 +270,7 @@
         out_specs=(VMEM, VMEM, VMEM),
         scratch_shapes=[
             pltpu.VMEM((2 * tiles_here, wide, side), jnp.bfloat16),
-            pltpu.VMEM((2 * tiles_here, side, wide), jnp.float32),
+            pltpu.VMEM((2 * tiles_here, wide, side), jnp.float32),
             pltpu.VMEM((side, UNROLL * rows), jnp.bfloat16),
             pltpu.VMEM((side, UNROLL * rows), jnp.bfloat16),
             pltpu.VMEM((wide, UNROLL * rows), jnp.float32),

time: 66.1 us -> 65.3 us (0.988)
    all_to_all x1, starting transfers between devices: 21.8 us -> 21 us  [body(): lax.all_to_all(residual, 'tile', split_axis=0, concat_axis=0, tiled=True,...]
where the time goes in v3:
time: 65.3 us; the launch traced here: 65 us
  starting transfers between devices  32.4 us (50%)
  waiting for transfers between devices  12.2 us (19%)
  Pallas kernels  9.05 us (14%)
  blocking collectives  6.71 us (10%)
  local copies, waits for them, and re-layouts  2.28 us (3%)
  other arithmetic  1.61 us (2%)
  between operations  0.72 us (1%)
    all_to_all x1, starting transfers between devices, body(): lax.all_to_all(residual, 'tile', split_axis=0, concat_axis=0, tiled=True,...  21 us
    all_to_all x1, waiting for transfers between devices, body(): lax.all_to_all(sent, 'tile', split_axis=0, concat_axis=0, tiled=True, axi...  10.8 us
    all_gather x1, blocking collectives, body(): lax.all_gather(grid_rounded, 'freq', axis=0, tiled=True).astype(jnp.float32)  6.71 us
    pallas_call x1, Pallas kernels, body(): pl.pallas_call(lambda *refs: pack_kernel(pairs, capacity, tiles_here, pla...  5.1 us
    ppermute x1, starting transfers between devices, body(): model_other = lax.ppermute(model_own, 'tile', swap)  4.1 us
    pallas_call x1, Pallas kernels, body(): pl.pallas_call(lambda *refs: grid_kernel(pairs, capacity, *refs), out_sha...  3.95 us
    ppermute x1, starting transfers between devices, body(): grid_sum = own + lax.ppermute(other, 'tile', swap).astype(jnp.float32)  3.72 us
    all_to_all x1, starting transfers between devices, body(): lax.all_to_all(sent, 'tile', split_axis=0, concat_axis=0, tiled=True, axi...  3.55 us
  transfers between devices with their start and end apart: 4, of which 2 were waited for; matrix products, arithmetic and copies ran while one was open for 1% of the time, Pallas kernels for 8%

profile of v3, /device:TPU:0, one launch (start us, length us, event | category | flops | bytes accessed | tf_op | source)
XLA Modules:
  0.0 65.0 jit_solution(14545201498594672019)
XLA Ops:
  0.6 0.0 copy-start
  0.6 4.1 %collective-permute-start = (bf16[2,128,256]{2,1,0:T(8,128)(2,1)}, bf16[2,128,256]{2,1,0:T(8,128)(2,1)S(1)}, u32[]{:S(2)}, u32[]{:S(2)}) collective-permute-start(bf16[2,128,256]{2,1,0:T(8,128)(2,1)} %bitcast.23), channel_id=1, source_target_pairs={{0,16},{2,18},{4,20},{6,22},{8,24},{10,26},{12,28},{14,30},{16,0},... | collective-permute-start | bytes 393224 | tf_op jit(solution)/shard_map/ppermute | solution.py:229
  4.7 5.1 %pack_blocks.1 = (f32[392,4,128]{2,1,0:T(4,128)}, s32[128]{0:T(128)}) custom-call(s32[128]{0:T(128)} %bitcast.25, s32[128]{0:T(128)} %bitcast.26, f32[128,2,128]{2,1,0:T(2,128)} %bitcast.20, s32[128,2,128]{2,1,0:T(2,128)} %bitcast.21, s32[128,2,128]{2,1,0:T(2,128)} %bitcast.22), custom_call_target="tpu_custom_call" | custom-call | tf_op jit(solution)/shard_map/pack_blocks/pallas_call | solution.py:230
  9.9 1.4 %collective-permute-done = bf16[2,128,256]{2,1,0:T(8,128)(2,1)S(1)} collective-permute-done((bf16[2,128,256]{2,1,0:T(8,128)(2,1)}, bf16[2,128,256]{2,1,0:T(8,128)(2,1)S(1)}, u32[]{:S(2)}, u32[]{:S(2)}) %collective-permute-start) | collective-permute-done | bytes 131104 | tf_op jit(solution)/shard_map/ppermute | solution.py:229
  11.3 3.5 %all-to-all-start = ((f32[392,4,128]{2,1,0:T(4,128)}), f32[392,4,128]{2,1,0:T(4,128)S(1)}, u32[]{:S(2)}, u32[]{:S(2)}) async-start(f32[392,4,128]{2,1,0:T(4,128)} %get-tuple-element.10), calls=%async_computation | async-start | bytes 1605632 | tf_op jit(solution)/shard_map/all_to_all | solution.py:251
  14.8 0.0 copy-start.2
  14.8 0.0 copy-start.1
  14.9 0.7 %copy-done.2 = bf16[16,8,8]{0,2,1:T(8,128)(2,1)S(1)} copy-done((bf16[16,8,8]{0,2,1:T(8,128)(2,1)S(1)}, bf16[16,8,8]{0,2,1:T(8,128)(2,1)}, u32[]{:S(2)}) %copy-start.2) | copy-done | bytes 2072
  15.6 0.1 copy.13.refs_2_
  15.6 0.1 copy-done.1
  15.8 10.8 %all-to-all-done.refs_1_ = f32[392,4,128]{2,1,0:T(4,128)S(1)} async-done(((f32[392,4,128]{2,1,0:T(4,128)}), f32[392,4,128]{2,1,0:T(4,128)S(1)}, u32[]{:S(2)}, u32[]{:S(2)}) %all-to-all-start) | async-done | bytes 802848 | tf_op jit(solution)/shard_map/all_to_all | solution.py:251
  26.6 3.9 %grid_blocks.1 = (bf16[392,2,128]{2,1,0:T(2,128)(2,1)}, f32[2,128,256]{2,1,0:T(8,128)S(1)}, bf16[2,128,256]{2,1,0:T(8,128)(2,1)S(1)}) custom-call(s32[1]{0:T(128)} %bitcast.refs_0_, f32[392,4,128]{2,1,0:T(4,128)S(1)} %all-to-all-done.refs_1_, f32[24,128]{1,0:T(8,128)S(1)} %copy.13.refs_2_, bf16[4,128,256]{2,1,0:T(8,128)(2,1)S(1)} %maximum_select_fusion.refs_3_), custom_call_target="tpu_custom_call" | custom-call | tf_op jit(solution)/shard_map/grid_blocks/pallas_call | solution.py:262
  30.5 3.7 %collective-permute-start.1 = (bf16[2,128,256]{2,1,0:T(8,128)(2,1)S(1)}, bf16[2,128,256]{2,1,0:T(8,128)(2,1)S(1)}, u32[]{:S(2)}, u32[]{:S(2)}) collective-permute-start(bf16[2,128,256]{2,1,0:T(8,128)(2,1)S(1)} %get-tuple-element.15), channel_id=1, source_target_pairs={{0,16},{2,18},{4,20},{6,22},{8,24},{10,26},{12,28},{14,30},{16,0},... | collective-permute-start | bytes 393224 | tf_op jit(solution)/shard_map/ppermute | solution.py:291
  34.2 0.0 copy-done
  34.3 0.0 copy-start.3
  34.3 0.6 copy-done.3
  34.9 21.0 %all-to-all-start.1 = ((bf16[392,2,128]{2,1,0:T(2,128)(2,1)}), bf16[392,2,128]{2,1,0:T(2,128)(2,1)S(1)}, u32[]{:S(2)}, u32[]{:S(2)}) async-start(bf16[392,2,128]{2,1,0:T(2,128)(2,1)} %get-tuple-element.12), calls=%async_computation.1 | async-start | bytes 401408 | tf_op jit(solution)/shard_map/all_to_all | solution.py:287
  56.0 0.0 collective-permute-done.1
  56.0 6.7 %all-gather = bf16[4,128,256]{2,1,0:T(8,128)(2,1)S(1)} all-gather(bf16[2,128,256]{2,1,0:T(8,128)(2,1)S(1)} %add_convert_fusion), channel_id=2, replica_groups=mesh['tile'=16,'freq'=2] {'freq'}, dimensions={0}, use_global_device_ids=true | all-gather | bytes 393216 | tf_op jit(solution)/shard_map/all_gather | solution.py:296
  62.7 0.8 %fusion = f32[2,128,256]{2,1,0:T(8,128)} fusion(bf16[2,2,128,256]{3,2,1,0:T(8,128)(2,1)S(1)} %bitcast.18, f32[2]{0:T(128)S(1)} %dynamic-slice_bitcast_fusion), kind=kLoop, calls=%fused_computation.2 | loop fusion | flops 327680 | bytes 524296 | tf_op jit(solution)/shard_map/reduce_sum | solution.py:294
  63.5 0.0 all-to-all-done.1
  63.5 0.7 %gather_fusion = bf16[128,2,128]{2,1,0:T(2,128)(2,1)S(1)} fusion(bf16[392,2,128]{2,1,0:T(2,128)(2,1)S(1)} %all-to-all-done.1, s32[1024]{0:T(1024)S(1)} %pad_clamp_fusion), kind=kCustom, calls=%fused_computation | custom fusion | bytes 131584 | tf_op jit(solution)/shard_map/jit(_take)/gather | solution.py:290
  64.3 0.7 %bitcast_convert_fusion = f32[1,128,2,128]{3,2,1,0:T(2,128)} fusion(bf16[128,2,128]{2,1,0:T(2,128)(2,1)S(1)} %gather_fusion), kind=kLoop, calls=%fused_computation.5 | loop fusion | flops 32768 | bytes 196608 | tf_op jit(solution)/shard_map/convert_element_type | solution.py:290
  (6 shorter events, 0.1 us)
Async XLA Ops:
  0.6 33.6 %copy-start = (f32[2,2]{1,0:T(2,128)S(1)}, f32[2,2]{1,0:T(2,128)}, u32[]{:S(2)}) copy-start(f32[2,2]{1,0:T(2,128)} %param.15) | copy-start | bytes 52
  0.6 10.6 %collective-permute-start = (bf16[2,128,256]{2,1,0:T(8,128)(2,1)}, bf16[2,128,256]{2,1,0:T(8,128)(2,1)S(1)}, u32[]{:S(2)}, u32[]{:S(2)}) collective-permute-start(bf16[2,128,256]{2,1,0:T(8,128)(2,1)} %bitcast.23), channel_id=1, source_target_pairs={{0,16},{2,18},{4,20},{6,22},{8,24},{10,26},{12,28},{14,30},{16,0},... | collective-permute-start | bytes 393224 | tf_op jit(solution)/shard_map/ppermute | solution.py:229
  11.3 15.3 %all-to-all-start = ((f32[392,4,128]{2,1,0:T(4,128)}), f32[392,4,128]{2,1,0:T(4,128)S(1)}, u32[]{:S(2)}, u32[]{:S(2)}) async-start(f32[392,4,128]{2,1,0:T(4,128)} %get-tuple-element.10), calls=%async_computation | async-start | bytes 1605632 | tf_op jit(solution)/shard_map/all_to_all | solution.py:251
  14.8 0.7 %copy-start.2 = (bf16[16,8,8]{0,2,1:T(8,128)(2,1)S(1)}, bf16[16,8,8]{0,2,1:T(8,128)(2,1)}, u32[]{:S(2)}) copy-start(bf16[16,8,8]{0,2,1:T(8,128)(2,1)} %param.14) | copy-start | bytes 6148
  14.8 0.9 %copy-start.1 = (bf16[1,2,128,256]{3,2,1,0:T(8,128)(2,1)S(1)}, bf16[1,2,128,256]{3,2,1,0:T(8,128)(2,1)}, u32[]{:S(2)}) copy-start(bf16[1,2,128,256]{3,2,1,0:T(8,128)(2,1)} %param.13) | copy-start | bytes 393220
  30.5 25.4 %collective-permute-start.1 = (bf16[2,128,256]{2,1,0:T(8,128)(2,1)S(1)}, bf16[2,128,256]{2,1,0:T(8,128)(2,1)S(1)}, u32[]{:S(2)}, u32[]{:S(2)}) collective-permute-start(bf16[2,128,256]{2,1,0:T(8,128)(2,1)S(1)} %get-tuple-element.15), channel_id=1, source_target_pairs={{0,16},{2,18},{4,20},{6,22},{8,24},{10,26},{12,28},{14,30},{16,0},... | collective-permute-start | bytes 393224 | tf_op jit(solution)/shard_map/ppermute | solution.py:291
  34.3 0.7 %copy-start.3 = (s32[128]{0:T(128)S(1)}, s32[128]{0:T(128)}, u32[]{:S(2)}) copy-start(s32[128]{0:T(128)} %get-tuple-element.13) | copy-start | bytes 1540
  34.9 28.6 %all-to-all-start.1 = ((bf16[392,2,128]{2,1,0:T(2,128)(2,1)}), bf16[392,2,128]{2,1,0:T(2,128)(2,1)S(1)}, u32[]{:S(2)}, u32[]{:S(2)}) async-start(bf16[392,2,128]{2,1,0:T(2,128)(2,1)} %get-tuple-element.12), calls=%async_computation.1 | async-start | bytes 401408 | tf_op jit(solution)/shard_map/all_to_all | solution.py:287

commit v4 on v2

--- a/solution.py
+++ b/solution.py
@@ -107,7 +107,7 @@
 
 
 def grid_kernel(pairs, capacity, member_ref, got_ref, table_ref, model_ref, residual_ref, own_ref,
-                other_ref, turned_ref, grid_ref, row_ref, kept_ref, partial_ref, weighted_ref, code_ref, about_ref, list_ref, sem):
+                other_ref, turned_ref, grid_ref, row_a, row_b, partial_a, partial_b, weighted_ref, code_ref, about_ref, list_ref, sem):
     tiles, side, wide = model_ref.shape
     groups = side // 16
     zero_row = table_ref.shape[0] - 8
@@ -140,9 +140,9 @@
 
         lax.fori_loop(0, pairs, enlist, start + spare)
         start = start + count + spare
-    for u in range(UNROLL):
+    for u in range(2 * UNROLL):
         list_ref[start + u] = (zero_row << PLANE_SHIFT) + capacity
-    chunks = jnp.maximum(start >> UNROLL.bit_length() - 1, 1)
+    chunks = start >> UNROLL.bit_length() - 1
     zero = jnp.zeros((16, 128), jnp.bfloat16)
 
     def read(which):
@@ -153,7 +153,7 @@
     def chunk_tile(turn):
         return (list_ref[turn * UNROLL] >> TILE_SHIFT) & 15
 
-    def front(turn):
+    def front(turn, row_ref, partial_ref):
         for u in range(UNROLL):
             _, table_row, data = read(turn * UNROLL + u)
             taps, group = spread_parts(data[2:3].astype(jnp.int32), table_row)
@@ -167,8 +167,7 @@
             turned_ref[chunk_tile(turn)], row_ref[...], preferred_element_type=jnp.float32
         )
 
-    def back(turn):
-        kept_ref[...] = row_ref[...]
+    def back(turn, row_ref, partial_ref):
         for u in range(UNROLL):
             slot, table_row, data = read(turn * UNROLL + u)
             columns = slice(128 * u, 128 * u + 128)
@@ -192,20 +191,21 @@
                         group == k, samples[part], zero
                     )
         grid_ref[chunk_tile(turn)] += lax.dot_general(
-            kept_ref[...],
+            row_ref[...],
             weighted_ref[...],
             (((1,), (1,)), ((), ())),
             preferred_element_type=jnp.float32,
         )
 
     def step(turn, carry):
-        back(turn - 1)
-        front(turn)
+        front(2 * turn + 1, row_b, partial_b)
+        back(2 * turn, row_a, partial_a)
+        front(2 * turn + 2, row_a, partial_a)
+        back(2 * turn + 1, row_b, partial_b)
         return carry
 
-    front(0)
-    lax.fori_loop(1, chunks, step, 0)
-    back(chunks - 1)
+    front(0, row_a, partial_a)
+    lax.fori_loop(0, (chunks + 1) >> 1, step, 0)
     half = tiles // 2
     member = member_ref[0]
     for t in range(half):
@@ -274,6 +274,7 @@
             pltpu.VMEM((side, UNROLL * rows), jnp.bfloat16),
             pltpu.VMEM((side, UNROLL * rows), jnp.bfloat16),
             pltpu.VMEM((wide, UNROLL * rows), jnp.float32),
+            pltpu.VMEM((wide, UNROLL * rows), jnp.float32),
             pltpu.VMEM((wide, UNROLL * rows), jnp.bfloat16),
             pltpu.VMEM((pairs, 2, rows), jnp.int32),
             pltpu.SMEM((pairs, 2, rows), jnp.int32),

time: 66.1 us -> 62 us (0.938)
  starting transfers between devices: 32.8 us -> 28.5 us
    all_to_all x1, starting transfers between devices: 21.8 us -> 17.3 us  [body(): lax.all_to_all(residual, 'tile', split_axis=0, concat_axis=0, tiled=True,...]
  transfers between devices with their start and end apart: 4 -> 4, of which waited for: 2 -> 2; matrix products, arithmetic and copies ran while one was open for 1% -> 2% of each run, Pallas kernels for 8% -> 8%
where the time goes in v4:
time: 62 us; the launch traced here: 61.8 us
  starting transfers between devices  28.5 us (46%)
  waiting for transfers between devices  12.2 us (20%)
  Pallas kernels  9.12 us (15%)
  blocking collectives  7.38 us (12%)
  local copies, waits for them, and re-layouts  2.28 us (4%)
  other arithmetic  1.61 us (3%)
  between operations  0.72 us (1%)
    all_to_all x1, starting transfers between devices, body(): lax.all_to_all(residual, 'tile', split_axis=0, concat_axis=0, tiled=True,...  17.3 us
    all_to_all x1, waiting for transfers between devices, body(): lax.all_to_all(sent, 'tile', split_axis=0, concat_axis=0, tiled=True, axi...  10.8 us
    all_gather x1, blocking collectives, body(): lax.all_gather(grid_rounded, 'freq', axis=0, tiled=True).astype(jnp.float32)  7.38 us
    pallas_call x1, Pallas kernels, body(): pl.pallas_call(lambda *refs: pack_kernel(pairs, capacity, tiles_here, pla...  5.1 us
    ppermute x1, starting transfers between devices, body(): model_other = lax.ppermute(model_own, 'tile', swap)  4.1 us
    pallas_call x1, Pallas kernels, body(): pl.pallas_call(lambda *refs: grid_kernel(pairs, capacity, *refs), out_sha...  4.02 us
    ppermute x1, starting transfers between devices, body(): grid_sum = own + lax.ppermute(other, 'tile', swap).astype(jnp.float32)  3.55 us
    all_to_all x1, starting transfers between devices, body(): lax.all_to_all(sent, 'tile', split_axis=0, concat_axis=0, tiled=True, axi...  3.55 us
  transfers between devices with their start and end apart: 4, of which 2 were waited for; matrix products, arithmetic and copies ran while one was open for 2% of the time, Pallas kernels for 8%

profile of v4, /device:TPU:0, one launch (start us, length us, event | category | flops | bytes accessed | tf_op | source)
XLA Modules:
  0.0 61.8 jit_solution(4668186685774310506)
XLA Ops:
  0.6 0.0 copy-start
  0.6 4.1 %collective-permute-start = (bf16[2,128,256]{2,1,0:T(8,128)(2,1)}, bf16[2,128,256]{2,1,0:T(8,128)(2,1)S(1)}, u32[]{:S(2)}, u32[]{:S(2)}) collective-permute-start(bf16[2,128,256]{2,1,0:T(8,128)(2,1)} %bitcast.23), channel_id=1, source_target_pairs={{0,16},{2,18},{4,20},{6,22},{8,24},{10,26},{12,28},{14,30},{16,0},... | collective-permute-start | bytes 393224 | tf_op jit(solution)/shard_map/ppermute | solution.py:229
  4.7 5.1 %pack_blocks.1 = (f32[392,4,128]{2,1,0:T(4,128)}, s32[128]{0:T(128)}) custom-call(s32[128]{0:T(128)} %bitcast.25, s32[128]{0:T(128)} %bitcast.26, f32[128,2,128]{2,1,0:T(2,128)} %bitcast.20, s32[128,2,128]{2,1,0:T(2,128)} %bitcast.21, s32[128,2,128]{2,1,0:T(2,128)} %bitcast.22), custom_call_target="tpu_custom_call" | custom-call | tf_op jit(solution)/shard_map/pack_blocks/pallas_call | solution.py:230
  9.9 1.4 %collective-permute-done = bf16[2,128,256]{2,1,0:T(8,128)(2,1)S(1)} collective-permute-done((bf16[2,128,256]{2,1,0:T(8,128)(2,1)}, bf16[2,128,256]{2,1,0:T(8,128)(2,1)S(1)}, u32[]{:S(2)}, u32[]{:S(2)}) %collective-permute-start) | collective-permute-done | bytes 131104 | tf_op jit(solution)/shard_map/ppermute | solution.py:229
  11.3 3.5 %all-to-all-start = ((f32[392,4,128]{2,1,0:T(4,128)}), f32[392,4,128]{2,1,0:T(4,128)S(1)}, u32[]{:S(2)}, u32[]{:S(2)}) async-start(f32[392,4,128]{2,1,0:T(4,128)} %get-tuple-element.10), calls=%async_computation | async-start | bytes 1605632 | tf_op jit(solution)/shard_map/all_to_all | solution.py:251
  14.8 0.0 copy-start.2
  14.8 0.0 copy-start.1
  14.9 0.7 %copy-done.2 = bf16[16,8,8]{0,2,1:T(8,128)(2,1)S(1)} copy-done((bf16[16,8,8]{0,2,1:T(8,128)(2,1)S(1)}, bf16[16,8,8]{0,2,1:T(8,128)(2,1)}, u32[]{:S(2)}) %copy-start.2) | copy-done | bytes 2072
  15.6 0.1 copy.13.refs_2_
  15.6 0.1 copy-done.1
  15.8 10.8 %all-to-all-done.refs_1_ = f32[392,4,128]{2,1,0:T(4,128)S(1)} async-done(((f32[392,4,128]{2,1,0:T(4,128)}), f32[392,4,128]{2,1,0:T(4,128)S(1)}, u32[]{:S(2)}, u32[]{:S(2)}) %all-to-all-start) | async-done | bytes 802848 | tf_op jit(solution)/shard_map/all_to_all | solution.py:251
  26.6 4.0 %grid_blocks.1 = (bf16[392,2,128]{2,1,0:T(2,128)(2,1)}, f32[2,128,256]{2,1,0:T(8,128)S(1)}, bf16[2,128,256]{2,1,0:T(8,128)(2,1)S(1)}) custom-call(s32[1]{0:T(128)} %bitcast.refs_0_, f32[392,4,128]{2,1,0:T(4,128)S(1)} %all-to-all-done.refs_1_, f32[24,128]{1,0:T(8,128)S(1)} %copy.13.refs_2_, bf16[4,128,256]{2,1,0:T(8,128)(2,1)S(1)} %maximum_select_fusion.refs_3_), custom_call_target="tpu_custom_call" | custom-call | tf_op jit(solution)/shard_map/grid_blocks/pallas_call | solution.py:262
  30.6 3.6 %collective-permute-start.1 = (bf16[2,128,256]{2,1,0:T(8,128)(2,1)S(1)}, bf16[2,128,256]{2,1,0:T(8,128)(2,1)S(1)}, u32[]{:S(2)}, u32[]{:S(2)}) collective-permute-start(bf16[2,128,256]{2,1,0:T(8,128)(2,1)S(1)} %get-tuple-element.15), channel_id=1, source_target_pairs={{0,16},{2,18},{4,20},{6,22},{8,24},{10,26},{12,28},{14,30},{16,0},... | collective-permute-start | bytes 393224 | tf_op jit(solution)/shard_map/ppermute | solution.py:292
  34.1 0.0 copy-done
  34.2 0.0 copy-start.3
  34.2 0.6 %copy-done.3 = s32[128]{0:T(128)S(1)} copy-done((s32[128]{0:T(128)S(1)}, s32[128]{0:T(128)}, u32[]{:S(2)}) %copy-start.3) | copy-done | bytes 536
  34.8 17.3 %all-to-all-start.1 = ((bf16[392,2,128]{2,1,0:T(2,128)(2,1)}), bf16[392,2,128]{2,1,0:T(2,128)(2,1)S(1)}, u32[]{:S(2)}, u32[]{:S(2)}) async-start(bf16[392,2,128]{2,1,0:T(2,128)(2,1)} %get-tuple-element.12), calls=%async_computation.1 | async-start | bytes 401408 | tf_op jit(solution)/shard_map/all_to_all | solution.py:288
  52.1 0.0 collective-permute-done.1
  52.1 7.4 %all-gather = bf16[4,128,256]{2,1,0:T(8,128)(2,1)S(1)} all-gather(bf16[2,128,256]{2,1,0:T(8,128)(2,1)S(1)} %add_convert_fusion), channel_id=2, replica_groups=mesh['tile'=16,'freq'=2] {'freq'}, dimensions={0}, use_global_device_ids=true | all-gather | bytes 393216 | tf_op jit(solution)/shard_map/all_gather | solution.py:297
  59.5 0.8 %fusion = f32[2,128,256]{2,1,0:T(8,128)} fusion(bf16[2,2,128,256]{3,2,1,0:T(8,128)(2,1)S(1)} %bitcast.18, f32[2]{0:T(128)S(1)} %dynamic-slice_bitcast_fusion), kind=kLoop, calls=%fused_computation.2 | loop fusion | flops 327680 | bytes 524296 | tf_op jit(solution)/shard_map/reduce_sum | solution.py:295
  60.3 0.0 all-to-all-done.1
  60.3 0.7 %gather_fusion = bf16[128,2,128]{2,1,0:T(2,128)(2,1)S(1)} fusion(bf16[392,2,128]{2,1,0:T(2,128)(2,1)S(1)} %all-to-all-done.1, s32[1024]{0:T(1024)S(1)} %pad_clamp_fusion), kind=kCustom, calls=%fused_computation | custom fusion | bytes 131584 | tf_op jit(solution)/shard_map/jit(_take)/gather | solution.py:291
  61.1 0.7 %bitcast_convert_fusion = f32[1,128,2,128]{3,2,1,0:T(2,128)} fusion(bf16[128,2,128]{2,1,0:T(2,128)(2,1)S(1)} %gather_fusion), kind=kLoop, calls=%fused_computation.5 | loop fusion | flops 32768 | bytes 196608 | tf_op jit(solution)/shard_map/convert_element_type | solution.py:291
  (6 shorter events, 0.1 us)
Async XLA Ops:
  0.6 33.5 %copy-start = (f32[2,2]{1,0:T(2,128)S(1)}, f32[2,2]{1,0:T(2,128)}, u32[]{:S(2)}) copy-start(f32[2,2]{1,0:T(2,128)} %param.15) | copy-start | bytes 52
  0.6 10.6 %collective-permute-start = (bf16[2,128,256]{2,1,0:T(8,128)(2,1)}, bf16[2,128,256]{2,1,0:T(8,128)(2,1)S(1)}, u32[]{:S(2)}, u32[]{:S(2)}) collective-permute-start(bf16[2,128,256]{2,1,0:T(8,128)(2,1)} %bitcast.23), channel_id=1, source_target_pairs={{0,16},{2,18},{4,20},{6,22},{8,24},{10,26},{12,28},{14,30},{16,0},... | collective-permute-start | bytes 393224 | tf_op jit(solution)/shard_map/ppermute | solution.py:229
  11.3 15.3 %all-to-all-start = ((f32[392,4,128]{2,1,0:T(4,128)}), f32[392,4,128]{2,1,0:T(4,128)S(1)}, u32[]{:S(2)}, u32[]{:S(2)}) async-start(f32[392,4,128]{2,1,0:T(4,128)} %get-tuple-element.10), calls=%async_computation | async-start | bytes 1605632 | tf_op jit(solution)/shard_map/all_to_all | solution.py:251
  14.8 0.7 %copy-start.2 = (bf16[16,8,8]{0,2,1:T(8,128)(2,1)S(1)}, bf16[16,8,8]{0,2,1:T(8,128)(2,1)}, u32[]{:S(2)}) copy-start(bf16[16,8,8]{0,2,1:T(8,128)(2,1)} %param.14) | copy-start | bytes 6148
  14.8 0.9 %copy-start.1 = (bf16[1,2,128,256]{3,2,1,0:T(8,128)(2,1)S(1)}, bf16[1,2,128,256]{3,2,1,0:T(8,128)(2,1)}, u32[]{:S(2)}) copy-start(bf16[1,2,128,256]{3,2,1,0:T(8,128)(2,1)} %param.13) | copy-start | bytes 393220
  30.6 21.5 %collective-permute-start.1 = (bf16[2,128,256]{2,1,0:T(8,128)(2,1)S(1)}, bf16[2,128,256]{2,1,0:T(8,128)(2,1)S(1)}, u32[]{:S(2)}, u32[]{:S(2)}) collective-permute-start(bf16[2,128,256]{2,1,0:T(8,128)(2,1)S(1)} %get-tuple-element.15), channel_id=1, source_target_pairs={{0,16},{2,18},{4,20},{6,22},{8,24},{10,26},{12,28},{14,30},{16,0},... | collective-permute-start | bytes 393224 | tf_op jit(solution)/shard_map/ppermute | solution.py:292
  34.2 0.7 %copy-start.3 = (s32[128]{0:T(128)S(1)}, s32[128]{0:T(128)}, u32[]{:S(2)}) copy-start(s32[128]{0:T(128)} %get-tuple-element.13) | copy-start | bytes 1540
  34.8 25.5 %all-to-all-start.1 = ((bf16[392,2,128]{2,1,0:T(2,128)(2,1)}), bf16[392,2,128]{2,1,0:T(2,128)(2,1)S(1)}, u32[]{:S(2)}, u32[]{:S(2)}) async-start(bf16[392,2,128]{2,1,0:T(2,128)(2,1)} %get-tuple-element.12), calls=%async_computation.1 | async-start | bytes 401408 | tf_op jit(solution)/shard_map/all_to_all | solution.py:288

commit v5 on v4

--- a/solution.py
+++ b/solution.py
@@ -25,13 +25,20 @@
     return (local >> 1) * half + jnp.where((local & 1) == 0, rank, half - 1 - rank)
 
 
-def pack_kernel(pairs, capacity, tiles_here, planes, plane_ref, tile_ref, vis_hbm, cell_hbm, sub_hbm,
-                sent_ref, slot_ref, vis_ref, cell_ref, sub_ref, about_ref, count_ref, load_sem, about_sem):
+def pack_kernel(pairs, capacity, tiles_here, planes, plane_hbm, tile_hbm, vis_hbm, cell_hbm, sub_hbm,
+                sent_ref, slot_ref, plane_ref, tile_ref, vis_ref, cell_ref, sub_ref, about_ref, count_ref,
+                load_sem, about_sem):
     blocks = tile_ref.shape[0]
     loads = [
         pltpu.make_async_copy(source, target, load_sem.at[i])
         for i, (source, target) in enumerate(
-            [(vis_hbm, vis_ref), (cell_hbm, cell_ref), (sub_hbm, sub_ref)]
+            [
+                (tile_hbm, tile_ref),
+                (plane_hbm, plane_ref),
+                (vis_hbm, vis_ref),
+                (cell_hbm, cell_ref),
+                (sub_hbm, sub_ref),
+            ]
         )
     ]
     for copy in loads:
@@ -49,7 +56,7 @@
     ]
     for copy in fills:
         copy.start()
-    for copy in fills + loads:
+    for copy in fills + loads[:2]:
         copy.wait()
 
     def assign(b):
@@ -70,14 +77,15 @@
         position = (cell_ref[b] * 8 + sub_ref[b]).astype(jnp.float32)
         sent_ref[slot_ref[b]] = jnp.concatenate([vis_ref[b], position], axis=0)
 
-    def step(turn, carry):
-        for which in range(8):
-            assign(turn * 8 + which)
-        for which in range(8):
-            move(turn * 8 + which)
-        return carry
-
-    lax.fori_loop(0, blocks // 8, step, 0)
+    def each(work):
+        def step(turn, carry):
+            for which in range(8):
+                work(turn * 8 + which)
+            return carry
+
+        lax.fori_loop(0, blocks // 8, step, 0)
+
+    each(assign)
     for d in range(pairs):
         for t in range(2 * tiles_here):
             about_ref[d, 1, t] = count_ref[d * 2 * tiles_here + t].astype(jnp.float32)
@@ -87,27 +95,37 @@
     ]
     for copy in returns:
         copy.start()
+    for copy in loads[2:]:
+        copy.wait()
+    each(move)
     for copy in returns:
         copy.wait()
 
 
-def spread_parts(position, table_row):
-    position = jnp.broadcast_to(position, (16, 128))
-    delta = lax.broadcasted_iota(jnp.int32, (16, 128), 0) - (position >> 3)
-    index = (delta & 15) + ((position & 7) << 4)
-    table = jnp.broadcast_to(table_row, (8, 128))
-    taps = jnp.concatenate(
-        [
-            jnp.take_along_axis(table, index[:8], axis=1, mode="promise_in_bounds"),
-            jnp.take_along_axis(table, index[8:], axis=1, mode="promise_in_bounds"),
-        ],
-        axis=0,
-    )
-    return taps, (15 - delta) >> 4
+def unpack_kernel(slot_ref, returned_ref, residual_ref):
+    def step(turn, carry):
+        for which in range(8):
+            b = turn * 8 + which
+            residual_ref[b] = returned_ref[slot_ref[b]].astype(jnp.float32)
+        return carry
+
+    lax.fori_loop(0, residual_ref.shape[0] // 8, step, 0)
+
+
+def spread_parts(start, offset, table):
+    sublane = lax.broadcasted_iota(jnp.int32, (8, 128), 0)
+    taps, group = [], []
+    for low in (0, 8):
+        delta = sublane + low - start
+        taps.append(
+            jnp.take_along_axis(table, (delta & 15) + offset, axis=1, mode="promise_in_bounds")
+        )
+        group.append((15 - delta) >> 4)
+    return jnp.concatenate(taps, axis=0), jnp.concatenate(group, axis=0)
 
 
 def grid_kernel(pairs, capacity, member_ref, got_ref, table_ref, model_ref, residual_ref, own_ref,
-                other_ref, turned_ref, grid_ref, row_a, row_b, partial_a, partial_b, weighted_ref, code_ref, about_ref, list_ref, sem):
+                other_ref, turned_ref, grid_ref, row_a, row_b, partial_a, partial_b, weighted_a, weighted_b, code_ref, about_ref, list_ref, sem):
     tiles, side, wide = model_ref.shape
     groups = side // 16
     zero_row = table_ref.shape[0] - 8
@@ -133,10 +151,18 @@
             list_ref[start + u] = (zero_row << PLANE_SHIFT) + (t << TILE_SHIFT) + capacity
 
         def enlist(s, filled, t=t):
-            for k in range(capacity // 2):
-                place = k if t % 2 == 0 else capacity // 2 - 1 - k
-                list_ref[filled + k] = about_ref[s, 0, t // 2 * (capacity // 2) + place]
-            return filled + about_ref[s, 1, t]
+            first = t // 2 * (capacity // 2)
+            found = about_ref[s, 1, t]
+
+            def some(turn, carry):
+                for which in range(8):
+                    k = turn * 8 + which
+                    place = k if t % 2 == 0 else capacity // 2 - 1 - k
+                    list_ref[filled + k] = about_ref[s, 0, jnp.maximum(first + place, 0)]
+                return carry
+
+            lax.fori_loop(0, (found + 7) >> 3, some, 0)
+            return filled + found
 
         lax.fori_loop(0, pairs, enlist, start + spare)
         start = start + count + spare
@@ -148,15 +174,27 @@
     def read(which):
         entry = list_ref[which]
         slot = entry & ((1 << TILE_SHIFT) - 1)
-        return slot, table_ref[pl.ds(entry >> PLANE_SHIFT, 1), :], got_ref[slot]
+        data = got_ref[slot]
+        position = data.astype(jnp.int32)
+        start, offset = position >> 3, (position & 7) << 4
+        table = jnp.broadcast_to(table_ref[pl.ds(entry >> PLANE_SHIFT, 1), :], (8, 128))
+
+        def parts(row):
+            return spread_parts(
+                jnp.broadcast_to(start[row : row + 1], (8, 128)),
+                jnp.broadcast_to(offset[row : row + 1], (8, 128)),
+                table,
+            )
+
+        return slot, data, parts
 
     def chunk_tile(turn):
         return (list_ref[turn * UNROLL] >> TILE_SHIFT) & 15
 
     def front(turn, row_ref, partial_ref):
         for u in range(UNROLL):
-            _, table_row, data = read(turn * UNROLL + u)
-            taps, group = spread_parts(data[2:3].astype(jnp.int32), table_row)
+            _, _, parts = read(turn * UNROLL + u)
+            taps, group = parts(2)
             taps = taps.astype(jnp.bfloat16)
             group = group.astype(jnp.float32).astype(jnp.bfloat16)
             for k in range(groups):
@@ -167,11 +205,11 @@
             turned_ref[chunk_tile(turn)], row_ref[...], preferred_element_type=jnp.float32
         )
 
-    def back(turn, row_ref, partial_ref):
+    def back(turn, row_ref, partial_ref, weighted_ref):
         for u in range(UNROLL):
-            slot, table_row, data = read(turn * UNROLL + u)
+            slot, data, parts = read(turn * UNROLL + u)
             columns = slice(128 * u, 128 * u + 128)
-            taps, group = spread_parts(data[3:4].astype(jnp.int32), table_row)
+            taps, group = parts(3)
             residuals, samples = [], []
             for part in range(2):
                 picked = jnp.zeros((16, 128), jnp.float32)
@@ -199,9 +237,9 @@
 
     def step(turn, carry):
         front(2 * turn + 1, row_b, partial_b)
-        back(2 * turn, row_a, partial_a)
+        back(2 * turn, row_a, partial_a, weighted_a)
         front(2 * turn + 2, row_a, partial_a)
-        back(2 * turn + 1, row_b, partial_b)
+        back(2 * turn + 1, row_b, partial_b, weighted_b)
         return carry
 
     front(0, row_a, partial_a)
@@ -233,21 +271,22 @@
             jax.ShapeDtypeStruct((slots, 4, rows), jnp.float32),
             jax.ShapeDtypeStruct((blocks,), jnp.int32),
         ),
-        in_specs=[SMEM, SMEM, HBM, HBM, HBM],
+        in_specs=[HBM] * 5,
         out_specs=(VMEM, SMEM),
         scratch_shapes=[
+            pltpu.SMEM((blocks,), jnp.int32),
+            pltpu.SMEM((blocks,), jnp.int32),
             pltpu.VMEM((blocks, 2, rows), jnp.float32),
             pltpu.VMEM((blocks, 2, rows), jnp.int32),
             pltpu.VMEM((blocks, 2, rows), jnp.int32),
             pltpu.SMEM((pairs, 4, rows), jnp.float32),
             pltpu.SMEM((pairs * 2 * tiles_here,), jnp.int32),
-            pltpu.SemaphoreType.DMA((3,)),
+            pltpu.SemaphoreType.DMA((5,)),
             pltpu.SemaphoreType.DMA((pairs,)),
         ],
         compiler_params=WHOLE_PARAMS,
         name="pack_blocks",
     )(w_plane[0], block_tile[0], visibilities[0], uv_cell[0], sub_pixel[0])
-    sent, model_other = lax.optimization_barrier((sent, model_other))
     got = lax.all_to_all(
         sent, "tile", split_axis=0, concat_axis=0, tiled=True, axis_index_groups=halves
     )
@@ -276,6 +315,7 @@
             pltpu.VMEM((wide, UNROLL * rows), jnp.float32),
             pltpu.VMEM((wide, UNROLL * rows), jnp.float32),
             pltpu.VMEM((wide, UNROLL * rows), jnp.bfloat16),
+            pltpu.VMEM((wide, UNROLL * rows), jnp.bfloat16),
             pltpu.VMEM((pairs, 2, rows), jnp.int32),
             pltpu.SMEM((pairs, 2, rows), jnp.int32),
             pltpu.SMEM((slots + capacity + 2 * tiles_here * UNROLL + UNROLL,), jnp.int32),
@@ -288,16 +328,29 @@
     returned = lax.all_to_all(
         residual, "tile", split_axis=0, concat_axis=0, tiled=True, axis_index_groups=halves
     )
-    residuals = jnp.take(returned, slot, axis=0, mode="clip").astype(jnp.float32)[None]
     grid_sum = own + lax.ppermute(other, "tile", swap).astype(jnp.float32)
-    grid_rounded = grid_sum.astype(jnp.bfloat16)[None]
-    own_row = lax.dynamic_index_in_dim(coupling, lax.axis_index("freq"), 0, keepdims=False)
-    coupled_grid = jnp.sum(
-        own_row[:, None, None, None]
-        * lax.all_gather(grid_rounded, "freq", axis=0, tiled=True).astype(jnp.float32),
-        axis=0,
-    )[None]
-    return (residuals, coupled_grid)
+    grid_rounded = grid_sum.astype(jnp.bfloat16)
+    freqs = lax.axis_size("freq")
+    plane = lax.axis_index("freq")
+    own_row = lax.dynamic_index_in_dim(coupling, plane, 0, keepdims=False)
+    if freqs == 2:
+        grid_next = lax.ppermute(grid_rounded, "freq", [(0, 1), (1, 0)])
+        coupled_grid = own_row[plane] * grid_rounded.astype(jnp.float32) + own_row[
+            1 - plane
+        ] * grid_next.astype(jnp.float32)
+    else:
+        gathered = lax.all_gather(grid_rounded[None], "freq", axis=0, tiled=True)
+        coupled_grid = jnp.sum(own_row[:, None, None, None] * gathered.astype(jnp.float32), axis=0)
+    residuals = pl.pallas_call(
+        unpack_kernel,
+        out_shape=jax.ShapeDtypeStruct((blocks, 2, rows), jnp.float32),
+        in_specs=[SMEM, VMEM],
+        out_specs=VMEM,
+        compiler_params=PARAMS,
+        cost_estimate=pl.CostEstimate(flops=0, bytes_accessed=4000000, transcendentals=0),
+        name="unpack_residuals",
+    )(slot, returned)
+    return (residuals[None], coupled_grid[None])
 
 
 def solution(mesh):

time: 62 us -> 63.8 us (1.029)
  Pallas kernels: 9.12 us -> 24.8 us
  starting transfers between devices: 28.5 us -> 13.7 us
  waiting for transfers between devices: 12.2 us -> 21.5 us
  blocking collectives: 7.38 us -> 0 us
  local copies, waits for them, and re-layouts: 2.28 us -> 1.4 us
    pallas_call x1, Pallas kernels: 4.02 us -> 19.2 us  [body(): pl.pallas_call(lambda *refs: grid_kernel(pairs, capacity, *refs), out_sha...]
    all_to_all x1, starting transfers between devices: 17.3 us -> 4.18 us  [body(): lax.all_to_all(residual, 'tile', split_axis=0, concat_axis=0, tiled=True,...]
    all_to_all x1, waiting for transfers between devices: 10.8 us -> 2.05 us  [body(): lax.all_to_all(sent, 'tile', split_axis=0, concat_axis=0, tiled=True, axi...]
    ppermute x1, waiting for transfers between devices: 1.41 us -> 9.81 us  [body(): model_other = lax.ppermute(model_own, 'tile', swap)]
    all_gather x1 -> x0, blocking collectives: 7.38 us -> none  [body(): lax.all_gather(grid_rounded, 'freq', axis=0, tiled=True).astype(jnp.float32)]
    ppermute x1, waiting for transfers between devices: 0.01 us -> 7.33 us  [body(): grid_sum = own + lax.ppermute(other, 'tile', swap).astype(jnp.float32)]
    all_to_all x1, waiting for transfers between devices: 0.01 us -> 2.35 us  [body(): lax.all_to_all(residual, 'tile', split_axis=0, concat_axis=0, tiled=True,...]
    ppermute x1, starting transfers between devices: 3.55 us -> 1.41 us  [body(): grid_sum = own + lax.ppermute(other, 'tile', swap).astype(jnp.float32)]
  transfers between devices with their start and end apart: 4 -> 5, of which waited for: 2 -> 4; matrix products, arithmetic and copies ran while one was open for 2% -> 4% of each run, Pallas kernels for 8% -> 0%
where the time goes in v5:
time: 63.8 us; the launch traced here: 64.2 us
  Pallas kernels  24.8 us (39%)
  waiting for transfers between devices  21.5 us (34%)
  starting transfers between devices  13.7 us (21%)
  other arithmetic  2.06 us (3%)
  local copies, waits for them, and re-layouts  1.4 us (2%)
  between operations  0.7 us (1%)
    pallas_call x1, Pallas kernels, body(): pl.pallas_call(lambda *refs: grid_kernel(pairs, capacity, *refs), out_sha...  19.2 us
    ppermute x1, waiting for transfers between devices, body(): model_other = lax.ppermute(model_own, 'tile', swap)  9.81 us
    ppermute x1, waiting for transfers between devices, body(): grid_sum = own + lax.ppermute(other, 'tile', swap).astype(jnp.float32)  7.33 us
    all_to_all x1, starting transfers between devices, body(): lax.all_to_all(sent, 'tile', split_axis=0, concat_axis=0, tiled=True, axi...  5.4 us
    all_to_all x1, starting transfers between devices, body(): lax.all_to_all(residual, 'tile', split_axis=0, concat_axis=0, tiled=True,...  4.18 us
    pallas_call x1, Pallas kernels, body(): pl.pallas_call(lambda *refs: pack_kernel(pairs, capacity, tiles_here, pla...  4.17 us
    ppermute x1, starting transfers between devices, body(): model_other = lax.ppermute(model_own, 'tile', swap)  2.65 us
    all_to_all x1, waiting for transfers between devices, body(): lax.all_to_all(residual, 'tile', split_axis=0, concat_axis=0, tiled=True,...  2.35 us
  transfers between devices with their start and end apart: 5, of which 4 were waited for; matrix products, arithmetic and copies ran while one was open for 4% of the time, Pallas kernels for 0%

profile of v5, /device:TPU:0, one launch (start us, length us, event | category | flops | bytes accessed | tf_op | source)
XLA Modules:
  0.0 64.2 jit_solution(13938356921905276972)
XLA Ops:
  0.6 4.2 %pack_blocks.1 = (f32[392,4,128]{2,1,0:T(4,128)}, s32[128]{0:T(128)}) custom-call(s32[128]{0:T(128)} %bitcast.21, s32[128]{0:T(128)} %bitcast.22, f32[128,2,128]{2,1,0:T(2,128)} %bitcast.15, s32[128,2,128]{2,1,0:T(2,128)} %bitcast.16, s32[128,2,128]{2,1,0:T(2,128)} %bitcast.17), custom_call_target="tpu_custom_call" | custom-call | tf_op jit(solution)/shard_map/pack_blocks/pallas_call | solution.py:268
  4.8 0.0 copy-start.1
  4.8 5.4 %all-to-all-start = ((f32[392,4,128]{2,1,0:T(4,128)}), f32[392,4,128]{2,1,0:T(4,128)S(1)}, u32[]{:S(2)}, u32[]{:S(2)}) async-start(f32[392,4,128]{2,1,0:T(4,128)} %get-tuple-element.8), calls=%async_computation | async-start | bytes 1605632 | tf_op jit(solution)/shard_map/all_to_all | solution.py:290
  10.2 0.0 copy-start.2
  10.2 0.0 copy-done.1
  10.2 2.7 %collective-permute-start = (bf16[2,128,256]{2,1,0:T(8,128)(2,1)S(1)}, bf16[2,128,256]{2,1,0:T(8,128)(2,1)S(1)}, u32[]{:S(2)}, u32[]{:S(2)}) collective-permute-start(bf16[2,128,256]{2,1,0:T(8,128)(2,1)S(1)} %bitcast.18), channel_id=1, source_target_pairs={{0,16},{2,18},{4,20},{6,22},{8,24},{10,26},{12,28},{14,30},{16,0},... | collective-permute-start | bytes 393224 | tf_op jit(solution)/shard_map/ppermute | solution.py:267
  12.9 0.0 copy-done.2
  12.9 0.1 copy.12.refs_2_
  13.0 9.8 %collective-permute-done = bf16[2,128,256]{2,1,0:T(8,128)(2,1)S(1)} collective-permute-done((bf16[2,128,256]{2,1,0:T(8,128)(2,1)S(1)}, bf16[2,128,256]{2,1,0:T(8,128)(2,1)S(1)}, u32[]{:S(2)}, u32[]{:S(2)}) %collective-permute-start) | collective-permute-done | bytes 131104 | tf_op jit(solution)/shard_map/ppermute | solution.py:267
  22.8 2.0 %all-to-all-done.refs_1_ = f32[392,4,128]{2,1,0:T(4,128)S(1)} async-done(((f32[392,4,128]{2,1,0:T(4,128)}), f32[392,4,128]{2,1,0:T(4,128)S(1)}, u32[]{:S(2)}, u32[]{:S(2)}) %all-to-all-start) | async-done | bytes 802848 | tf_op jit(solution)/shard_map/all_to_all | solution.py:290
  24.9 19.2 %grid_blocks.1 = (bf16[392,2,128]{2,1,0:T(2,128)(2,1)}, f32[2,128,256]{2,1,0:T(8,128)S(1)}, bf16[2,128,256]{2,1,0:T(8,128)(2,1)S(1)}) custom-call(s32[1]{0:T(128)} %bitcast.5.refs_0_, f32[392,4,128]{2,1,0:T(4,128)S(1)} %all-to-all-done.refs_1_, f32[24,128]{1,0:T(8,128)S(1)} %copy.12.refs_2_, bf16[4,128,256]{2,1,0:T(8,128)(2,1)S(1)} %maximum_select_fusion.refs_3_), custom_call_target="tpu_custom_call" | custom-call | tf_op jit(solution)/shard_map/grid_blocks/pallas_call | solution.py:301
  44.1 1.4 %collective-permute-start.1 = (bf16[2,128,256]{2,1,0:T(8,128)(2,1)S(1)}, bf16[2,128,256]{2,1,0:T(8,128)(2,1)S(1)}, u32[]{:S(2)}, u32[]{:S(2)}) collective-permute-start(bf16[2,128,256]{2,1,0:T(8,128)(2,1)S(1)} %get-tuple-element.11), channel_id=1, source_target_pairs={{0,16},{2,18},{4,20},{6,22},{8,24},{10,26},{12,28},{14,30},{16,0},... | collective-permute-start | bytes 393224 | tf_op jit(solution)/shard_map/ppermute | solution.py:331
  45.5 7.3 %collective-permute-done.1 = bf16[2,128,256]{2,1,0:T(8,128)(2,1)S(1)} collective-permute-done((bf16[2,128,256]{2,1,0:T(8,128)(2,1)S(1)}, bf16[2,128,256]{2,1,0:T(8,128)(2,1)S(1)}, u32[]{:S(2)}, u32[]{:S(2)}) %collective-permute-start.1) | collective-permute-done | bytes 131104 | tf_op jit(solution)/shard_map/ppermute | solution.py:331
  52.9 0.1 collective-permute-start.2
  53.0 4.2 %all-to-all-start.1 = ((bf16[392,2,128]{2,1,0:T(2,128)(2,1)}), bf16[392,2,128]{2,1,0:T(2,128)(2,1)S(1)}, u32[]{:S(2)}, u32[]{:S(2)}) async-start(bf16[392,2,128]{2,1,0:T(2,128)(2,1)} %get-tuple-element.9), calls=%async_computation.1 | async-start | bytes 401408 | tf_op jit(solution)/shard_map/all_to_all | solution.py:328
  57.1 0.0 copy-start.3
  57.1 0.7 %copy-done.3 = f32[2,2]{1,0:T(2,128)S(1)} copy-done((f32[2,2]{1,0:T(2,128)S(1)}, f32[2,2]{1,0:T(2,128)}, u32[]{:S(2)}) %copy-start.3) | copy-done | bytes 40
  57.8 0.6 %fusion = (f32[1,1]{1,0:T(1,128)}, f32[1,1]{1,0:T(1,128)}) fusion(f32[2,2]{1,0:T(2,128)S(1)} %copy-done.3, s32[]{:T(128)S(6)} %select_n.29, s32[]{:T(128)S(6)} %select_n.31), kind=kLoop, calls=%fused_computation.4 | loop fusion | bytes 24 | tf_op jit(solution)/shard_map/dynamic_slice | solution.py:338
  58.5 0.0 collective-permute-done.2
  58.5 2.0 %add_bitcast_fusion = f32[1,2,128,256]{3,2,1,0:T(8,128)} fusion(bf16[2,128,256]{2,1,0:T(8,128)(2,1)S(1)} %collective-permute-done.2, bf16[2,128,256]{2,1,0:T(8,128)(2,1)S(1)} %add_convert_fusion, f32[]{:T(128)} %bitcast.10, f32[]{:T(128)} %bitcast.9), kind=kLoop, calls=%fused_computation.1 | loop fusion | flops 327680 | bytes 524296 | tf_op jit(solution)/shard_map/broadcast_in_dim | solution.py:353
  60.5 0.0 copy-start
  60.5 2.3 %all-to-all-done.1.returned_ref = bf16[392,2,128]{2,1,0:T(2,128)(2,1)S(1)} async-done(((bf16[392,2,128]{2,1,0:T(2,128)(2,1)}), bf16[392,2,128]{2,1,0:T(2,128)(2,1)S(1)}, u32[]{:S(2)}, u32[]{:S(2)}) %all-to-all-start.1) | async-done | bytes 200736 | tf_op jit(solution)/shard_map/all_to_all | solution.py:328
  62.8 0.0 copy-done
  62.8 1.4 %unpack_residuals.1 = f32[128,2,128]{2,1,0:T(2,128)} custom-call(s32[128]{0:T(128)S(1)} %copy-done, bf16[392,2,128]{2,1,0:T(2,128)(2,1)S(1)} %all-to-all-done.1.returned_ref), custom_call_target="tpu_custom_call" | custom-call | bytes 4000000 | tf_op jit(solution)/shard_map/unpack_residuals/pallas_call | solution.py:344
  (4 shorter events, 0.1 us)
Async XLA Ops:
  4.8 5.4 %copy-start.1 = (bf16[1,2,128,256]{3,2,1,0:T(8,128)(2,1)S(1)}, bf16[1,2,128,256]{3,2,1,0:T(8,128)(2,1)}, u32[]{:S(2)}) copy-start(bf16[1,2,128,256]{3,2,1,0:T(8,128)(2,1)} %param.13) | copy-start | bytes 393220
  4.8 20.0 %all-to-all-start = ((f32[392,4,128]{2,1,0:T(4,128)}), f32[392,4,128]{2,1,0:T(4,128)S(1)}, u32[]{:S(2)}, u32[]{:S(2)}) async-start(f32[392,4,128]{2,1,0:T(4,128)} %get-tuple-element.8), calls=%async_computation | async-start | bytes 1605632 | tf_op jit(solution)/shard_map/all_to_all | solution.py:290
  10.2 2.7 %copy-start.2 = (bf16[16,8,8]{0,2,1:T(8,128)(2,1)S(1)}, bf16[16,8,8]{0,2,1:T(8,128)(2,1)}, u32[]{:S(2)}) copy-start(bf16[16,8,8]{0,2,1:T(8,128)(2,1)} %param.14) | copy-start | bytes 6148
  10.2 12.5 %collective-permute-start = (bf16[2,128,256]{2,1,0:T(8,128)(2,1)S(1)}, bf16[2,128,256]{2,1,0:T(8,128)(2,1)S(1)}, u32[]{:S(2)}, u32[]{:S(2)}) collective-permute-start(bf16[2,128,256]{2,1,0:T(8,128)(2,1)S(1)} %bitcast.18), channel_id=1, source_target_pairs={{0,16},{2,18},{4,20},{6,22},{8,24},{10,26},{12,28},{14,30},{16,0},... | collective-permute-start | bytes 393224 | tf_op jit(solution)/shard_map/ppermute | solution.py:267
  44.1 8.7 %collective-permute-start.1 = (bf16[2,128,256]{2,1,0:T(8,128)(2,1)S(1)}, bf16[2,128,256]{2,1,0:T(8,128)(2,1)S(1)}, u32[]{:S(2)}, u32[]{:S(2)}) collective-permute-start(bf16[2,128,256]{2,1,0:T(8,128)(2,1)S(1)} %get-tuple-element.11), channel_id=1, source_target_pairs={{0,16},{2,18},{4,20},{6,22},{8,24},{10,26},{12,28},{14,30},{16,0},... | collective-permute-start | bytes 393224 | tf_op jit(solution)/shard_map/ppermute | solution.py:331
  52.9 5.6 %collective-permute-start.2 = (bf16[2,128,256]{2,1,0:T(8,128)(2,1)S(1)}, bf16[2,128,256]{2,1,0:T(8,128)(2,1)S(1)}, u32[]{:S(2)}, u32[]{:S(2)}) collective-permute-start(bf16[2,128,256]{2,1,0:T(8,128)(2,1)S(1)} %add_convert_fusion), channel_id=1, source_target_pairs={{0,1},{1,0},{2,3},{3,2},{4,5},{5,4},{6,7},{7,6},{8,9},{9,8},{10,11... | collective-permute-start | bytes 393224 | tf_op jit(solution)/shard_map/ppermute | solution.py:337
  53.0 9.9 %all-to-all-start.1 = ((bf16[392,2,128]{2,1,0:T(2,128)(2,1)}), bf16[392,2,128]{2,1,0:T(2,128)(2,1)S(1)}, u32[]{:S(2)}, u32[]{:S(2)}) async-start(bf16[392,2,128]{2,1,0:T(2,128)(2,1)} %get-tuple-element.9), calls=%async_computation.1 | async-start | bytes 401408 | tf_op jit(solution)/shard_map/all_to_all | solution.py:328
  57.1 0.7 %copy-start.3 = (f32[2,2]{1,0:T(2,128)S(1)}, f32[2,2]{1,0:T(2,128)}, u32[]{:S(2)}) copy-start(f32[2,2]{1,0:T(2,128)} %param.15) | copy-start | bytes 52
  60.5 2.4 %copy-start = (s32[128]{0:T(128)S(1)}, s32[128]{0:T(128)}, u32[]{:S(2)}) copy-start(s32[128]{0:T(128)} %get-tuple-element.7.slot_ref) | copy-start | bytes 1540

commit v6 on v5

--- a/solution.py
+++ b/solution.py
@@ -5,7 +5,7 @@
 from jax.experimental.pallas import tpu as pltpu
 from jax.sharding import PartitionSpec as P
 
-UNROLL = 4
+UNROLL = 8
 VMEM = pl.BlockSpec(memory_space=pltpu.VMEM)
 SMEM = pl.BlockSpec(memory_space=pltpu.SMEM)
 HBM = pl.BlockSpec(memory_space=pltpu.HBM)
@@ -102,7 +102,17 @@
         copy.wait()
 
 
-def unpack_kernel(slot_ref, returned_ref, residual_ref):
+def finish_kernel(plane_ref, coupling_ref, slot_ref, returned_ref, *refs):
+    *grid_refs, residual_ref, coupled_ref = refs
+    plane = plane_ref[0]
+    if len(grid_refs) == 2:
+        grids = [(plane, grid_refs[0]), (1 - plane, grid_refs[1])]
+    else:
+        grids = [(g, grid_refs[0].at[g]) for g in range(grid_refs[0].shape[0])]
+    coupled_ref[...] = sum(
+        coupling_ref[plane, g] * grid_ref[...].astype(jnp.float32) for g, grid_ref in grids
+    )
+
     def step(turn, carry):
         for which in range(8):
             b = turn * 8 + which
@@ -328,28 +338,23 @@
     returned = lax.all_to_all(
         residual, "tile", split_axis=0, concat_axis=0, tiled=True, axis_index_groups=halves
     )
-    grid_sum = own + lax.ppermute(other, "tile", swap).astype(jnp.float32)
-    grid_rounded = grid_sum.astype(jnp.bfloat16)
-    freqs = lax.axis_size("freq")
-    plane = lax.axis_index("freq")
-    own_row = lax.dynamic_index_in_dim(coupling, plane, 0, keepdims=False)
-    if freqs == 2:
-        grid_next = lax.ppermute(grid_rounded, "freq", [(0, 1), (1, 0)])
-        coupled_grid = own_row[plane] * grid_rounded.astype(jnp.float32) + own_row[
-            1 - plane
-        ] * grid_next.astype(jnp.float32)
+    got_other, returned = lax.optimization_barrier((lax.ppermute(other, "tile", swap), returned))
+    grid_rounded = (own + got_other.astype(jnp.float32)).astype(jnp.bfloat16)
+    if lax.axis_size("freq") == 2:
+        grids = [grid_rounded, lax.ppermute(grid_rounded, "freq", [(0, 1), (1, 0)])]
     else:
-        gathered = lax.all_gather(grid_rounded[None], "freq", axis=0, tiled=True)
-        coupled_grid = jnp.sum(own_row[:, None, None, None] * gathered.astype(jnp.float32), axis=0)
-    residuals = pl.pallas_call(
-        unpack_kernel,
-        out_shape=jax.ShapeDtypeStruct((blocks, 2, rows), jnp.float32),
-        in_specs=[SMEM, VMEM],
-        out_specs=VMEM,
+        grids = [lax.all_gather(grid_rounded, "freq", axis=0)]
+    residuals, coupled_grid = pl.pallas_call(
+        finish_kernel,
+        out_shape=(
+            jax.ShapeDtypeStruct((blocks, 2, rows), jnp.float32),
+            jax.ShapeDtypeStruct((tiles_here, side, wide), jnp.float32),
+        ),
+        in_specs=[SMEM, SMEM, SMEM, VMEM] + [VMEM] * len(grids),
+        out_specs=(VMEM, VMEM),
         compiler_params=PARAMS,
-        cost_estimate=pl.CostEstimate(flops=0, bytes_accessed=4000000, transcendentals=0),
-        name="unpack_residuals",
-    )(slot, returned)
+        name="finish",
+    )(lax.axis_index("freq")[None], coupling, slot, returned, *grids)
     return (residuals[None], coupled_grid[None])
 
 

time: 63.8 us -> 63.8 us (level)
  Pallas kernels: 24.8 us -> 22 us
  starting transfers between devices: 13.7 us -> 16.3 us
  waiting for transfers between devices: 21.5 us -> 24 us
  other arithmetic: 2.06 us -> 0.07 us
  local copies, waits for them, and re-layouts: 1.4 us -> 0.75 us
    ppermute x2, waiting for transfers between devices: 7.33 us -> 12.2 us  [the longest x1 8.8 us: body(): lax.ppermute(other, 'tile', swap)]
    pallas_call x1, Pallas kernels: 19.2 us -> 16.3 us  [body(): pl.pallas_call(lambda *refs: grid_kernel(pairs, capacity, *refs), out_sha...]
    all_to_all x1, waiting for transfers between devices: 2.35 us -> 0.01 us  [body(): lax.all_to_all(residual, 'tile', split_axis=0, concat_axis=0, tiled=True,...]
    broadcast_in_dim x1 -> x0, other arithmetic: 1.99 us -> none  [body(): return (residuals[None], coupled_grid[None])]
    ppermute x2, starting transfers between devices: 1.48 us -> 3.28 us  [the longest x1 2.41 us: body(): grids = [grid_rounded, lax.ppermute(grid_rounded, 'freq', [(0, 1), (1, 0)])]]
    all_to_all x1, starting transfers between devices: 4.18 us -> 4.97 us  [body(): lax.all_to_all(residual, 'tile', split_axis=0, concat_axis=0, tiled=True,...]
    dynamic_slice x1 -> x0, local copies, waits for them, and re-layouts: 0.65 us -> none  [body(): own_row[plane] * grid_rounded.astype(jnp.float32)]
  transfers between devices with their start and end apart: 5 -> 5, of which waited for: 4 -> 4; matrix products, arithmetic and copies ran while one was open for 4% -> 0% of each run, Pallas kernels for 0% -> 0%
where the time goes in v6:
time: 63.8 us
  waiting for transfers between devices  24 us (38%)
  Pallas kernels  22 us (34%)
  starting transfers between devices  16.3 us (26%)
  local copies, waits for them, and re-layouts  0.75 us (1%)
  between operations  0.69 us (1%)
    pallas_call x1, Pallas kernels, body(): pl.pallas_call(lambda *refs: grid_kernel(pairs, capacity, *refs), out_sha...  16.3 us
    ppermute x1, waiting for transfers between devices, body(): model_other = lax.ppermute(model_own, 'tile', swap)  9.81 us
    ppermute x1, waiting for transfers between devices, body(): lax.ppermute(other, 'tile', swap)  8.8 us
    all_to_all x1, starting transfers between devices, body(): lax.all_to_all(sent, 'tile', split_axis=0, concat_axis=0, tiled=True, axi...  5.4 us
    all_to_all x1, starting transfers between devices, body(): lax.all_to_all(residual, 'tile', split_axis=0, concat_axis=0, tiled=True,...  4.97 us
    pallas_call x1, Pallas kernels, body(): pl.pallas_call(lambda *refs: pack_kernel(pairs, capacity, tiles_here, pla...  4.17 us
    ppermute x1, waiting for transfers between devices, body(): grids = [grid_rounded, lax.ppermute(grid_rounded, 'freq', [(0, 1), (1, 0)])]  3.39 us
    ppermute x1, starting transfers between devices, body(): model_other = lax.ppermute(model_own, 'tile', swap)  2.65 us
  transfers between devices with their start and end apart: 5, of which 4 were waited for; matrix products, arithmetic and copies ran while one was open for 0% of the time, Pallas kernels for 0%

profile of v6, /device:TPU:0, one launch (start us, length us, event | category | flops | bytes accessed | tf_op | source)
XLA Modules:
  0.0 63.8 jit_solution(8917590279746212147)
XLA Ops:
  0.6 4.2 %pack_blocks.1 = (f32[392,4,128]{2,1,0:T(4,128)}, s32[128]{0:T(128)}) custom-call(s32[128]{0:T(128)} %bitcast.18, s32[128]{0:T(128)} %bitcast.19, f32[128,2,128]{2,1,0:T(2,128)} %bitcast.13, s32[128,2,128]{2,1,0:T(2,128)} %bitcast.14, s32[128,2,128]{2,1,0:T(2,128)} %bitcast.15), custom_call_target="tpu_custom_call" | custom-call | tf_op jit(solution)/shard_map/pack_blocks/pallas_call | solution.py:278
  4.8 0.0 copy-start.2
  4.8 5.4 %all-to-all-start = ((f32[392,4,128]{2,1,0:T(4,128)}), f32[392,4,128]{2,1,0:T(4,128)S(1)}, u32[]{:S(2)}, u32[]{:S(2)}) async-start(f32[392,4,128]{2,1,0:T(4,128)} %get-tuple-element.12), calls=%async_computation | async-start | bytes 1605632 | tf_op jit(solution)/shard_map/all_to_all | solution.py:300
  10.2 0.0 copy-start.3
  10.2 0.0 copy-done.2
  10.2 2.7 %collective-permute-start = (bf16[2,128,256]{2,1,0:T(8,128)(2,1)S(1)}, bf16[2,128,256]{2,1,0:T(8,128)(2,1)S(1)}, u32[]{:S(2)}, u32[]{:S(2)}) collective-permute-start(bf16[2,128,256]{2,1,0:T(8,128)(2,1)S(1)} %bitcast.16), channel_id=1, source_target_pairs={{0,16},{2,18},{4,20},{6,22},{8,24},{10,26},{12,28},{14,30},{16,0},... | collective-permute-start | bytes 393224 | tf_op jit(solution)/shard_map/ppermute | solution.py:277
  12.9 0.0 copy-done.3
  12.9 0.1 copy.12.refs_2_
  13.0 9.8 %collective-permute-done = bf16[2,128,256]{2,1,0:T(8,128)(2,1)S(1)} collective-permute-done((bf16[2,128,256]{2,1,0:T(8,128)(2,1)S(1)}, bf16[2,128,256]{2,1,0:T(8,128)(2,1)S(1)}, u32[]{:S(2)}, u32[]{:S(2)}) %collective-permute-start) | collective-permute-done | bytes 131104 | tf_op jit(solution)/shard_map/ppermute | solution.py:277
  22.8 2.0 %all-to-all-done.refs_1_ = f32[392,4,128]{2,1,0:T(4,128)S(1)} async-done(((f32[392,4,128]{2,1,0:T(4,128)}), f32[392,4,128]{2,1,0:T(4,128)S(1)}, u32[]{:S(2)}, u32[]{:S(2)}) %all-to-all-start) | async-done | bytes 802848 | tf_op jit(solution)/shard_map/all_to_all | solution.py:300
  24.9 16.3 %grid_blocks.1 = (bf16[392,2,128]{2,1,0:T(2,128)(2,1)}, f32[2,128,256]{2,1,0:T(8,128)S(1)}, bf16[2,128,256]{2,1,0:T(8,128)(2,1)S(1)}) custom-call(s32[1]{0:T(128)} %bitcast.6.refs_0_, f32[392,4,128]{2,1,0:T(4,128)S(1)} %all-to-all-done.refs_1_, f32[24,128]{1,0:T(8,128)S(1)} %copy.12.refs_2_, bf16[4,128,256]{2,1,0:T(8,128)(2,1)S(1)} %maximum_select_fusion.refs_3_), custom_call_target="tpu_custom_call" | custom-call | tf_op jit(solution)/shard_map/grid_blocks/pallas_call | solution.py:311
  41.1 5.0 %all-to-all-start.1 = ((bf16[392,2,128]{2,1,0:T(2,128)(2,1)}), bf16[392,2,128]{2,1,0:T(2,128)(2,1)S(1)}, u32[]{:S(2)}, u32[]{:S(2)}) async-start(bf16[392,2,128]{2,1,0:T(2,128)(2,1)} %get-tuple-element.14), calls=%async_computation.1 | async-start | bytes 401408 | tf_op jit(solution)/shard_map/all_to_all | solution.py:338
  46.1 0.9 %collective-permute-start.1 = (bf16[2,128,256]{2,1,0:T(8,128)(2,1)S(1)}, bf16[2,128,256]{2,1,0:T(8,128)(2,1)S(1)}, u32[]{:S(2)}, u32[]{:S(2)}) collective-permute-start(bf16[2,128,256]{2,1,0:T(8,128)(2,1)S(1)} %get-tuple-element.13), channel_id=1, source_target_pairs={{0,16},{2,18},{4,20},{6,22},{8,24},{10,26},{12,28},{14,30},{16,0},... | collective-permute-start | bytes 393224 | tf_op jit(solution)/shard_map/ppermute | solution.py:341
  47.0 8.8 %collective-permute-done.1 = bf16[2,128,256]{2,1,0:T(8,128)(2,1)S(1)} collective-permute-done((bf16[2,128,256]{2,1,0:T(8,128)(2,1)S(1)}, bf16[2,128,256]{2,1,0:T(8,128)(2,1)S(1)}, u32[]{:S(2)}, u32[]{:S(2)}) %collective-permute-start.1) | collective-permute-done | bytes 131104 | tf_op jit(solution)/shard_map/ppermute | solution.py:341
  55.8 0.0 all-to-all-done.1.returned_ref
  55.8 2.4 %collective-permute-start.2 = (bf16[2,128,256]{2,1,0:T(8,128)(2,1)S(1)}, bf16[2,128,256]{2,1,0:T(8,128)(2,1)S(1)}, u32[]{:S(2)}, u32[]{:S(2)}) collective-permute-start(bf16[2,128,256]{2,1,0:T(8,128)(2,1)S(1)} %add_convert_fusion.refs_0_), channel_id=1, source_target_pairs={{0,1},{1,0},{2,3},{3,2},{4,5},{5,4},{6,7},{7,6},{8,9},{9,8},{10,11... | collective-permute-start | bytes 393224 | tf_op jit(solution)/shard_map/ppermute | solution.py:344
  58.2 3.4 %collective-permute-done.2.refs_1_ = bf16[2,128,256]{2,1,0:T(8,128)(2,1)S(1)} collective-permute-done((bf16[2,128,256]{2,1,0:T(8,128)(2,1)S(1)}, bf16[2,128,256]{2,1,0:T(8,128)(2,1)S(1)}, u32[]{:S(2)}, u32[]{:S(2)}) %collective-permute-start.2) | collective-permute-done | bytes 131104 | tf_op jit(solution)/shard_map/ppermute | solution.py:344
  61.6 0.0 copy-start
  61.6 0.0 copy-start.1
  61.6 0.7 %copy-done = f32[2,2]{1,0:T(2,128)S(1)} copy-done((f32[2,2]{1,0:T(2,128)S(1)}, f32[2,2]{1,0:T(2,128)}, u32[]{:S(2)}) %copy-start) | copy-done | bytes 40
  62.3 0.0 copy-done.1
  62.3 1.5 %finish.1 = (f32[128,2,128]{2,1,0:T(2,128)}, f32[2,128,256]{2,1,0:T(8,128)}) custom-call(s32[1]{0:T(128)} %bitcast.plane_ref, f32[2,2]{1,0:T(2,128)S(1)} %copy-done, s32[128]{0:T(128)S(1)} %copy-done.1, bf16[392,2,128]{2,1,0:T(2,128)(2,1)S(1)} %all-to-all-done.1.returned_ref, bf16[2,128,256]{2,1,0:T(8,128)(2,1)S(1)} %add_convert_fusion.refs_0_, ...), custom_call_target="tpu_custom_call" | custom-call | tf_op jit(solution)/shard_map/finish/pallas_call | solution.py:347
  (4 shorter events, 0.1 us)
Async XLA Ops:
  4.8 5.4 %copy-start.2 = (bf16[1,2,128,256]{3,2,1,0:T(8,128)(2,1)S(1)}, bf16[1,2,128,256]{3,2,1,0:T(8,128)(2,1)}, u32[]{:S(2)}) copy-start(bf16[1,2,128,256]{3,2,1,0:T(8,128)(2,1)} %param.13) | copy-start | bytes 393220
  4.8 20.0 %all-to-all-start = ((f32[392,4,128]{2,1,0:T(4,128)}), f32[392,4,128]{2,1,0:T(4,128)S(1)}, u32[]{:S(2)}, u32[]{:S(2)}) async-start(f32[392,4,128]{2,1,0:T(4,128)} %get-tuple-element.12), calls=%async_computation | async-start | bytes 1605632 | tf_op jit(solution)/shard_map/all_to_all | solution.py:300
  10.2 2.7 %copy-start.3 = (bf16[16,8,8]{0,2,1:T(8,128)(2,1)S(1)}, bf16[16,8,8]{0,2,1:T(8,128)(2,1)}, u32[]{:S(2)}) copy-start(bf16[16,8,8]{0,2,1:T(8,128)(2,1)} %param.14) | copy-start | bytes 6148
  10.2 12.5 %collective-permute-start = (bf16[2,128,256]{2,1,0:T(8,128)(2,1)S(1)}, bf16[2,128,256]{2,1,0:T(8,128)(2,1)S(1)}, u32[]{:S(2)}, u32[]{:S(2)}) collective-permute-start(bf16[2,128,256]{2,1,0:T(8,128)(2,1)S(1)} %bitcast.16), channel_id=1, source_target_pairs={{0,16},{2,18},{4,20},{6,22},{8,24},{10,26},{12,28},{14,30},{16,0},... | collective-permute-start | bytes 393224 | tf_op jit(solution)/shard_map/ppermute | solution.py:277
  41.1 14.6 %all-to-all-start.1 = ((bf16[392,2,128]{2,1,0:T(2,128)(2,1)}), bf16[392,2,128]{2,1,0:T(2,128)(2,1)S(1)}, u32[]{:S(2)}, u32[]{:S(2)}) async-start(bf16[392,2,128]{2,1,0:T(2,128)(2,1)} %get-tuple-element.14), calls=%async_computation.1 | async-start | bytes 401408 | tf_op jit(solution)/shard_map/all_to_all | solution.py:338
  46.1 9.7 %collective-permute-start.1 = (bf16[2,128,256]{2,1,0:T(8,128)(2,1)S(1)}, bf16[2,128,256]{2,1,0:T(8,128)(2,1)S(1)}, u32[]{:S(2)}, u32[]{:S(2)}) collective-permute-start(bf16[2,128,256]{2,1,0:T(8,128)(2,1)S(1)} %get-tuple-element.13), channel_id=1, source_target_pairs={{0,16},{2,18},{4,20},{6,22},{8,24},{10,26},{12,28},{14,30},{16,0},... | collective-permute-start | bytes 393224 | tf_op jit(solution)/shard_map/ppermute | solution.py:341
  55.8 5.8 %collective-permute-start.2 = (bf16[2,128,256]{2,1,0:T(8,128)(2,1)S(1)}, bf16[2,128,256]{2,1,0:T(8,128)(2,1)S(1)}, u32[]{:S(2)}, u32[]{:S(2)}) collective-permute-start(bf16[2,128,256]{2,1,0:T(8,128)(2,1)S(1)} %add_convert_fusion.refs_0_), channel_id=1, source_target_pairs={{0,1},{1,0},{2,3},{3,2},{4,5},{5,4},{6,7},{7,6},{8,9},{9,8},{10,11... | collective-permute-start | bytes 393224 | tf_op jit(solution)/shard_map/ppermute | solution.py:344
  61.6 0.7 %copy-start = (f32[2,2]{1,0:T(2,128)S(1)}, f32[2,2]{1,0:T(2,128)}, u32[]{:S(2)}) copy-start(f32[2,2]{1,0:T(2,128)} %coupling_ref.1) | copy-start | bytes 52
  61.6 0.7 %copy-start.1 = (s32[128]{0:T(128)S(1)}, s32[128]{0:T(128)}, u32[]{:S(2)}) copy-start(s32[128]{0:T(128)} %get-tuple-element.11.slot_ref) | copy-start | bytes 1540

commit v7 on v6

--- a/solution.py
+++ b/solution.py
@@ -102,15 +102,10 @@
         copy.wait()
 
 
-def finish_kernel(plane_ref, coupling_ref, slot_ref, returned_ref, *refs):
-    *grid_refs, residual_ref, coupled_ref = refs
-    plane = plane_ref[0]
-    if len(grid_refs) == 2:
-        grids = [(plane, grid_refs[0]), (1 - plane, grid_refs[1])]
-    else:
-        grids = [(g, grid_refs[0].at[g]) for g in range(grid_refs[0].shape[0])]
+def finish_kernel(plane_ref, coupling_ref, slot_ref, returned_ref, grid_ref, residual_ref, coupled_ref):
     coupled_ref[...] = sum(
-        coupling_ref[plane, g] * grid_ref[...].astype(jnp.float32) for g, grid_ref in grids
+        coupling_ref[plane_ref[0], g] * grid_ref[g].astype(jnp.float32)
+        for g in range(grid_ref.shape[0])
     )
 
     def step(turn, carry):
@@ -179,7 +174,6 @@
     for u in range(2 * UNROLL):
         list_ref[start + u] = (zero_row << PLANE_SHIFT) + capacity
     chunks = start >> UNROLL.bit_length() - 1
-    zero = jnp.zeros((16, 128), jnp.bfloat16)
 
     def read(which):
         entry = list_ref[which]
@@ -205,12 +199,10 @@
         for u in range(UNROLL):
             _, _, parts = read(turn * UNROLL + u)
             taps, group = parts(2)
-            taps = taps.astype(jnp.bfloat16)
-            group = group.astype(jnp.float32).astype(jnp.bfloat16)
             for k in range(groups):
                 row_ref[16 * k : 16 * k + 16, 128 * u : 128 * u + 128] = jnp.where(
-                    group == k, taps, zero
-                )
+                    group == k, taps, 0.0
+                ).astype(jnp.bfloat16)
         partial_ref[...] = jnp.dot(
             turned_ref[chunk_tile(turn)], row_ref[...], preferred_element_type=jnp.float32
         )
@@ -229,15 +221,14 @@
                 model = jnp.sum(picked * taps, axis=0, keepdims=True)
                 residual = data[part : part + 1] - model
                 residuals.append(residual)
-                samples.append((residual * taps).astype(jnp.bfloat16))
+                samples.append(residual * taps)
             residual_ref[slot] = jnp.concatenate(residuals, axis=0).astype(jnp.bfloat16)
-            group = group.astype(jnp.float32).astype(jnp.bfloat16)
             for part in range(2):
                 for k in range(groups):
                     low = part * side + 16 * k
                     weighted_ref[low : low + 16, columns] = jnp.where(
-                        group == k, samples[part], zero
-                    )
+                        group == k, samples[part], 0.0
+                    ).astype(jnp.bfloat16)
         grid_ref[chunk_tile(turn)] += lax.dot_general(
             row_ref[...],
             weighted_ref[...],
@@ -338,23 +329,19 @@
     returned = lax.all_to_all(
         residual, "tile", split_axis=0, concat_axis=0, tiled=True, axis_index_groups=halves
     )
-    got_other, returned = lax.optimization_barrier((lax.ppermute(other, "tile", swap), returned))
-    grid_rounded = (own + got_other.astype(jnp.float32)).astype(jnp.bfloat16)
-    if lax.axis_size("freq") == 2:
-        grids = [grid_rounded, lax.ppermute(grid_rounded, "freq", [(0, 1), (1, 0)])]
-    else:
-        grids = [lax.all_gather(grid_rounded, "freq", axis=0)]
+    grid_sum = own + lax.ppermute(other, "tile", swap).astype(jnp.float32)
+    grids = lax.all_gather(grid_sum.astype(jnp.bfloat16)[None], "freq", axis=0, tiled=True)
     residuals, coupled_grid = pl.pallas_call(
         finish_kernel,
         out_shape=(
             jax.ShapeDtypeStruct((blocks, 2, rows), jnp.float32),
             jax.ShapeDtypeStruct((tiles_here, side, wide), jnp.float32),
         ),
-        in_specs=[SMEM, SMEM, SMEM, VMEM] + [VMEM] * len(grids),
+        in_specs=[SMEM, SMEM, SMEM, VMEM, VMEM],
         out_specs=(VMEM, VMEM),
         compiler_params=PARAMS,
         name="finish",
-    )(lax.axis_index("freq")[None], coupling, slot, returned, *grids)
+    )(lax.axis_index("freq")[None], coupling, slot, returned, grids)
     return (residuals[None], coupled_grid[None])
 
 

time: 63.8 us -> 59.3 us (0.929)
  waiting for transfers between devices: 24 us -> 11.9 us
  Pallas kernels: 22 us -> 10.4 us
  starting transfers between devices: 16.3 us -> 26.6 us
  blocking collectives: 0 us -> 8.38 us
    ppermute x2 -> x1, waiting for transfers between devices: 12.2 us -> 0.01 us  [body(): grid_sum = own + lax.ppermute(other, 'tile', swap).astype(jnp.float32)]
    all_to_all x1, starting transfers between devices: 4.97 us -> 17.1 us  [body(): lax.all_to_all(residual, 'tile', split_axis=0, concat_axis=0, tiled=True,...]
    pallas_call x1, Pallas kernels: 16.3 us -> 4.74 us  [body(): pl.pallas_call(lambda *refs: grid_kernel(pairs, capacity, *refs), out_sha...]
    all_gather x0 -> x1, blocking collectives: none -> 8.38 us  [body(): lax.all_gather(grid_sum.astype(jnp.bfloat16)[None], 'freq', axis=0, tiled...]
    ppermute x2 -> x1, starting transfers between devices: 3.28 us -> 1.39 us  [body(): grid_sum = own + lax.ppermute(other, 'tile', swap).astype(jnp.float32)]
  transfers between devices with their start and end apart: 5 -> 4, of which waited for: 4 -> 2; matrix products, arithmetic and copies ran while one was open for 0% -> 0% of each run, Pallas kernels for 0% -> 0%
where the time goes in v7:
time: 59.3 us; the launch traced here: 58.8 us
  starting transfers between devices  26.6 us (45%)
  waiting for transfers between devices  11.9 us (20%)
  Pallas kernels  10.4 us (18%)
  blocking collectives  8.38 us (14%)
  local copies, waits for them, and re-layouts  0.75 us (1%)
  between operations  0.69 us (1%)
    all_to_all x1, starting transfers between devices, body(): lax.all_to_all(residual, 'tile', split_axis=0, concat_axis=0, tiled=True,...  17.1 us
    ppermute x1, waiting for transfers between devices, body(): model_other = lax.ppermute(model_own, 'tile', swap)  9.81 us
    all_gather x1, blocking collectives, body(): lax.all_gather(grid_sum.astype(jnp.bfloat16)[None], 'freq', axis=0, tiled...  8.38 us
    all_to_all x1, starting transfers between devices, body(): lax.all_to_all(sent, 'tile', split_axis=0, concat_axis=0, tiled=True, axi...  5.4 us
    pallas_call x1, Pallas kernels, body(): pl.pallas_call(lambda *refs: grid_kernel(pairs, capacity, *refs), out_sha...  4.74 us
    pallas_call x1, Pallas kernels, body(): pl.pallas_call(lambda *refs: pack_kernel(pairs, capacity, tiles_here, pla...  4.16 us
    ppermute x1, starting transfers between devices, body(): model_other = lax.ppermute(model_own, 'tile', swap)  2.65 us
    all_to_all x1, waiting for transfers between devices, body(): lax.all_to_all(sent, 'tile', split_axis=0, concat_axis=0, tiled=True, axi...  2.05 us
  transfers between devices with their start and end apart: 4, of which 2 were waited for; matrix products, arithmetic and copies ran while one was open for 0% of the time, Pallas kernels for 0%

profile of v7, /device:TPU:0, one launch (start us, length us, event | category | flops | bytes accessed | tf_op | source)
XLA Modules:
  0.0 58.8 jit_solution(8012926857423823716)
XLA Ops:
  0.6 4.2 %pack_blocks.1 = (f32[392,4,128]{2,1,0:T(4,128)}, s32[128]{0:T(128)}) custom-call(s32[128]{0:T(128)} %bitcast.20, s32[128]{0:T(128)} %bitcast.21, f32[128,2,128]{2,1,0:T(2,128)} %bitcast.15, s32[128,2,128]{2,1,0:T(2,128)} %bitcast.16, s32[128,2,128]{2,1,0:T(2,128)} %bitcast.17), custom_call_target="tpu_custom_call" | custom-call | tf_op jit(solution)/shard_map/pack_blocks/pallas_call | solution.py:269
  4.8 0.0 copy-start.2
  4.8 5.4 %all-to-all-start = ((f32[392,4,128]{2,1,0:T(4,128)}), f32[392,4,128]{2,1,0:T(4,128)S(1)}, u32[]{:S(2)}, u32[]{:S(2)}) async-start(f32[392,4,128]{2,1,0:T(4,128)} %get-tuple-element.10), calls=%async_computation | async-start | bytes 1605632 | tf_op jit(solution)/shard_map/all_to_all | solution.py:291
  10.2 0.0 copy-start.3
  10.2 0.0 copy-done.2
  10.2 2.7 %collective-permute-start = (bf16[2,128,256]{2,1,0:T(8,128)(2,1)S(1)}, bf16[2,128,256]{2,1,0:T(8,128)(2,1)S(1)}, u32[]{:S(2)}, u32[]{:S(2)}) collective-permute-start(bf16[2,128,256]{2,1,0:T(8,128)(2,1)S(1)} %bitcast.18), channel_id=1, source_target_pairs={{0,16},{2,18},{4,20},{6,22},{8,24},{10,26},{12,28},{14,30},{16,0},... | collective-permute-start | bytes 393224 | tf_op jit(solution)/shard_map/ppermute | solution.py:268
  12.9 0.0 copy-done.3
  12.9 0.1 copy.13.refs_2_
  13.0 9.8 %collective-permute-done = bf16[2,128,256]{2,1,0:T(8,128)(2,1)S(1)} collective-permute-done((bf16[2,128,256]{2,1,0:T(8,128)(2,1)S(1)}, bf16[2,128,256]{2,1,0:T(8,128)(2,1)S(1)}, u32[]{:S(2)}, u32[]{:S(2)}) %collective-permute-start) | collective-permute-done | bytes 131104 | tf_op jit(solution)/shard_map/ppermute | solution.py:268
  22.8 2.0 %all-to-all-done.refs_1_ = f32[392,4,128]{2,1,0:T(4,128)S(1)} async-done(((f32[392,4,128]{2,1,0:T(4,128)}), f32[392,4,128]{2,1,0:T(4,128)S(1)}, u32[]{:S(2)}, u32[]{:S(2)}) %all-to-all-start) | async-done | bytes 802848 | tf_op jit(solution)/shard_map/all_to_all | solution.py:291
  24.8 4.7 %grid_blocks.1 = (bf16[392,2,128]{2,1,0:T(2,128)(2,1)}, f32[2,128,256]{2,1,0:T(8,128)S(1)}, bf16[2,128,256]{2,1,0:T(8,128)(2,1)S(1)}) custom-call(s32[1]{0:T(128)} %bitcast.6.refs_0_, f32[392,4,128]{2,1,0:T(4,128)S(1)} %all-to-all-done.refs_1_, f32[24,128]{1,0:T(8,128)S(1)} %copy.13.refs_2_, bf16[4,128,256]{2,1,0:T(8,128)(2,1)S(1)} %maximum_select_fusion.refs_3_), custom_call_target="tpu_custom_call" | custom-call | tf_op jit(solution)/shard_map/grid_blocks/pallas_call | solution.py:302
  29.6 1.4 %collective-permute-start.1 = (bf16[2,128,256]{2,1,0:T(8,128)(2,1)S(1)}, bf16[2,128,256]{2,1,0:T(8,128)(2,1)S(1)}, u32[]{:S(2)}, u32[]{:S(2)}) collective-permute-start(bf16[2,128,256]{2,1,0:T(8,128)(2,1)S(1)} %get-tuple-element.13), channel_id=1, source_target_pairs={{0,16},{2,18},{4,20},{6,22},{8,24},{10,26},{12,28},{14,30},{16,0},... | collective-permute-start | bytes 393224 | tf_op jit(solution)/shard_map/ppermute | solution.py:332
  31.0 17.1 %all-to-all-start.1 = ((bf16[392,2,128]{2,1,0:T(2,128)(2,1)}), bf16[392,2,128]{2,1,0:T(2,128)(2,1)S(1)}, u32[]{:S(2)}, u32[]{:S(2)}) async-start(bf16[392,2,128]{2,1,0:T(2,128)(2,1)} %get-tuple-element.11), calls=%async_computation.1 | async-start | bytes 401408 | tf_op jit(solution)/shard_map/all_to_all | solution.py:329
  48.1 0.0 collective-permute-done.1
  48.2 8.4 %all-gather = bf16[4,128,256]{2,1,0:T(8,128)(2,1)S(1)} all-gather(bf16[2,128,256]{2,1,0:T(8,128)(2,1)S(1)} %add_convert_fusion), channel_id=2, replica_groups=mesh['tile'=16,'freq'=2] {'freq'}, dimensions={0}, use_global_device_ids=true | all-gather | bytes 393216 | tf_op jit(solution)/shard_map/all_gather | solution.py:333
  56.5 0.0 all-to-all-done.1.returned_ref
  56.5 0.0 copy-start
  56.5 0.0 copy-start.1
  56.6 0.7 %copy-done = f32[2,2]{1,0:T(2,128)S(1)} copy-done((f32[2,2]{1,0:T(2,128)S(1)}, f32[2,2]{1,0:T(2,128)}, u32[]{:S(2)}) %copy-start) | copy-done | bytes 40
  57.2 0.0 copy-done.1
  57.2 1.5 %finish.1 = (f32[128,2,128]{2,1,0:T(2,128)}, f32[2,128,256]{2,1,0:T(8,128)}) custom-call(s32[1]{0:T(128)} %bitcast.plane_ref, f32[2,2]{1,0:T(2,128)S(1)} %copy-done, s32[128]{0:T(128)S(1)} %copy-done.1, bf16[392,2,128]{2,1,0:T(2,128)(2,1)S(1)} %all-to-all-done.1.returned_ref, bf16[2,2,128,256]{3,2,1,0:T(8,128)(2,1)S(1)} %bitcast.14), custom_call_target="tpu_custom_call" | custom-call | tf_op jit(solution)/shard_map/finish/pallas_call | solution.py:334
  (4 shorter events, 0.1 us)
Async XLA Ops:
  4.8 5.4 %copy-start.2 = (bf16[1,2,128,256]{3,2,1,0:T(8,128)(2,1)S(1)}, bf16[1,2,128,256]{3,2,1,0:T(8,128)(2,1)}, u32[]{:S(2)}) copy-start(bf16[1,2,128,256]{3,2,1,0:T(8,128)(2,1)} %param.13) | copy-start | bytes 393220
  4.8 20.0 %all-to-all-start = ((f32[392,4,128]{2,1,0:T(4,128)}), f32[392,4,128]{2,1,0:T(4,128)S(1)}, u32[]{:S(2)}, u32[]{:S(2)}) async-start(f32[392,4,128]{2,1,0:T(4,128)} %get-tuple-element.10), calls=%async_computation | async-start | bytes 1605632 | tf_op jit(solution)/shard_map/all_to_all | solution.py:291
  10.2 2.7 %copy-start.3 = (bf16[16,8,8]{0,2,1:T(8,128)(2,1)S(1)}, bf16[16,8,8]{0,2,1:T(8,128)(2,1)}, u32[]{:S(2)}) copy-start(bf16[16,8,8]{0,2,1:T(8,128)(2,1)} %param.14) | copy-start | bytes 6148
  10.2 12.5 %collective-permute-start = (bf16[2,128,256]{2,1,0:T(8,128)(2,1)S(1)}, bf16[2,128,256]{2,1,0:T(8,128)(2,1)S(1)}, u32[]{:S(2)}, u32[]{:S(2)}) collective-permute-start(bf16[2,128,256]{2,1,0:T(8,128)(2,1)S(1)} %bitcast.18), channel_id=1, source_target_pairs={{0,16},{2,18},{4,20},{6,22},{8,24},{10,26},{12,28},{14,30},{16,0},... | collective-permute-start | bytes 393224 | tf_op jit(solution)/shard_map/ppermute | solution.py:268
  29.6 18.5 %collective-permute-start.1 = (bf16[2,128,256]{2,1,0:T(8,128)(2,1)S(1)}, bf16[2,128,256]{2,1,0:T(8,128)(2,1)S(1)}, u32[]{:S(2)}, u32[]{:S(2)}) collective-permute-start(bf16[2,128,256]{2,1,0:T(8,128)(2,1)S(1)} %get-tuple-element.13), channel_id=1, source_target_pairs={{0,16},{2,18},{4,20},{6,22},{8,24},{10,26},{12,28},{14,30},{16,0},... | collective-permute-start | bytes 393224 | tf_op jit(solution)/shard_map/ppermute | solution.py:332
  31.0 25.6 %all-to-all-start.1 = ((bf16[392,2,128]{2,1,0:T(2,128)(2,1)}), bf16[392,2,128]{2,1,0:T(2,128)(2,1)S(1)}, u32[]{:S(2)}, u32[]{:S(2)}) async-start(bf16[392,2,128]{2,1,0:T(2,128)(2,1)} %get-tuple-element.11), calls=%async_computation.1 | async-start | bytes 401408 | tf_op jit(solution)/shard_map/all_to_all | solution.py:329
  56.5 0.7 %copy-start = (f32[2,2]{1,0:T(2,128)S(1)}, f32[2,2]{1,0:T(2,128)}, u32[]{:S(2)}) copy-start(f32[2,2]{1,0:T(2,128)} %coupling_ref.1) | copy-start | bytes 52
  56.5 0.7 %copy-start.1 = (s32[128]{0:T(128)S(1)}, s32[128]{0:T(128)}, u32[]{:S(2)}) copy-start(s32[128]{0:T(128)} %get-tuple-element.9.slot_ref) | copy-start | bytes 1540

commit v8 on v7

--- a/solution.py
+++ b/solution.py
@@ -5,7 +5,9 @@
 from jax.experimental.pallas import tpu as pltpu
 from jax.sharding import PartitionSpec as P
 
-UNROLL = 8
+UNROLL = 2
+CHUNKS = 8
+AHEAD = 2
 VMEM = pl.BlockSpec(memory_space=pltpu.VMEM)
 SMEM = pl.BlockSpec(memory_space=pltpu.SMEM)
 HBM = pl.BlockSpec(memory_space=pltpu.HBM)
@@ -130,7 +132,8 @@
 
 
 def grid_kernel(pairs, capacity, member_ref, got_ref, table_ref, model_ref, residual_ref, own_ref,
-                other_ref, turned_ref, grid_ref, row_a, row_b, partial_a, partial_b, weighted_a, weighted_b, code_ref, about_ref, list_ref, sem):
+                other_ref, turned_ref, grid_ref, code_ref, about_ref, list_ref, sem, *buffers):
+    row_refs, partial_refs, weighted_refs = buffers[:4], buffers[4:8], buffers[8:]
     tiles, side, wide = model_ref.shape
     groups = side // 16
     zero_row = table_ref.shape[0] - 8
@@ -171,9 +174,10 @@
 
         lax.fori_loop(0, pairs, enlist, start + spare)
         start = start + count + spare
-    for u in range(2 * UNROLL):
+    for u in range((CHUNKS + AHEAD) * UNROLL):
         list_ref[start + u] = (zero_row << PLANE_SHIFT) + capacity
     chunks = start >> UNROLL.bit_length() - 1
+    zero = jnp.zeros((16, 128), jnp.bfloat16)
 
     def read(which):
         entry = list_ref[which]
@@ -195,19 +199,24 @@
     def chunk_tile(turn):
         return (list_ref[turn * UNROLL] >> TILE_SHIFT) & 15
 
-    def front(turn, row_ref, partial_ref):
+    def front(turn, which):
+        row_ref, partial_ref = row_refs[which % len(row_refs)], partial_refs[which % len(partial_refs)]
         for u in range(UNROLL):
             _, _, parts = read(turn * UNROLL + u)
             taps, group = parts(2)
+            taps = taps.astype(jnp.bfloat16)
+            group = group.astype(jnp.float32).astype(jnp.bfloat16)
             for k in range(groups):
                 row_ref[16 * k : 16 * k + 16, 128 * u : 128 * u + 128] = jnp.where(
-                    group == k, taps, 0.0
-                ).astype(jnp.bfloat16)
+                    group == k, taps, zero
+                )
         partial_ref[...] = jnp.dot(
             turned_ref[chunk_tile(turn)], row_ref[...], preferred_element_type=jnp.float32
         )
 
-    def back(turn, row_ref, partial_ref, weighted_ref):
+    def back(turn, which):
+        row_ref, partial_ref = row_refs[which % len(row_refs)], partial_refs[which % len(partial_refs)]
+        weighted_ref = weighted_refs[which % len(weighted_refs)]
         for u in range(UNROLL):
             slot, data, parts = read(turn * UNROLL + u)
             columns = slice(128 * u, 128 * u + 128)
@@ -221,14 +230,15 @@
                 model = jnp.sum(picked * taps, axis=0, keepdims=True)
                 residual = data[part : part + 1] - model
                 residuals.append(residual)
-                samples.append(residual * taps)
+                samples.append((residual * taps).astype(jnp.bfloat16))
             residual_ref[slot] = jnp.concatenate(residuals, axis=0).astype(jnp.bfloat16)
+            group = group.astype(jnp.float32).astype(jnp.bfloat16)
             for part in range(2):
                 for k in range(groups):
                     low = part * side + 16 * k
                     weighted_ref[low : low + 16, columns] = jnp.where(
-                        group == k, samples[part], 0.0
-                    ).astype(jnp.bfloat16)
+                        group == k, samples[part], zero
+                    )
         grid_ref[chunk_tile(turn)] += lax.dot_general(
             row_ref[...],
             weighted_ref[...],
@@ -237,14 +247,14 @@
         )
 
     def step(turn, carry):
-        front(2 * turn + 1, row_b, partial_b)
-        back(2 * turn, row_a, partial_a, weighted_a)
-        front(2 * turn + 2, row_a, partial_a)
-        back(2 * turn + 1, row_b, partial_b, weighted_b)
+        for which in range(CHUNKS):
+            front(turn * CHUNKS + which + AHEAD, which + AHEAD)
+            back(turn * CHUNKS + which, which)
         return carry
 
-    front(0, row_a, partial_a)
-    lax.fori_loop(0, (chunks + 1) >> 1, step, 0)
+    for which in range(AHEAD):
+        front(which, which)
+    lax.fori_loop(0, scalar_div(chunks + CHUNKS - 1, CHUNKS), step, 0)
     half = tiles // 2
     member = member_ref[0]
     for t in range(half):
@@ -291,6 +301,7 @@
     got = lax.all_to_all(
         sent, "tile", split_axis=0, concat_axis=0, tiled=True, axis_index_groups=halves
     )
+    slot, got = lax.optimization_barrier((slot + lax.div(lax.axis_index("tile"), owners), got))
     model = jnp.where(
         member == 0,
         jnp.concatenate([model_own, model_other]),
@@ -311,16 +322,15 @@
         scratch_shapes=[
             pltpu.VMEM((2 * tiles_here, wide, side), jnp.bfloat16),
             pltpu.VMEM((2 * tiles_here, side, wide), jnp.float32),
-            pltpu.VMEM((side, UNROLL * rows), jnp.bfloat16),
-            pltpu.VMEM((side, UNROLL * rows), jnp.bfloat16),
-            pltpu.VMEM((wide, UNROLL * rows), jnp.float32),
-            pltpu.VMEM((wide, UNROLL * rows), jnp.float32),
-            pltpu.VMEM((wide, UNROLL * rows), jnp.bfloat16),
-            pltpu.VMEM((wide, UNROLL * rows), jnp.bfloat16),
             pltpu.VMEM((pairs, 2, rows), jnp.int32),
             pltpu.SMEM((pairs, 2, rows), jnp.int32),
-            pltpu.SMEM((slots + capacity + 2 * tiles_here * UNROLL + UNROLL,), jnp.int32),
+            pltpu.SMEM(
+                (slots + capacity + (2 * tiles_here + CHUNKS + AHEAD) * UNROLL,), jnp.int32
+            ),
             pltpu.SemaphoreType.DMA,
+            *[pltpu.VMEM((side, UNROLL * rows), jnp.bfloat16)] * 4,
+            *[pltpu.VMEM((wide, UNROLL * rows), jnp.float32)] * 4,
+            *[pltpu.VMEM((wide, UNROLL * rows), jnp.bfloat16)] * 2,
         ],
         compiler_params=PARAMS,
         name="grid_blocks",

time: 59.3 us -> 55 us (0.927)
  blocking collectives: 8.38 us -> 6.58 us
  waiting for transfers between devices: 11.9 us -> 10.5 us
  local copies, waits for them, and re-layouts: 0.75 us -> 2.14 us
  starting transfers between devices: 26.6 us -> 25.3 us
  Pallas kernels: 10.4 us -> 9.15 us
    all_gather x1, blocking collectives: 8.38 us -> 6.58 us  [body(): lax.all_gather(grid_sum.astype(jnp.bfloat16)[None], 'freq', axis=0, tiled...]
    unnamed x8, local copies, waits for them, and re-layouts: 0.69 us -> 2.08 us
    ppermute x1, waiting for transfers between devices: 9.81 us -> 8.42 us  [body(): model_other = lax.ppermute(model_own, 'tile', swap)]
    all_to_all x1, starting transfers between devices: 17.1 us -> 15.9 us  [body(): lax.all_to_all(residual, 'tile', split_axis=0, concat_axis=0, tiled=True,...]
    pallas_call x1, Pallas kernels: 4.74 us -> 3.47 us  [body(): pl.pallas_call(lambda *refs: grid_kernel(pairs, capacity, *refs), out_sha...]
where the time goes in v8:
time: 55 us; the launch traced here: 54.4 us
  starting transfers between devices  25.3 us (46%)
  waiting for transfers between devices  10.5 us (19%)
  Pallas kernels  9.15 us (17%)
  blocking collectives  6.58 us (12%)
  local copies, waits for them, and re-layouts  2.14 us (4%)
  between operations  0.69 us (1%)
    all_to_all x1, starting transfers between devices, body(): lax.all_to_all(residual, 'tile', split_axis=0, concat_axis=0, tiled=True,...  15.9 us
    ppermute x1, waiting for transfers between devices, body(): model_other = lax.ppermute(model_own, 'tile', swap)  8.42 us
    all_gather x1, blocking collectives, body(): lax.all_gather(grid_sum.astype(jnp.bfloat16)[None], 'freq', axis=0, tiled...  6.58 us
    all_to_all x1, starting transfers between devices, body(): lax.all_to_all(sent, 'tile', split_axis=0, concat_axis=0, tiled=True, axi...  5.4 us
    pallas_call x1, Pallas kernels, body(): pl.pallas_call(lambda *refs: pack_kernel(pairs, capacity, tiles_here, pla...  4.16 us
    pallas_call x1, Pallas kernels, body(): pl.pallas_call(lambda *refs: grid_kernel(pairs, capacity, *refs), out_sha...  3.47 us
    ppermute x1, starting transfers between devices, body(): model_other = lax.ppermute(model_own, 'tile', swap)  2.65 us
    unnamed x8, local copies, waits for them, and re-layouts  2.08 us
  transfers between devices with their start and end apart: 4, of which 2 were waited for; matrix products, arithmetic and copies ran while one was open for 0% of the time, Pallas kernels for 0%

profile of v8, /device:TPU:0, one launch (start us, length us, event | category | flops | bytes accessed | tf_op | source)
XLA Modules:
  0.0 54.4 jit_solution(4860066540245536942)
XLA Ops:
  0.6 4.2 %pack_blocks.1 = (f32[392,4,128]{2,1,0:T(4,128)}, s32[128]{0:T(128)}) custom-call(s32[128]{0:T(128)} %bitcast.20, s32[128]{0:T(128)} %bitcast.21, f32[128,2,128]{2,1,0:T(2,128)} %bitcast.15, s32[128,2,128]{2,1,0:T(2,128)} %bitcast.16, s32[128,2,128]{2,1,0:T(2,128)} %bitcast.17), custom_call_target="tpu_custom_call" | custom-call | tf_op jit(solution)/shard_map/pack_blocks/pallas_call | solution.py:279
  4.8 0.0 copy-start.1
  4.8 5.4 %all-to-all-start = ((f32[392,4,128]{2,1,0:T(4,128)}), f32[392,4,128]{2,1,0:T(4,128)S(1)}, u32[]{:S(2)}, u32[]{:S(2)}) async-start(f32[392,4,128]{2,1,0:T(4,128)} %get-tuple-element.12), calls=%async_computation | async-start | bytes 1605632 | tf_op jit(solution)/shard_map/all_to_all | solution.py:301
  10.2 0.0 copy-done.1
  10.2 2.7 %collective-permute-start = (bf16[2,128,256]{2,1,0:T(8,128)(2,1)S(1)}, bf16[2,128,256]{2,1,0:T(8,128)(2,1)S(1)}, u32[]{:S(2)}, u32[]{:S(2)}) collective-permute-start(bf16[2,128,256]{2,1,0:T(8,128)(2,1)S(1)} %bitcast.18), channel_id=1, source_target_pairs={{0,16},{2,18},{4,20},{6,22},{8,24},{10,26},{12,28},{14,30},{16,0},... | collective-permute-start | bytes 393224 | tf_op jit(solution)/shard_map/ppermute | solution.py:278
  12.9 0.0 copy-start.2
  12.9 0.7 %copy-done.2 = bf16[16,8,8]{0,2,1:T(8,128)(2,1)S(1)} copy-done((bf16[16,8,8]{0,2,1:T(8,128)(2,1)S(1)}, bf16[16,8,8]{0,2,1:T(8,128)(2,1)}, u32[]{:S(2)}) %copy-start.2) | copy-done | bytes 2072
  13.6 0.1 copy.13.refs_2_
  13.7 0.0 copy-start.3
  13.7 0.7 %copy-done.3 = s32[128]{0:T(128)S(1)} copy-done((s32[128]{0:T(128)S(1)}, s32[128]{0:T(128)}, u32[]{:S(2)}) %copy-start.3) | copy-done | bytes 536
  14.4 8.4 %collective-permute-done = bf16[2,128,256]{2,1,0:T(8,128)(2,1)S(1)} collective-permute-done((bf16[2,128,256]{2,1,0:T(8,128)(2,1)S(1)}, bf16[2,128,256]{2,1,0:T(8,128)(2,1)S(1)}, u32[]{:S(2)}, u32[]{:S(2)}) %collective-permute-start) | collective-permute-done | bytes 131104 | tf_op jit(solution)/shard_map/ppermute | solution.py:278
  22.8 2.0 %all-to-all-done.refs_1_ = f32[392,4,128]{2,1,0:T(4,128)S(1)} async-done(((f32[392,4,128]{2,1,0:T(4,128)}), f32[392,4,128]{2,1,0:T(4,128)S(1)}, u32[]{:S(2)}, u32[]{:S(2)}) %all-to-all-start) | async-done | bytes 802848 | tf_op jit(solution)/shard_map/all_to_all | solution.py:301
  24.8 3.5 %grid_blocks.1 = (bf16[392,2,128]{2,1,0:T(2,128)(2,1)}, f32[2,128,256]{2,1,0:T(8,128)S(1)}, bf16[2,128,256]{2,1,0:T(8,128)(2,1)S(1)}) custom-call(s32[1]{0:T(128)} %bitcast.6.refs_0_, f32[392,4,128]{2,1,0:T(4,128)S(1)} %all-to-all-done.refs_1_, f32[24,128]{1,0:T(8,128)S(1)} %copy.13.refs_2_, bf16[4,128,256]{2,1,0:T(8,128)(2,1)S(1)} %maximum_select_fusion.refs_3_), custom_call_target="tpu_custom_call" | custom-call | tf_op jit(solution)/shard_map/grid_blocks/pallas_call | solution.py:313
  28.3 1.4 %collective-permute-start.1 = (bf16[2,128,256]{2,1,0:T(8,128)(2,1)S(1)}, bf16[2,128,256]{2,1,0:T(8,128)(2,1)S(1)}, u32[]{:S(2)}, u32[]{:S(2)}) collective-permute-start(bf16[2,128,256]{2,1,0:T(8,128)(2,1)S(1)} %get-tuple-element.17), channel_id=1, source_target_pairs={{0,16},{2,18},{4,20},{6,22},{8,24},{10,26},{12,28},{14,30},{16,0},... | collective-permute-start | bytes 393224 | tf_op jit(solution)/shard_map/ppermute | solution.py:342
  29.7 15.9 %all-to-all-start.1 = ((bf16[392,2,128]{2,1,0:T(2,128)(2,1)}), bf16[392,2,128]{2,1,0:T(2,128)(2,1)S(1)}, u32[]{:S(2)}, u32[]{:S(2)}) async-start(bf16[392,2,128]{2,1,0:T(2,128)(2,1)} %get-tuple-element.15), calls=%async_computation.1 | async-start | bytes 401408 | tf_op jit(solution)/shard_map/all_to_all | solution.py:339
  45.6 0.0 collective-permute-done.1
  45.6 6.6 %all-gather = bf16[4,128,256]{2,1,0:T(8,128)(2,1)S(1)} all-gather(bf16[2,128,256]{2,1,0:T(8,128)(2,1)S(1)} %add_convert_fusion), channel_id=2, replica_groups=mesh['tile'=16,'freq'=2] {'freq'}, dimensions={0}, use_global_device_ids=true | all-gather | bytes 393216 | tf_op jit(solution)/shard_map/all_gather | solution.py:343
  52.2 0.0 all-to-all-done.1.returned_ref
  52.2 0.0 copy-start
  52.2 0.7 %copy-done = f32[2,2]{1,0:T(2,128)S(1)} copy-done((f32[2,2]{1,0:T(2,128)S(1)}, f32[2,2]{1,0:T(2,128)}, u32[]{:S(2)}) %copy-start) | copy-done | bytes 40
  52.9 1.5 %finish.1 = (f32[128,2,128]{2,1,0:T(2,128)}, f32[2,128,256]{2,1,0:T(8,128)}) custom-call(s32[1]{0:T(128)} %bitcast.plane_ref, f32[2,2]{1,0:T(2,128)S(1)} %copy-done, s32[128]{0:T(128)S(1)} %broadcast_add_fusion.slot_ref, bf16[392,2,128]{2,1,0:T(2,128)(2,1)S(1)} %all-to-all-done.1.returned_ref, bf16[2,2,128,256]{3,2,1,0:T(8,128)(2,1)S(1)} %bitcast.14), custom_call_target="tpu_custom_call" | custom-call | tf_op jit(solution)/shard_map/finish/pallas_call | solution.py:344
  (5 shorter events, 0.1 us)
Async XLA Ops:
  4.8 5.4 %copy-start.1 = (bf16[1,2,128,256]{3,2,1,0:T(8,128)(2,1)S(1)}, bf16[1,2,128,256]{3,2,1,0:T(8,128)(2,1)}, u32[]{:S(2)}) copy-start(bf16[1,2,128,256]{3,2,1,0:T(8,128)(2,1)} %param.13) | copy-start | bytes 393220
  4.8 20.0 %all-to-all-start = ((f32[392,4,128]{2,1,0:T(4,128)}), f32[392,4,128]{2,1,0:T(4,128)S(1)}, u32[]{:S(2)}, u32[]{:S(2)}) async-start(f32[392,4,128]{2,1,0:T(4,128)} %get-tuple-element.12), calls=%async_computation | async-start | bytes 1605632 | tf_op jit(solution)/shard_map/all_to_all | solution.py:301
  10.2 12.6 %collective-permute-start = (bf16[2,128,256]{2,1,0:T(8,128)(2,1)S(1)}, bf16[2,128,256]{2,1,0:T(8,128)(2,1)S(1)}, u32[]{:S(2)}, u32[]{:S(2)}) collective-permute-start(bf16[2,128,256]{2,1,0:T(8,128)(2,1)S(1)} %bitcast.18), channel_id=1, source_target_pairs={{0,16},{2,18},{4,20},{6,22},{8,24},{10,26},{12,28},{14,30},{16,0},... | collective-permute-start | bytes 393224 | tf_op jit(solution)/shard_map/ppermute | solution.py:278
  12.9 0.7 %copy-start.2 = (bf16[16,8,8]{0,2,1:T(8,128)(2,1)S(1)}, bf16[16,8,8]{0,2,1:T(8,128)(2,1)}, u32[]{:S(2)}) copy-start(bf16[16,8,8]{0,2,1:T(8,128)(2,1)} %param.14) | copy-start | bytes 6148
  13.7 0.7 %copy-start.3 = (s32[128]{0:T(128)S(1)}, s32[128]{0:T(128)}, u32[]{:S(2)}) copy-start(s32[128]{0:T(128)} %get-tuple-element.11) | copy-start | bytes 1540
  28.3 17.2 %collective-permute-start.1 = (bf16[2,128,256]{2,1,0:T(8,128)(2,1)S(1)}, bf16[2,128,256]{2,1,0:T(8,128)(2,1)S(1)}, u32[]{:S(2)}, u32[]{:S(2)}) collective-permute-start(bf16[2,128,256]{2,1,0:T(8,128)(2,1)S(1)} %get-tuple-element.17), channel_id=1, source_target_pairs={{0,16},{2,18},{4,20},{6,22},{8,24},{10,26},{12,28},{14,30},{16,0},... | collective-permute-start | bytes 393224 | tf_op jit(solution)/shard_map/ppermute | solution.py:342
  29.7 22.5 %all-to-all-start.1 = ((bf16[392,2,128]{2,1,0:T(2,128)(2,1)}), bf16[392,2,128]{2,1,0:T(2,128)(2,1)S(1)}, u32[]{:S(2)}, u32[]{:S(2)}) async-start(bf16[392,2,128]{2,1,0:T(2,128)(2,1)} %get-tuple-element.15), calls=%async_computation.1 | async-start | bytes 401408 | tf_op jit(solution)/shard_map/all_to_all | solution.py:339
  52.2 0.7 %copy-start = (f32[2,2]{1,0:T(2,128)S(1)}, f32[2,2]{1,0:T(2,128)}, u32[]{:S(2)}) copy-start(f32[2,2]{1,0:T(2,128)} %coupling_ref.1) | copy-start | bytes 52

commit v9 on v8

v9 whole, which is shorter than its diff:
```python
import jax
import jax.numpy as jnp
from jax import lax
from jax.experimental import pallas as pl
from jax.experimental.pallas import tpu as pltpu
from jax.sharding import PartitionSpec as P

UNROLL = 2
CHUNKS = 8
AHEAD = 2
VMEM = pl.BlockSpec(memory_space=pltpu.VMEM)
SMEM = pl.BlockSpec(memory_space=pltpu.SMEM)
HBM = pl.BlockSpec(memory_space=pltpu.HBM)
PARAMS = pltpu.CompilerParams(vmem_limit_bytes=32 * 1024 * 1024)
WHOLE_PARAMS = pltpu.CompilerParams(vmem_limit_bytes=62 * 1024 * 1024)
TILE_SHIFT = 12
PLANE_SHIFT = 16
SOURCE_SHIFT = 21


def scalar_div(value, count):
    shift = count.bit_length() - 1
    return value >> shift if count == 1 << shift else lax.div(value, count)


def pack_kernel(pairs, capacity, tiles_here, plane_hbm, tile_hbm, vis_hbm, cell_hbm, sub_hbm,
                first_hbm, last_hbm, slot_ref, plane_ref, tile_ref, vis_ref, cell_ref, sub_ref, sent_ref,
                about_ref, turned_ref, count_ref, load_sem, about_sem, sent_sem):
    blocks = tile_ref.shape[0]
    half = capacity // 2
    stride = 2 * half + 1
    loads = [
        pltpu.make_async_copy(source, target, load_sem.at[i])
        for i, (source, target) in enumerate(
            [
                (tile_hbm, tile_ref),
                (plane_hbm, plane_ref),
                (vis_hbm, vis_ref),
                (cell_hbm, cell_ref),
                (sub_hbm, sub_ref),
            ]
        )
    ]
    for copy in loads:
        copy.start()
    for d in range(pairs):
        for t in range(2 * tiles_here):
            count_ref[d * 2 * tiles_here + t] = 0
        for k in range(2 * half):
            about_ref[2 * d, 0, k] = 0.0
            about_ref[2 * d + 1, 0, k] = 0.0
    for copy in loads[:2]:
        copy.wait()

    def assign(b):
        tile = tile_ref[b]
        owner = scalar_div(tile, tiles_here)
        high = (owner >= pairs).astype(jnp.int32)
        pair = owner - high * pairs
        local = tile - (owner - high) * tiles_here
        key = pair * (2 * tiles_here) + local
        rank = count_ref[key]
        count_ref[key] = rank + 1
        place = jnp.where((local & 1) == 0, rank, capacity - 1 - rank)
        last = (place >= half).astype(jnp.int32)
        lane = place - last * half + (local >> 1) * half
        target = 2 * pair + last
        slot_ref[b] = target * stride + lane
        about_ref[target, 0, lane] = (plane_ref[b] << PLANE_SHIFT).astype(jnp.float32)

    def move(b):
        position = (cell_ref[b] * 8 + sub_ref[b]).astype(jnp.float32)
        sent_ref[slot_ref[b]] = jnp.concatenate([vis_ref[b], position], axis=0)

    def each(work):
        def step(turn, carry):
            for which in range(8):
                work(turn * 8 + which)
            return carry

        lax.fori_loop(0, blocks // 8, step, 0)

    each(assign)
    for d in range(pairs):
        for t in range(2 * tiles_here):
            count = count_ref[d * 2 * tiles_here + t]
            near, far = jnp.minimum(count, half), jnp.maximum(count - half, 0)
            about_ref[2 * d, 1, t] = (near if t % 2 == 0 else far).astype(jnp.float32)
            about_ref[2 * d + 1, 1, t] = (far if t % 2 == 0 else near).astype(jnp.float32)
    turn_about = pltpu.make_async_copy(about_ref, turned_ref, about_sem)
    turn_about.start()
    for copy in loads[2:]:
        copy.wait()
    each(move)
    turn_about.wait()
    part = lax.broadcasted_iota(jnp.int32, (4, 128), 0)
    lane = lax.broadcasted_iota(jnp.int32, (4, 128), 1)
    filled = ((part == 0) & (lane < 2 * half)) | ((part == 1) & (lane < 2 * tiles_here))
    for d in range(2 * pairs):
        sent_ref[d * stride + 2 * half] = jnp.where(filled, turned_ref[d], 0.0)
    stores = [
        pltpu.make_async_copy(
            sent_ref.at[pl.ds((2 * d + last) * stride, stride)],
            target.at[pl.ds(d * stride, stride)],
            sent_sem.at[2 * d + last],
        )
        for last, target in enumerate([first_hbm, last_hbm])
        for d in range(pairs)
    ]
    for copy in stores:
        copy.start()
    for copy in stores:
        copy.wait()


def finish_kernel(row_ref, slot_ref, returned_ref, grid_ref, residual_ref, coupled_ref):
    coupled_ref[...] = sum(
        row_ref[g] * grid_ref[g].astype(jnp.float32) for g in range(grid_ref.shape[0])
    )

    def step(turn, carry):
        for which in range(8):
            b = turn * 8 + which
            residual_ref[b] = returned_ref[slot_ref[b]].astype(jnp.float32)
        return carry

    lax.fori_loop(0, residual_ref.shape[0] // 8, step, 0)


def spread_parts(start, offset, table):
    sublane = lax.broadcasted_iota(jnp.int32, (8, 128), 0)
    taps, group = [], []
    for low in (0, 8):
        delta = sublane + low - start
        taps.append(
            jnp.take_along_axis(table, (delta & 15) + offset, axis=1, mode="promise_in_bounds")
        )
        group.append((15 - delta) >> 4)
    return jnp.concatenate(taps, axis=0), jnp.concatenate(group, axis=0)


def grid_kernel(pairs, half, first, *refs):
    if first:
        got_ref, table_ref, model_ref, residual_ref, turned_ref, grid_ref, *scratch = refs
    else:
        (member_ref, got_ref, table_ref, turned_ref, before_ref, earlier_ref, residual_ref, own_ref,
         other_ref, grid_ref, *scratch) = refs
    code_ref, about_ref, list_ref, sem, *buffers = scratch
    row_refs, partial_refs, weighted_refs = buffers[:4], buffers[4:8], buffers[8:]
    tiles, wide, side = turned_ref.shape
    groups = side // 16
    stride = 2 * half + 1
    zero_row = table_ref.shape[0] - 8
    lane = lax.broadcasted_iota(jnp.int32, (1, 128), 1)
    for s in range(pairs):
        about = got_ref[s * stride + 2 * half].astype(jnp.int32)
        code_ref[s, 0:1, :] = about[0:1] + (lane + (s * stride + (s << SOURCE_SHIFT)))
        code_ref[s, 1:2, :] = about[1:2]
    fill = pltpu.make_async_copy(code_ref, about_ref, sem)
    fill.start()
    if first:
        for t in range(tiles):
            turned_ref[t] = model_ref[t].T
        grid_ref[...] = jnp.zeros_like(grid_ref)
    else:
        grid_ref[...] = before_ref[...]
        for s in range(pairs):
            residual_ref[pl.ds(2 * s * stride, stride)] = earlier_ref[pl.ds(s * stride, stride)]
    fill.wait()

    start = jnp.int32(0)
    for t in range(tiles):
        count = jnp.int32(0)
        for s in range(pairs):
            count = count + about_ref[s, 1, t]
        spare = -count & (UNROLL - 1)
        for u in range(UNROLL):
            list_ref[start + u] = (zero_row << PLANE_SHIFT) + (t << TILE_SHIFT) + 2 * half

        def enlist(s, filled, t=t):
            base = t // 2 * half
            found = about_ref[s, 1, t]

            def some(turn, carry):
                for which in range(8):
                    k = turn * 8 + which
                    place = k if t % 2 == 0 else half - 1 - k
                    code = about_ref[s, 0, jnp.maximum(base + place, 0)]
                    list_ref[filled + k] = code + (t << TILE_SHIFT)
                return carry

            lax.fori_loop(0, (found + 7) >> 3, some, 0)
            return filled + found

        lax.fori_loop(0, pairs, enlist, start + spare)
        start = start + count + spare
    for u in range((CHUNKS + AHEAD) * UNROLL):
        list_ref[start + u] = (zero_row << PLANE_SHIFT) + 2 * half
    chunks = start >> UNROLL.bit_length() - 1
    zero = jnp.zeros((16, 128), jnp.bfloat16)

    def read(which):
        entry = list_ref[which]
        slot = entry & ((1 << TILE_SHIFT) - 1)
        data = got_ref[slot]
        position = data.astype(jnp.int32)
        start, offset = position >> 3, (position & 7) << 4
        plane = (entry >> PLANE_SHIFT) & ((1 << (SOURCE_SHIFT - PLANE_SHIFT)) - 1)
        table = jnp.broadcast_to(table_ref[pl.ds(plane, 1), :], (8, 128))

        def parts(row):
            return spread_parts(
                jnp.broadcast_to(start[row : row + 1], (8, 128)),
                jnp.broadcast_to(offset[row : row + 1], (8, 128)),
                table,
            )

        place = slot if first else slot + ((entry >> SOURCE_SHIFT) + 1) * stride
        return place, data, parts

    def chunk_tile(turn):
        return (list_ref[turn * UNROLL] >> TILE_SHIFT) & 15

    def front(turn, which):
        row_ref, partial_ref = row_refs[which % len(row_refs)], partial_refs[which % len(partial_refs)]
        for u in range(UNROLL):
            _, _, parts = read(turn * UNROLL + u)
            taps, group = parts(2)
            taps = taps.astype(jnp.bfloat16)
            group = group.astype(jnp.float32).astype(jnp.bfloat16)
            for k in range(groups):
                row_ref[16 * k : 16 * k + 16, 128 * u : 128 * u + 128] = jnp.where(
                    group == k, taps, zero
                )
        partial_ref[...] = jnp.dot(
            turned_ref[chunk_tile(turn)], row_ref[...], preferred_element_type=jnp.float32
        )

    def back(turn, which):
        row_ref, partial_ref = row_refs[which % len(row_refs)], partial_refs[which % len(partial_refs)]
        weighted_ref = weighted_refs[which % len(weighted_refs)]
        for u in range(UNROLL):
            place, data, parts = read(turn * UNROLL + u)
            columns = slice(128 * u, 128 * u + 128)
            taps, group = parts(3)
            residuals, samples = [], []
            for part in range(2):
                picked = jnp.zeros((16, 128), jnp.float32)
                for k in range(groups):
                    low = part * side + 16 * k
                    picked = jnp.where(group == k, partial_ref[low : low + 16, columns], picked)
                model = jnp.sum(picked * taps, axis=0, keepdims=True)
                residual = data[part : part + 1] - model
                residuals.append(residual)
                samples.append((residual * taps).astype(jnp.bfloat16))
            residual_ref[place] = jnp.concatenate(residuals, axis=0).astype(jnp.bfloat16)
            group = group.astype(jnp.float32).astype(jnp.bfloat16)
            for part in range(2):
                for k in range(groups):
                    low = part * side + 16 * k
                    weighted_ref[low : low + 16, columns] = jnp.where(
                        group == k, samples[part], zero
                    )
        grid_ref[chunk_tile(turn)] += lax.dot_general(
            row_ref[...],
            weighted_ref[...],
            (((1,), (1,)), ((), ())),
            preferred_element_type=jnp.float32,
        )

    def step(turn, carry):
        for which in range(CHUNKS):
            front(turn * CHUNKS + which + AHEAD, which + AHEAD)
            back(turn * CHUNKS + which, which)
        return carry

    for which in range(AHEAD):
        front(which, which)
    lax.fori_loop(0, scalar_div(chunks + CHUNKS - 1, CHUNKS), step, 0)
    if not first:
        here = tiles // 2
        member = member_ref[0]
        for t in range(here):
            own_ref[t] = grid_ref[member * here + t]
            other_ref[t] = grid_ref[(1 - member) * here + t].astype(jnp.bfloat16)


def body(visibilities, uv_cell, sub_pixel, w_plane, block_tile, model_grid, kernel_table, coupling):
    owners = lax.axis_size("tile")
    pairs = owners // 2
    _, blocks, _, rows = visibilities.shape
    capacity = 3 * blocks // owners
    half = capacity // 2
    _, tiles_here, side, wide = model_grid.shape
    planes, oversample, support = kernel_table.shape
    slots = pairs * (2 * half + 1)
    tiles = 2 * tiles_here
    member = lax.axis_index("tile") // pairs
    swap = [(t, (t + pairs) % owners) for t in range(owners)]
    halves = [list(range(pairs)), list(range(pairs, owners))]

    def exchange(values):
        return lax.all_to_all(
            values, "tile", split_axis=0, concat_axis=0, tiled=True, axis_index_groups=halves
        )

    model_own = model_grid[0]
    model_other = lax.ppermute(model_own, "tile", swap)
    sent_first, sent_last, slot = pl.pallas_call(
        lambda *refs: pack_kernel(pairs, capacity, tiles_here, *refs),
        out_shape=(
            jax.ShapeDtypeStruct((slots, 4, rows), jnp.float32),
            jax.ShapeDtypeStruct((slots, 4, rows), jnp.float32),
            jax.ShapeDtypeStruct((blocks,), jnp.int32),
        ),
        in_specs=[HBM] * 5,
        out_specs=(HBM, HBM, SMEM),
        scratch_shapes=[
            pltpu.SMEM((blocks,), jnp.int32),
            pltpu.SMEM((blocks,), jnp.int32),
            pltpu.VMEM((blocks, 2, rows), jnp.float32),
            pltpu.VMEM((blocks, 2, rows), jnp.int32),
            pltpu.VMEM((blocks, 2, rows), jnp.int32),
            pltpu.VMEM((2 * slots, 4, rows), jnp.float32),
            pltpu.SMEM((2 * pairs, 4, rows), jnp.float32),
            pltpu.VMEM((2 * pairs, 4, rows), jnp.float32),
            pltpu.SMEM((pairs * tiles,), jnp.int32),
            pltpu.SemaphoreType.DMA((5,)),
            pltpu.SemaphoreType.DMA,
            pltpu.SemaphoreType.DMA((2 * pairs,)),
        ],
        compiler_params=WHOLE_PARAMS,
        name="pack_blocks",
    )(w_plane[0], block_tile[0], visibilities[0], uv_cell[0], sub_pixel[0])
    got_first = exchange(sent_first)
    got_last = exchange(sent_last)
    own_row = lax.dynamic_index_in_dim(coupling, lax.axis_index("freq"), 0, keepdims=False)
    slot, own_row, got_first = lax.optimization_barrier(
        (slot + lax.div(lax.axis_index("tile"), owners), own_row, got_first)
    )
    model = jnp.where(
        member == 0,
        jnp.concatenate([model_own, model_other]),
        jnp.concatenate([model_other, model_own]),
    )
    table = jnp.pad(
        kernel_table.astype(jnp.float32), ((0, 8), (0, 0), (0, 16 - support))
    ).reshape(planes + 8, 16 * oversample)

    def grid_blocks(first, out_shape, *operands):
        return pl.pallas_call(
            lambda *refs: grid_kernel(pairs, half, first, *refs),
            out_shape=out_shape,
            in_specs=[VMEM] * len(operands) if first else [SMEM] + [VMEM] * (len(operands) - 1),
            out_specs=tuple([VMEM] * len(out_shape)),
            scratch_shapes=([] if first else [pltpu.VMEM((tiles, side, wide), jnp.float32)])
            + [
                pltpu.VMEM((pairs, 2, rows), jnp.int32),
                pltpu.SMEM((pairs, 2, rows), jnp.int32),
                pltpu.SMEM((slots + capacity + (tiles + CHUNKS + AHEAD) * UNROLL,), jnp.int32),
                pltpu.SemaphoreType.DMA,
                *[pltpu.VMEM((side, UNROLL * rows), jnp.bfloat16)] * 4,
                *[pltpu.VMEM((wide, UNROLL * rows), jnp.float32)] * 4,
                *[pltpu.VMEM((wide, UNROLL * rows), jnp.bfloat16)] * 2,
            ],
            compiler_params=PARAMS,
            cost_estimate=pl.CostEstimate(
                flops=10**10, bytes_accessed=4 * 10**6, transcendentals=0
            ),
            name="grid_first" if first else "grid_last",
        )(*operands)

    residual, turned, grid = grid_blocks(
        True,
        (
            jax.ShapeDtypeStruct((slots, 2, rows), jnp.bfloat16),
            jax.ShapeDtypeStruct((tiles, wide, side), jnp.bfloat16),
            jax.ShapeDtypeStruct((tiles, side, wide), jnp.float32),
        ),
        got_first,
        table,
        model,
    )
    residual, own, other = grid_blocks(
        False,
        (
            jax.ShapeDtypeStruct((2 * slots, 2, rows), jnp.bfloat16),
            jax.ShapeDtypeStruct((tiles_here, side, wide), jnp.float32),
            jax.ShapeDtypeStruct((tiles_here, side, wide), jnp.bfloat16),
        ),
        member[None],
        got_last,
        table,
        turned,
        grid,
        residual,
    )

    returned = exchange(residual)
    grid_sum = own + lax.ppermute(other, "tile", swap).astype(jnp.float32)
    grids = lax.all_gather(grid_sum.astype(jnp.bfloat16)[None], "freq", axis=0, tiled=True)
    residuals, coupled_grid = pl.pallas_call(
        finish_kernel,
        out_shape=(
            jax.ShapeDtypeStruct((blocks, 2, rows), jnp.float32),
            jax.ShapeDtypeStruct((tiles_here, side, wide), jnp.float32),
        ),
        in_specs=[SMEM, SMEM, VMEM, VMEM],
        out_specs=(VMEM, VMEM),
        compiler_params=PARAMS,
        name="finish",
    )(own_row, slot, returned, grids)
    return (residuals[None], coupled_grid[None])


def solution(mesh):
    return jax.shard_map(
        body,
        mesh=mesh,
        in_specs=(
            P("freq", "tile", None, None),
            P("freq", "tile", None, None),
            P("freq", "tile", None, None),
            P("freq", "tile"),
            P("freq", "tile"),
            P("freq", "tile", None, None),
            P(),
            P(),
        ),
        out_specs=(P("freq", "tile", None, None), P("freq", "tile", None, None)),
        check_vma=False,
    )
```

time: 55 us -> 61.1 us (1.11)
  Pallas kernels: 9.15 us -> 13 us
  blocking collectives: 6.58 us -> 8.85 us
  local copies, waits for them, and re-layouts: 2.14 us -> 0.75 us
  waiting for transfers between devices: 10.5 us -> 11.8 us
    all_to_all x2 -> x3, waiting for transfers between devices: 2.05 us -> 6.82 us  [exchange(): lax.all_to_all(values, 'tile', split_axis=0, concat_axis=0, tiled=True, a...]
    pallas_call x2 -> x3, Pallas kernels: 7.63 us -> 11.5 us  [the longest x2 6.19 us: grid_blocks(): pl.pallas_call(lambda *refs: grid_kernel(pairs, half, first, *refs), out_...]
    ppermute x1, waiting for transfers between devices: 8.42 us -> 4.94 us  [body(): model_other = lax.ppermute(model_own, 'tile', swap)]
    all_gather x1, blocking collectives: 6.58 us -> 8.85 us  [body(): lax.all_gather(grid_sum.astype(jnp.bfloat16)[None], 'freq', axis=0, tiled...]
    unnamed x8, local copies, waits for them, and re-layouts: 2.08 us -> 0.67 us
    all_to_all x2 -> x3, starting transfers between devices: 21.3 us -> 21.8 us  [exchange(): lax.all_to_all(values, 'tile', split_axis=0, concat_axis=0, tiled=True, a...]
  transfers between devices with their start and end apart: 4 -> 5, of which waited for: 2 -> 3; matrix products, arithmetic and copies ran while one was open for 0% -> 0% of each run, Pallas kernels for 0% -> 5%
where the time goes in v9:
time: 61.1 us; the launch traced here: 60.6 us
  starting transfers between devices  25.5 us (42%)
  Pallas kernels  13 us (21%)
  waiting for transfers between devices  11.8 us (19%)
  blocking collectives  8.85 us (14%)
  local copies, waits for them, and re-layouts  0.75 us (1%)
  between operations  0.72 us (1%)
    all_to_all x3, starting transfers between devices, exchange(): lax.all_to_all(values, 'tile', split_axis=0, concat_axis=0, tiled=True, a...  21.8 us
    all_gather x1, blocking collectives, body(): lax.all_gather(grid_sum.astype(jnp.bfloat16)[None], 'freq', axis=0, tiled...  8.85 us
    all_to_all x3, waiting for transfers between devices, exchange(): lax.all_to_all(values, 'tile', split_axis=0, concat_axis=0, tiled=True, a...  6.82 us
    pallas_call x2, Pallas kernels, grid_blocks(): pl.pallas_call(lambda *refs: grid_kernel(pairs, half, first, *refs), out_...  6.19 us
    pallas_call x1, Pallas kernels, body(): pl.pallas_call(lambda *refs: pack_kernel(pairs, capacity, tiles_here, *re...  5.3 us
    ppermute x1, waiting for transfers between devices, body(): model_other = lax.ppermute(model_own, 'tile', swap)  4.94 us
    ppermute x1, starting transfers between devices, body(): model_other = lax.ppermute(model_own, 'tile', swap)  2.65 us
    pallas_call x1, Pallas kernels, body(): pl.pallas_call(finish_kernel, out_shape=(jax.ShapeDtypeStruct((blocks, 2,...  1.52 us
  transfers between devices with their start and end apart: 5, of which 3 were waited for; matrix products, arithmetic and copies ran while one was open for 0% of the time, Pallas kernels for 5%

profile of v9, /device:TPU:0, one launch (start us, length us, event | category | flops | bytes accessed | tf_op | source)
XLA Modules:
  0.0 60.6 jit_solution(1105498281891158839)
XLA Ops:
  0.6 0.0 copy-start
  0.6 5.3 %pack_blocks.1 = (f32[200,4,128]{2,1,0:T(4,128)}, f32[200,4,128]{2,1,0:T(4,128)}, s32[128]{0:T(128)}) custom-call(s32[128]{0:T(128)} %bitcast.21, s32[128]{0:T(128)} %bitcast.22, f32[128,2,128]{2,1,0:T(2,128)} %bitcast.16, s32[128,2,128]{2,1,0:T(2,128)} %bitcast.17, s32[128,2,128]{2,1,0:T(2,128)} %bitcast.18), custom_call_target="tpu_custom_call" | custom-call | tf_op jit(solution)/shard_map/pack_blocks/pallas_call | solution.py:309
  6.0 0.0 copy-start.1
  6.0 5.4 %all-to-all-start = ((f32[200,4,128]{2,1,0:T(4,128)}), f32[200,4,128]{2,1,0:T(4,128)S(1)}, u32[]{:S(2)}, u32[]{:S(2)}) async-start(f32[200,4,128]{2,1,0:T(4,128)} %get-tuple-element.17), calls=%async_computation | async-start | bytes 819200 | tf_op jit(solution)/shard_map/all_to_all | solution.py:303
  11.4 0.0 copy-start.2
  11.4 0.0 copy-done.1
  11.4 2.7 %collective-permute-start = (bf16[2,128,256]{2,1,0:T(8,128)(2,1)S(1)}, bf16[2,128,256]{2,1,0:T(8,128)(2,1)S(1)}, u32[]{:S(2)}, u32[]{:S(2)}) collective-permute-start(bf16[2,128,256]{2,1,0:T(8,128)(2,1)S(1)} %bitcast.19), channel_id=1, source_target_pairs={{0,16},{2,18},{4,20},{6,22},{8,24},{10,26},{12,28},{14,30},{16,0},... | collective-permute-start | bytes 393224 | tf_op jit(solution)/shard_map/ppermute | solution.py:308
  14.0 0.0 copy-done.2
  14.1 0.0 copy-start.3
  14.1 0.6 %copy-done.3 = s32[128]{0:T(128)S(1)} copy-done((s32[128]{0:T(128)S(1)}, s32[128]{0:T(128)}, u32[]{:S(2)}) %copy-start.3) | copy-done | bytes 536
  14.7 0.1 copy.13.refs_1_.refs_2_
  14.8 0.0 copy-done
  14.8 4.9 %collective-permute-done = bf16[2,128,256]{2,1,0:T(8,128)(2,1)S(1)} collective-permute-done((bf16[2,128,256]{2,1,0:T(8,128)(2,1)S(1)}, bf16[2,128,256]{2,1,0:T(8,128)(2,1)S(1)}, u32[]{:S(2)}, u32[]{:S(2)}) %collective-permute-start) | collective-permute-done | bytes 131104 | tf_op jit(solution)/shard_map/ppermute | solution.py:308
  19.8 2.0 %all-to-all-done.refs_0_ = f32[200,4,128]{2,1,0:T(4,128)S(1)} async-done(((f32[200,4,128]{2,1,0:T(4,128)}), f32[200,4,128]{2,1,0:T(4,128)S(1)}, u32[]{:S(2)}, u32[]{:S(2)}) %all-to-all-start) | async-done | bytes 409632 | tf_op jit(solution)/shard_map/all_to_all | solution.py:303
  21.8 4.9 %all-to-all-start.1 = ((f32[200,4,128]{2,1,0:T(4,128)}), f32[200,4,128]{2,1,0:T(4,128)S(1)}, u32[]{:S(2)}, u32[]{:S(2)}) async-start(f32[200,4,128]{2,1,0:T(4,128)} %get-tuple-element.20), calls=%async_computation.1 | async-start | bytes 819200 | tf_op jit(solution)/shard_map/all_to_all | solution.py:303
  26.7 2.8 %grid_first.1 = (bf16[200,2,128]{2,1,0:T(2,128)(2,1)S(1)}, bf16[4,256,128]{2,1,0:T(8,128)(2,1)S(1)}, f32[4,128,256]{2,1,0:T(8,128)S(1)}) custom-call(f32[200,4,128]{2,1,0:T(4,128)S(1)} %all-to-all-done.refs_0_, f32[24,128]{1,0:T(8,128)S(1)} %copy.13.refs_1_.refs_2_, bf16[4,128,256]{2,1,0:T(8,128)(2,1)S(1)} %maximum_select_fusion.refs_2_), custom_call_target="tpu_custom_call" | custom-call | flops 10000000000 | bytes 4000000 | tf_op jit(solution)/shard_map/grid_first/pallas_call | solution.py:351
  29.5 4.8 %all-to-all-done.1.refs_1_ = f32[200,4,128]{2,1,0:T(4,128)S(1)} async-done(((f32[200,4,128]{2,1,0:T(4,128)}), f32[200,4,128]{2,1,0:T(4,128)S(1)}, u32[]{:S(2)}, u32[]{:S(2)}) %all-to-all-start.1) | async-done | bytes 409632 | tf_op jit(solution)/shard_map/all_to_all | solution.py:303
  34.3 3.4 %grid_last.1 = (bf16[400,2,128]{2,1,0:T(2,128)(2,1)}, f32[2,128,256]{2,1,0:T(8,128)S(1)}, bf16[2,128,256]{2,1,0:T(8,128)(2,1)S(1)}) custom-call(s32[1]{0:T(128)} %bitcast.6.refs_0_, f32[200,4,128]{2,1,0:T(4,128)S(1)} %all-to-all-done.1.refs_1_, f32[24,128]{1,0:T(8,128)S(1)} %copy.13.refs_1_.refs_2_, bf16[4,256,128]{2,1,0:T(8,128)(2,1)S(1)} %get-tuple-element.22.refs_3_, ...), custom_call_target="tpu_custom_call" | custom-call | flops 10000000000 | bytes 4000000 | tf_op jit(solution)/shard_map/grid_last/pallas_call | solution.py:351
  37.7 1.0 %collective-permute-start.1 = (bf16[2,128,256]{2,1,0:T(8,128)(2,1)S(1)}, bf16[2,128,256]{2,1,0:T(8,128)(2,1)S(1)}, u32[]{:S(2)}, u32[]{:S(2)}) collective-permute-start(bf16[2,128,256]{2,1,0:T(8,128)(2,1)S(1)} %get-tuple-element.27), channel_id=1, source_target_pairs={{0,16},{2,18},{4,20},{6,22},{8,24},{10,26},{12,28},{14,30},{16,0},... | collective-permute-start | bytes 393224 | tf_op jit(solution)/shard_map/ppermute | solution.py:400
  38.7 11.6 %all-to-all-start.2 = ((bf16[400,2,128]{2,1,0:T(2,128)(2,1)}), bf16[400,2,128]{2,1,0:T(2,128)(2,1)S(1)}, u32[]{:S(2)}, u32[]{:S(2)}) async-start(bf16[400,2,128]{2,1,0:T(2,128)(2,1)} %get-tuple-element.25), calls=%async_computation.2 | async-start | bytes 409600 | tf_op jit(solution)/shard_map/all_to_all | solution.py:303
  50.2 0.0 collective-permute-done.1
  50.3 8.9 %all-gather = bf16[4,128,256]{2,1,0:T(8,128)(2,1)S(1)} all-gather(bf16[2,128,256]{2,1,0:T(8,128)(2,1)S(1)} %add_convert_fusion), channel_id=2, replica_groups=mesh['tile'=16,'freq'=2] {'freq'}, dimensions={0}, use_global_device_ids=true | all-gather | bytes 393216 | tf_op jit(solution)/shard_map/all_gather | solution.py:401
  59.1 0.0 all-to-all-done.2.returned_ref
  59.1 1.5 %finish.1 = (f32[128,2,128]{2,1,0:T(2,128)}, f32[2,128,256]{2,1,0:T(8,128)}) custom-call(f32[2]{0:T(128)S(1)} %dynamic-slice_bitcast_fusion.row_ref, s32[128]{0:T(128)S(1)} %broadcast_add_fusion.slot_ref, bf16[400,2,128]{2,1,0:T(2,128)(2,1)S(1)} %all-to-all-done.2.returned_ref, bf16[2,2,128,256]{3,2,1,0:T(8,128)(2,1)S(1)} %bitcast.15), custom_call_target="tpu_custom_call" | custom-call | tf_op jit(solution)/shard_map/finish/pallas_call | solution.py:402
  (6 shorter events, 0.1 us)
Async XLA Ops:
  0.6 14.2 %copy-start = (f32[2,2]{1,0:T(2,128)S(1)}, f32[2,2]{1,0:T(2,128)}, u32[]{:S(2)}) copy-start(f32[2,2]{1,0:T(2,128)} %param.15) | copy-start | bytes 52
  6.0 5.4 %copy-start.1 = (bf16[1,2,128,256]{3,2,1,0:T(8,128)(2,1)S(1)}, bf16[1,2,128,256]{3,2,1,0:T(8,128)(2,1)}, u32[]{:S(2)}) copy-start(bf16[1,2,128,256]{3,2,1,0:T(8,128)(2,1)} %param.13) | copy-start | bytes 393220
  6.0 15.8 %all-to-all-start = ((f32[200,4,128]{2,1,0:T(4,128)}), f32[200,4,128]{2,1,0:T(4,128)S(1)}, u32[]{:S(2)}, u32[]{:S(2)}) async-start(f32[200,4,128]{2,1,0:T(4,128)} %get-tuple-element.17), calls=%async_computation | async-start | bytes 819200 | tf_op jit(solution)/shard_map/all_to_all | solution.py:303
  11.4 2.7 %copy-start.2 = (bf16[16,8,8]{0,2,1:T(8,128)(2,1)S(1)}, bf16[16,8,8]{0,2,1:T(8,128)(2,1)}, u32[]{:S(2)}) copy-start(bf16[16,8,8]{0,2,1:T(8,128)(2,1)} %param.14) | copy-start | bytes 6148
  11.4 8.4 %collective-permute-start = (bf16[2,128,256]{2,1,0:T(8,128)(2,1)S(1)}, bf16[2,128,256]{2,1,0:T(8,128)(2,1)S(1)}, u32[]{:S(2)}, u32[]{:S(2)}) collective-permute-start(bf16[2,128,256]{2,1,0:T(8,128)(2,1)S(1)} %bitcast.19), channel_id=1, source_target_pairs={{0,16},{2,18},{4,20},{6,22},{8,24},{10,26},{12,28},{14,30},{16,0},... | collective-permute-start | bytes 393224 | tf_op jit(solution)/shard_map/ppermute | solution.py:308
  14.1 0.7 %copy-start.3 = (s32[128]{0:T(128)S(1)}, s32[128]{0:T(128)}, u32[]{:S(2)}) copy-start(s32[128]{0:T(128)} %get-tuple-element.16) | copy-start | bytes 1540
  21.8 12.5 %all-to-all-start.1 = ((f32[200,4,128]{2,1,0:T(4,128)}), f32[200,4,128]{2,1,0:T(4,128)S(1)}, u32[]{:S(2)}, u32[]{:S(2)}) async-start(f32[200,4,128]{2,1,0:T(4,128)} %get-tuple-element.20), calls=%async_computation.1 | async-start | bytes 819200 | tf_op jit(solution)/shard_map/all_to_all | solution.py:303
  37.7 12.6 %collective-permute-start.1 = (bf16[2,128,256]{2,1,0:T(8,128)(2,1)S(1)}, bf16[2,128,256]{2,1,0:T(8,128)(2,1)S(1)}, u32[]{:S(2)}, u32[]{:S(2)}) collective-permute-start(bf16[2,128,256]{2,1,0:T(8,128)(2,1)S(1)} %get-tuple-element.27), channel_id=1, source_target_pairs={{0,16},{2,18},{4,20},{6,22},{8,24},{10,26},{12,28},{14,30},{16,0},... | collective-permute-start | bytes 393224 | tf_op jit(solution)/shard_map/ppermute | solution.py:400
  38.7 20.5 %all-to-all-start.2 = ((bf16[400,2,128]{2,1,0:T(2,128)(2,1)}), bf16[400,2,128]{2,1,0:T(2,128)(2,1)S(1)}, u32[]{:S(2)}, u32[]{:S(2)}) async-start(bf16[400,2,128]{2,1,0:T(2,128)(2,1)} %get-tuple-element.25), calls=%async_computation.2 | async-start | bytes 409600 | tf_op jit(solution)/shard_map/all_to_all | solution.py:303

commit v10 on v8

--- a/solution.py
+++ b/solution.py
@@ -104,10 +104,9 @@
         copy.wait()
 
 
-def finish_kernel(plane_ref, coupling_ref, slot_ref, returned_ref, grid_ref, residual_ref, coupled_ref):
+def finish_kernel(row_ref, slot_ref, returned_ref, grid_ref, residual_ref, coupled_ref):
     coupled_ref[...] = sum(
-        coupling_ref[plane_ref[0], g] * grid_ref[g].astype(jnp.float32)
-        for g in range(grid_ref.shape[0])
+        row_ref[g] * grid_ref[g].astype(jnp.float32) for g in range(grid_ref.shape[0])
     )
 
     def step(turn, carry):
@@ -274,8 +273,13 @@
     swap = [(t, (t + pairs) % owners) for t in range(owners)]
     halves = [list(range(pairs)), list(range(pairs, owners))]
 
-    model_own = model_grid[0]
-    model_other = lax.ppermute(model_own, "tile", swap)
+    model = lax.all_gather(
+        model_grid[0],
+        "tile",
+        axis=0,
+        tiled=True,
+        axis_index_groups=[[t, t + pairs] for t in range(pairs)],
+    )
     sent, slot = pl.pallas_call(
         lambda *refs: pack_kernel(pairs, capacity, tiles_here, planes, *refs),
         out_shape=(
@@ -301,11 +305,9 @@
     got = lax.all_to_all(
         sent, "tile", split_axis=0, concat_axis=0, tiled=True, axis_index_groups=halves
     )
-    slot, got = lax.optimization_barrier((slot + lax.div(lax.axis_index("tile"), owners), got))
-    model = jnp.where(
-        member == 0,
-        jnp.concatenate([model_own, model_other]),
-        jnp.concatenate([model_other, model_own]),
+    own_row = lax.dynamic_index_in_dim(coupling, lax.axis_index("freq"), 0, keepdims=False)
+    slot, own_row, got = lax.optimization_barrier(
+        (slot + lax.div(lax.axis_index("tile"), owners), own_row, got)
     )
     table = jnp.pad(
         kernel_table.astype(jnp.float32), ((0, 8), (0, 0), (0, 16 - support))
@@ -347,11 +349,11 @@
             jax.ShapeDtypeStruct((blocks, 2, rows), jnp.float32),
             jax.ShapeDtypeStruct((tiles_here, side, wide), jnp.float32),
         ),
-        in_specs=[SMEM, SMEM, SMEM, VMEM, VMEM],
+        in_specs=[SMEM, SMEM, VMEM, VMEM],
         out_specs=(VMEM, VMEM),
         compiler_params=PARAMS,
         name="finish",
-    )(lax.axis_index("freq")[None], coupling, slot, returned, grids)
+    )(own_row, slot, returned, grids)
     return (residuals[None], coupled_grid[None])
 
 

time: 55 us -> 54.4 us (0.989)
  blocking collectives: 6.58 us -> 18.7 us
  waiting for transfers between devices: 10.5 us -> 1.41 us
  starting transfers between devices: 25.3 us -> 21.7 us
  Pallas kernels: 9.15 us -> 10.2 us
  local copies, waits for them, and re-layouts: 2.14 us -> 1.55 us
    all_gather x0 -> x1, blocking collectives: none -> 11.6 us  [body(): lax.all_gather(model_grid[0], 'tile', axis=0, tiled=True, axis_index_grou...]
    ppermute x1 -> x0, waiting for transfers between devices: 8.42 us -> none  [body(): model_other = lax.ppermute(model_own, 'tile', swap)]
    ppermute x1 -> x0, starting transfers between devices: 2.65 us -> none  [body(): model_other = lax.ppermute(model_own, 'tile', swap)]
    pallas_call x1, Pallas kernels: 3.47 us -> 4.55 us  [body(): pl.pallas_call(lambda *refs: grid_kernel(pairs, capacity, *refs), out_sha...]
    all_to_all x1, waiting for transfers between devices: 2.05 us -> 1.41 us  [body(): lax.all_to_all(sent, 'tile', split_axis=0, concat_axis=0, tiled=True, axi...]
    unnamed x8, local copies, waits for them, and re-layouts: 2.08 us -> 1.48 us
  transfers between devices with their start and end apart: 4 -> 3, of which waited for: 2 -> 1; matrix products, arithmetic and copies ran while one was open for 0% -> 0% of each run, Pallas kernels for 0% -> 0%
where the time goes in v10:
time: 54.4 us; the launch traced here: 54.3 us
  starting transfers between devices  21.7 us (40%)
  blocking collectives  18.7 us (34%)
  Pallas kernels  10.2 us (19%)
  local copies, waits for them, and re-layouts  1.55 us (3%)
  waiting for transfers between devices  1.41 us (3%)
  between operations  0.7 us (1%)
    all_to_all x1, starting transfers between devices, body(): lax.all_to_all(residual, 'tile', split_axis=0, concat_axis=0, tiled=True,...  15.5 us
    all_gather x1, blocking collectives, body(): lax.all_gather(model_grid[0], 'tile', axis=0, tiled=True, axis_index_grou...  11.6 us
    all_gather x1, blocking collectives, body(): lax.all_gather(grid_sum.astype(jnp.bfloat16)[None], 'freq', axis=0, tiled...  7.01 us
    all_to_all x1, starting transfers between devices, body(): lax.all_to_all(sent, 'tile', split_axis=0, concat_axis=0, tiled=True, axi...  5.27 us
    pallas_call x1, Pallas kernels, body(): pl.pallas_call(lambda *refs: grid_kernel(pairs, capacity, *refs), out_sha...  4.55 us
    pallas_call x1, Pallas kernels, body(): pl.pallas_call(lambda *refs: pack_kernel(pairs, capacity, tiles_here, pla...  4.15 us
    pallas_call x1, Pallas kernels, body(): pl.pallas_call(finish_kernel, out_shape=(jax.ShapeDtypeStruct((blocks, 2,...  1.52 us
    unnamed x8, local copies, waits for them, and re-layouts  1.48 us
  transfers between devices with their start and end apart: 3, of which 1 were waited for; matrix products, arithmetic and copies ran while one was open for 0% of the time, Pallas kernels for 0%

profile of v10, /device:TPU:0, one launch (start us, length us, event | category | flops | bytes accessed | tf_op | source)
XLA Modules:
  0.0 54.3 jit_solution(16712949728660040237)
XLA Ops:
  0.6 0.0 copy-start
  0.6 4.1 %pack_blocks.1 = (f32[392,4,128]{2,1,0:T(4,128)}, s32[128]{0:T(128)}) custom-call(s32[128]{0:T(128)} %bitcast.22, s32[128]{0:T(128)} %bitcast.23, f32[128,2,128]{2,1,0:T(2,128)} %bitcast.18, s32[128,2,128]{2,1,0:T(2,128)} %bitcast.19, s32[128,2,128]{2,1,0:T(2,128)} %bitcast.20), custom_call_target="tpu_custom_call" | custom-call | tf_op jit(solution)/shard_map/pack_blocks/pallas_call | solution.py:283
  4.8 5.3 %all-to-all-start = ((f32[392,4,128]{2,1,0:T(4,128)}), f32[392,4,128]{2,1,0:T(4,128)S(1)}, u32[]{:S(2)}, u32[]{:S(2)}) async-start(f32[392,4,128]{2,1,0:T(4,128)} %get-tuple-element.13), calls=%async_computation | async-start | bytes 1605632 | tf_op jit(solution)/shard_map/all_to_all | solution.py:305
  10.1 0.0 copy-start.2
  10.1 0.0 copy-start.1
  10.1 0.7 %copy-done.2 = bf16[16,8,8]{0,2,1:T(8,128)(2,1)S(1)} copy-done((bf16[16,8,8]{0,2,1:T(8,128)(2,1)S(1)}, bf16[16,8,8]{0,2,1:T(8,128)(2,1)}, u32[]{:S(2)}) %copy-start.2) | copy-done | bytes 2072
  10.8 0.1 copy.14.refs_2_
  10.9 0.1 copy-done.1
  11.0 11.6 %all-gather = bf16[1,4,128,256]{3,2,0,1:T(8,128)(2,1)S(1)} all-gather(bf16[1,2,128,256]{3,2,0,1:T(8,128)(2,1)S(1)} %bitcast.21), channel_id=2, replica_groups={{0,16},{2,18},{4,20},{6,22},{8,24},{10,26},{12,28},{14,30},{1,17},{3,19..., dimensions={1}, use_global_device_ids=true | all-gather | bytes 393216 | tf_op jit(solution)/shard_map/all_gather | solution.py:276
  22.6 0.0 copy-done
  22.6 0.0 copy-start.3
  22.6 0.6 %copy-done.3 = s32[128]{0:T(128)S(1)} copy-done((s32[128]{0:T(128)S(1)}, s32[128]{0:T(128)}, u32[]{:S(2)}) %copy-start.3) | copy-done | bytes 536
  23.3 1.4 %all-to-all-done.refs_1_ = f32[392,4,128]{2,1,0:T(4,128)S(1)} async-done(((f32[392,4,128]{2,1,0:T(4,128)}), f32[392,4,128]{2,1,0:T(4,128)S(1)}, u32[]{:S(2)}, u32[]{:S(2)}) %all-to-all-start) | async-done | bytes 802848 | tf_op jit(solution)/shard_map/all_to_all | solution.py:305
  24.7 4.5 %grid_blocks.1 = (bf16[392,2,128]{2,1,0:T(2,128)(2,1)}, f32[2,128,256]{2,1,0:T(8,128)S(1)}, bf16[2,128,256]{2,1,0:T(8,128)(2,1)S(1)}) custom-call(s32[1]{0:T(128)} %bitcast.6.refs_0_, f32[392,4,128]{2,1,0:T(4,128)S(1)} %all-to-all-done.refs_1_, f32[24,128]{1,0:T(8,128)S(1)} %copy.14.refs_2_, bf16[4,128,256]{2,1,0:T(8,128)(2,1)S(1)} %bitcast.17), custom_call_target="tpu_custom_call" | custom-call | tf_op jit(solution)/shard_map/grid_blocks/pallas_call | solution.py:315
  29.3 1.0 %collective-permute-start = (bf16[2,128,256]{2,1,0:T(8,128)(2,1)S(1)}, bf16[2,128,256]{2,1,0:T(8,128)(2,1)S(1)}, u32[]{:S(2)}, u32[]{:S(2)}) collective-permute-start(bf16[2,128,256]{2,1,0:T(8,128)(2,1)S(1)} %get-tuple-element.19), channel_id=1, source_target_pairs={{0,16},{2,18},{4,20},{6,22},{8,24},{10,26},{12,28},{14,30},{16,0},... | collective-permute-start | bytes 393224 | tf_op jit(solution)/shard_map/ppermute | solution.py:344
  30.3 15.5 %all-to-all-start.1 = ((bf16[392,2,128]{2,1,0:T(2,128)(2,1)}), bf16[392,2,128]{2,1,0:T(2,128)(2,1)S(1)}, u32[]{:S(2)}, u32[]{:S(2)}) async-start(bf16[392,2,128]{2,1,0:T(2,128)(2,1)} %get-tuple-element.17), calls=%async_computation.1 | async-start | bytes 401408 | tf_op jit(solution)/shard_map/all_to_all | solution.py:341
  45.7 0.0 collective-permute-done
  45.8 7.0 %all-gather.1 = bf16[4,128,256]{2,1,0:T(8,128)(2,1)S(1)} all-gather(bf16[2,128,256]{2,1,0:T(8,128)(2,1)S(1)} %add_convert_fusion), channel_id=3, replica_groups=mesh['tile'=16,'freq'=2] {'freq'}, dimensions={0}, use_global_device_ids=true | all-gather | bytes 393216 | tf_op jit(solution)/shard_map/all_gather | solution.py:345
  52.8 0.0 all-to-all-done.1.returned_ref
  52.8 1.5 %finish.1 = (f32[128,2,128]{2,1,0:T(2,128)}, f32[2,128,256]{2,1,0:T(8,128)}) custom-call(f32[2]{0:T(128)S(1)} %dynamic-slice_bitcast_fusion.row_ref, s32[128]{0:T(128)S(1)} %broadcast_add_fusion.slot_ref, bf16[392,2,128]{2,1,0:T(2,128)(2,1)S(1)} %all-to-all-done.1.returned_ref, bf16[2,2,128,256]{3,2,1,0:T(8,128)(2,1)S(1)} %bitcast.16), custom_call_target="tpu_custom_call" | custom-call | tf_op jit(solution)/shard_map/finish/pallas_call | solution.py:346
  (5 shorter events, 0.1 us)
Async XLA Ops:
  0.6 22.0 %copy-start = (f32[2,2]{1,0:T(2,128)S(1)}, f32[2,2]{1,0:T(2,128)}, u32[]{:S(2)}) copy-start(f32[2,2]{1,0:T(2,128)} %param.15) | copy-start | bytes 52
  4.8 19.9 %all-to-all-start = ((f32[392,4,128]{2,1,0:T(4,128)}), f32[392,4,128]{2,1,0:T(4,128)S(1)}, u32[]{:S(2)}, u32[]{:S(2)}) async-start(f32[392,4,128]{2,1,0:T(4,128)} %get-tuple-element.13), calls=%async_computation | async-start | bytes 1605632 | tf_op jit(solution)/shard_map/all_to_all | solution.py:305
  10.1 0.7 %copy-start.2 = (bf16[16,8,8]{0,2,1:T(8,128)(2,1)S(1)}, bf16[16,8,8]{0,2,1:T(8,128)(2,1)}, u32[]{:S(2)}) copy-start(bf16[16,8,8]{0,2,1:T(8,128)(2,1)} %param.14) | copy-start | bytes 6148
  10.1 0.9 %copy-start.1 = (bf16[1,2,128,256]{3,2,1,0:T(8,128)(2,1)S(1)}, bf16[1,2,128,256]{3,2,1,0:T(8,128)(2,1)}, u32[]{:S(2)}) copy-start(bf16[1,2,128,256]{3,2,1,0:T(8,128)(2,1)} %param.13) | copy-start | bytes 393220
  22.6 0.7 %copy-start.3 = (s32[128]{0:T(128)S(1)}, s32[128]{0:T(128)}, u32[]{:S(2)}) copy-start(s32[128]{0:T(128)} %get-tuple-element.12) | copy-start | bytes 1540
  29.3 16.5 %collective-permute-start = (bf16[2,128,256]{2,1,0:T(8,128)(2,1)S(1)}, bf16[2,128,256]{2,1,0:T(8,128)(2,1)S(1)}, u32[]{:S(2)}, u32[]{:S(2)}) collective-permute-start(bf16[2,128,256]{2,1,0:T(8,128)(2,1)S(1)} %get-tuple-element.19), channel_id=1, source_target_pairs={{0,16},{2,18},{4,20},{6,22},{8,24},{10,26},{12,28},{14,30},{16,0},... | collective-permute-start | bytes 393224 | tf_op jit(solution)/shard_map/ppermute | solution.py:344
  30.3 22.5 %all-to-all-start.1 = ((bf16[392,2,128]{2,1,0:T(2,128)(2,1)}), bf16[392,2,128]{2,1,0:T(2,128)(2,1)S(1)}, u32[]{:S(2)}, u32[]{:S(2)}) async-start(bf16[392,2,128]{2,1,0:T(2,128)(2,1)} %get-tuple-element.17), calls=%async_computation.1 | async-start | bytes 401408 | tf_op jit(solution)/shard_map/all_to_all | solution.py:341

commit v11 on v10

--- a/solution.py
+++ b/solution.py
@@ -15,6 +15,9 @@
 WHOLE_PARAMS = pltpu.CompilerParams(vmem_limit_bytes=62 * 1024 * 1024)
 TILE_SHIFT = 12
 PLANE_SHIFT = 16
+SOURCE_SHIFT = 21
+FULL = 32767
+SCALE = 2.0**20
 
 
 def scalar_div(value, count):
@@ -27,10 +30,19 @@
     return (local >> 1) * half + jnp.where((local & 1) == 0, rank, half - 1 - rank)
 
 
+def rows_per_source(capacity):
+    return (3 * (capacity + 1) + 7) // 8 * 8
+
+
+def two_halves(high, low):
+    return (high << 16) | (low & 0xFFFF)
+
+
 def pack_kernel(pairs, capacity, tiles_here, planes, plane_hbm, tile_hbm, vis_hbm, cell_hbm, sub_hbm,
-                sent_ref, slot_ref, plane_ref, tile_ref, vis_ref, cell_ref, sub_ref, about_ref, count_ref,
-                load_sem, about_sem):
+                sent_ref, slot_ref, plane_ref, tile_ref, vis_ref, cell_ref, sub_ref, about_ref, turned_ref,
+                count_ref, load_sem, about_sem):
     blocks = tile_ref.shape[0]
+    stride = rows_per_source(capacity)
     loads = [
         pltpu.make_async_copy(source, target, load_sem.at[i])
         for i, (source, target) in enumerate(
@@ -45,20 +57,10 @@
     ]
     for copy in loads:
         copy.start()
-    part = lax.broadcasted_iota(jnp.int32, (4, 128), 0)
-    empty = jnp.where(part == 0, float(planes << PLANE_SHIFT), 0.0)
-    abouts = [d * (capacity + 1) + capacity for d in range(pairs)]
     for d in range(pairs):
-        sent_ref[abouts[d]] = empty
         for t in range(2 * tiles_here):
             count_ref[d * 2 * tiles_here + t] = 0
-    fills = [
-        pltpu.make_async_copy(sent_ref.at[abouts[d]], about_ref.at[d], about_sem.at[d])
-        for d in range(pairs)
-    ]
-    for copy in fills:
-        copy.start()
-    for copy in fills + loads[:2]:
+    for copy in loads[:2]:
         copy.wait()
 
     def assign(b):
@@ -72,12 +74,7 @@
         count_ref[key] = rank + 1
         place = first_slot(local, rank, capacity)
         slot_ref[b] = pair * (capacity + 1) + place
-        code = (plane_ref[b] << PLANE_SHIFT) + (local << TILE_SHIFT)
-        about_ref[pair, 0, place] = code.astype(jnp.float32)
-
-    def move(b):
-        position = (cell_ref[b] * 8 + sub_ref[b]).astype(jnp.float32)
-        sent_ref[slot_ref[b]] = jnp.concatenate([vis_ref[b], position], axis=0)
+        about_ref[pair, 0, place] = plane_ref[b] << PLANE_SHIFT
 
     def each(work):
         def step(turn, carry):
@@ -90,18 +87,32 @@
     each(assign)
     for d in range(pairs):
         for t in range(2 * tiles_here):
-            about_ref[d, 1, t] = count_ref[d * 2 * tiles_here + t].astype(jnp.float32)
-    returns = [
-        pltpu.make_async_copy(about_ref.at[d], sent_ref.at[abouts[d]], about_sem.at[d])
-        for d in range(pairs)
-    ]
-    for copy in returns:
-        copy.start()
+            about_ref[d, 1, t] = count_ref[d * 2 * tiles_here + t]
+    turn_about = pltpu.make_async_copy(about_ref, turned_ref, about_sem)
+    turn_about.start()
     for copy in loads[2:]:
         copy.wait()
+    largest = jnp.max(jnp.max(jnp.abs(vis_ref[...]), axis=0), keepdims=True)
+    largest = jnp.maximum(jnp.ceil(largest * SCALE), 1.0)
+    inverse = (FULL * SCALE) / largest
+
+    def move(b):
+        slot = slot_ref[b]
+        row = 3 * slot + scalar_div(slot, capacity + 1) * (stride - 3 * (capacity + 1))
+        value = jnp.clip(jnp.round(vis_ref[b] * inverse), -FULL, FULL).astype(jnp.int32)
+        for i, pair in enumerate([value, cell_ref[b], sub_ref[b]]):
+            sent_ref[pl.ds(row + i, 1), :] = two_halves(pair[0:1], pair[1:2])
+
     each(move)
-    for copy in returns:
-        copy.wait()
+    turn_about.wait()
+    lane = lax.broadcasted_iota(jnp.int32, (1, 128), 1)
+    for d in range(pairs):
+        row = d * stride + 3 * capacity
+        sent_ref[row : row + 1, :] = turned_ref[d, 0:1, :]
+        sent_ref[row + 1 : row + 2, :] = jnp.zeros((1, 128), jnp.int32)
+        sent_ref[row + 2 : row + 3, :] = jnp.where(
+            lane < 2 * tiles_here, turned_ref[d, 1:2, :], largest.astype(jnp.int32)
+        )
 
 
 def finish_kernel(row_ref, slot_ref, returned_ref, grid_ref, residual_ref, coupled_ref):
@@ -136,11 +147,14 @@
     tiles, side, wide = model_ref.shape
     groups = side // 16
     zero_row = table_ref.shape[0] - 8
+    stride = rows_per_source(capacity)
     lane = lax.broadcasted_iota(jnp.int32, (1, 128), 1)
     for s in range(pairs):
-        about = got_ref[s * (capacity + 1) + capacity].astype(jnp.int32)
-        code_ref[s, 0:1, :] = about[0:1] + (lane + s * (capacity + 1))
-        code_ref[s, 1:2, :] = about[1:2]
+        row = s * stride + 3 * capacity
+        code_ref[s, 0:1, :] = got_ref[row : row + 1, :] + (
+            lane + s * (capacity + 1) + (s << SOURCE_SHIFT)
+        )
+        code_ref[s, 1:2, :] = got_ref[row + 2 : row + 3, :]
     fill = pltpu.make_async_copy(code_ref, about_ref, sem)
     fill.start()
     for t in range(tiles):
@@ -165,7 +179,8 @@
                 for which in range(8):
                     k = turn * 8 + which
                     place = k if t % 2 == 0 else capacity // 2 - 1 - k
-                    list_ref[filled + k] = about_ref[s, 0, jnp.maximum(first + place, 0)]
+                    code = about_ref[s, 0, jnp.maximum(first + place, 0)]
+                    list_ref[filled + k] = code + (t << TILE_SHIFT)
                 return carry
 
             lax.fori_loop(0, (found + 7) >> 3, some, 0)
@@ -181,19 +196,26 @@
     def read(which):
         entry = list_ref[which]
         slot = entry & ((1 << TILE_SHIFT) - 1)
-        data = got_ref[slot]
-        position = data.astype(jnp.int32)
-        start, offset = position >> 3, (position & 7) << 4
-        table = jnp.broadcast_to(table_ref[pl.ds(entry >> PLANE_SHIFT, 1), :], (8, 128))
-
-        def parts(row):
+        plane = (entry >> PLANE_SHIFT) & ((1 << (SOURCE_SHIFT - PLANE_SHIFT)) - 1)
+        source = entry >> SOURCE_SHIFT
+        row = 3 * slot + source * (stride - 3 * (capacity + 1))
+        table = jnp.broadcast_to(table_ref[pl.ds(plane, 1), :], (8, 128))
+
+        def words(i):
+            return got_ref[pl.ds(row + i, 1), :]
+
+        def parts(shift):
+            start = (words(1) >> shift) & 0xFFFF
+            offset = ((words(2) >> shift) & 7) << 4
             return spread_parts(
-                jnp.broadcast_to(start[row : row + 1], (8, 128)),
-                jnp.broadcast_to(offset[row : row + 1], (8, 128)),
-                table,
+                jnp.broadcast_to(start, (8, 128)), jnp.broadcast_to(offset, (8, 128)), table
             )
 
-        return slot, data, parts
+        def sample(part):
+            step = about_ref[source, 1, tiles].astype(jnp.float32) * (1.0 / (FULL * SCALE))
+            return ((words(0) << (16 * part)) >> 16).astype(jnp.float32) * step
+
+        return slot, sample, parts
 
     def chunk_tile(turn):
         return (list_ref[turn * UNROLL] >> TILE_SHIFT) & 15
@@ -202,7 +224,7 @@
         row_ref, partial_ref = row_refs[which % len(row_refs)], partial_refs[which % len(partial_refs)]
         for u in range(UNROLL):
             _, _, parts = read(turn * UNROLL + u)
-            taps, group = parts(2)
+            taps, group = parts(16)
             taps = taps.astype(jnp.bfloat16)
             group = group.astype(jnp.float32).astype(jnp.bfloat16)
             for k in range(groups):
@@ -217,9 +239,9 @@
         row_ref, partial_ref = row_refs[which % len(row_refs)], partial_refs[which % len(partial_refs)]
         weighted_ref = weighted_refs[which % len(weighted_refs)]
         for u in range(UNROLL):
-            slot, data, parts = read(turn * UNROLL + u)
+            slot, sample, parts = read(turn * UNROLL + u)
             columns = slice(128 * u, 128 * u + 128)
-            taps, group = parts(3)
+            taps, group = parts(0)
             residuals, samples = [], []
             for part in range(2):
                 picked = jnp.zeros((16, 128), jnp.float32)
@@ -227,7 +249,7 @@
                     low = part * side + 16 * k
                     picked = jnp.where(group == k, partial_ref[low : low + 16, columns], picked)
                 model = jnp.sum(picked * taps, axis=0, keepdims=True)
-                residual = data[part : part + 1] - model
+                residual = sample(part) - model
                 residuals.append(residual)
                 samples.append((residual * taps).astype(jnp.bfloat16))
             residual_ref[slot] = jnp.concatenate(residuals, axis=0).astype(jnp.bfloat16)
@@ -283,7 +305,7 @@
     sent, slot = pl.pallas_call(
         lambda *refs: pack_kernel(pairs, capacity, tiles_here, planes, *refs),
         out_shape=(
-            jax.ShapeDtypeStruct((slots, 4, rows), jnp.float32),
+            jax.ShapeDtypeStruct((pairs * rows_per_source(capacity), rows), jnp.int32),
             jax.ShapeDtypeStruct((blocks,), jnp.int32),
         ),
         in_specs=[HBM] * 5,
@@ -294,10 +316,11 @@
             pltpu.VMEM((blocks, 2, rows), jnp.float32),
             pltpu.VMEM((blocks, 2, rows), jnp.int32),
             pltpu.VMEM((blocks, 2, rows), jnp.int32),
-            pltpu.SMEM((pairs, 4, rows), jnp.float32),
+            pltpu.SMEM((pairs, 2, rows), jnp.int32),
+            pltpu.VMEM((pairs, 2, rows), jnp.int32),
             pltpu.SMEM((pairs * 2 * tiles_here,), jnp.int32),
             pltpu.SemaphoreType.DMA((5,)),
-            pltpu.SemaphoreType.DMA((pairs,)),
+            pltpu.SemaphoreType.DMA,
         ],
         compiler_params=WHOLE_PARAMS,
         name="pack_blocks",

time: 54.4 us -> 52 us (0.956)
  starting transfers between devices: 21.7 us -> 10.8 us
  Pallas kernels: 10.2 us -> 20.9 us
  blocking collectives: 18.7 us -> 15.9 us
    all_to_all x1, starting transfers between devices: 15.5 us -> 3.51 us  [body(): lax.all_to_all(residual, 'tile', split_axis=0, concat_axis=0, tiled=True,...]
    pallas_call x1, Pallas kernels: 4.55 us -> 15.6 us  [body(): pl.pallas_call(lambda *refs: grid_kernel(pairs, capacity, *refs), out_sha...]
    all_gather x1, blocking collectives: 11.6 us -> 9.71 us  [body(): lax.all_gather(model_grid[0], 'tile', axis=0, tiled=True, axis_index_grou...]
    ppermute x1, starting transfers between devices: 1 us -> 2.04 us  [body(): grid_sum = own + lax.ppermute(other, 'tile', swap).astype(jnp.float32)]
    all_gather x1, blocking collectives: 7.01 us -> 6.21 us  [body(): lax.all_gather(grid_sum.astype(jnp.bfloat16)[None], 'freq', axis=0, tiled...]
  transfers between devices with their start and end apart: 3 -> 3, of which waited for: 1 -> 2; matrix products, arithmetic and copies ran while one was open for 0% -> 0% of each run, Pallas kernels for 0% -> 0%
where the time goes in v11:
time: 52 us; the launch traced here: 51.7 us
  Pallas kernels  20.9 us (40%)
  blocking collectives  15.9 us (31%)
  starting transfers between devices  10.8 us (21%)
  waiting for transfers between devices  1.79 us (3%)
  local copies, waits for them, and re-layouts  1.55 us (3%)
  between operations  0.7 us (1%)
    pallas_call x1, Pallas kernels, body(): pl.pallas_call(lambda *refs: grid_kernel(pairs, capacity, *refs), out_sha...  15.6 us
    all_gather x1, blocking collectives, body(): lax.all_gather(model_grid[0], 'tile', axis=0, tiled=True, axis_index_grou...  9.71 us
    all_gather x1, blocking collectives, body(): lax.all_gather(grid_sum.astype(jnp.bfloat16)[None], 'freq', axis=0, tiled...  6.21 us
    all_to_all x1, starting transfers between devices, body(): lax.all_to_all(sent, 'tile', split_axis=0, concat_axis=0, tiled=True, axi...  5.27 us
    pallas_call x1, Pallas kernels, body(): pl.pallas_call(lambda *refs: pack_kernel(pairs, capacity, tiles_here, pla...  3.81 us
    all_to_all x1, starting transfers between devices, body(): lax.all_to_all(residual, 'tile', split_axis=0, concat_axis=0, tiled=True,...  3.51 us
    ppermute x1, starting transfers between devices, body(): grid_sum = own + lax.ppermute(other, 'tile', swap).astype(jnp.float32)  2.04 us
    pallas_call x1, Pallas kernels, body(): pl.pallas_call(finish_kernel, out_shape=(jax.ShapeDtypeStruct((blocks, 2,...  1.52 us
  transfers between devices with their start and end apart: 3, of which 2 were waited for; matrix products, arithmetic and copies ran while one was open for 0% of the time, Pallas kernels for 0%

profile of v11, /device:TPU:0, one launch (start us, length us, event | category | flops | bytes accessed | tf_op | source)
XLA Modules:
  0.0 51.7 jit_solution(8859730929487782772)
XLA Ops:
  0.6 0.0 copy-start
  0.6 3.8 %pack_blocks.1 = (s32[1216,128]{1,0:T(8,128)}, s32[128]{0:T(128)}) custom-call(s32[128]{0:T(128)} %bitcast.26, s32[128]{0:T(128)} %bitcast.27, f32[128,2,128]{2,1,0:T(2,128)} %bitcast.22, s32[128,2,128]{2,1,0:T(2,128)} %bitcast.23, s32[128,2,128]{2,1,0:T(2,128)} %bitcast.24), custom_call_target="tpu_custom_call" | custom-call | tf_op jit(solution)/shard_map/pack_blocks/pallas_call | solution.py:305
  4.5 5.3 %all-to-all-start = ((s32[8,152,128]{2,1,0:T(8,128)}), s32[8,152,128]{2,1,0:T(8,128)S(1)}, u32[]{:S(2)}, u32[]{:S(2)}) async-start(s32[8,152,128]{2,1,0:T(8,128)} %bitcast.21), calls=%async_computation | async-start | bytes 1245184 | tf_op jit(solution)/shard_map/all_to_all | solution.py:328
  9.7 0.0 copy-start.2
  9.7 0.0 copy-start.1
  9.8 0.7 %copy-done.2 = bf16[16,8,8]{0,2,1:T(8,128)(2,1)S(1)} copy-done((bf16[16,8,8]{0,2,1:T(8,128)(2,1)S(1)}, bf16[16,8,8]{0,2,1:T(8,128)(2,1)}, u32[]{:S(2)}) %copy-start.2) | copy-done | bytes 2072
  10.5 0.1 copy.14.refs_2_
  10.5 0.1 copy-done.1
  10.7 9.7 %all-gather = bf16[1,4,128,256]{3,2,0,1:T(8,128)(2,1)S(1)} all-gather(bf16[1,2,128,256]{3,2,0,1:T(8,128)(2,1)S(1)} %bitcast.25), channel_id=2, replica_groups={{0,16},{2,18},{4,20},{6,22},{8,24},{10,26},{12,28},{14,30},{1,17},{3,19..., dimensions={1}, use_global_device_ids=true | all-gather | bytes 393216 | tf_op jit(solution)/shard_map/all_gather | solution.py:298
  20.4 0.0 copy-done
  20.4 0.0 copy-start.3
  20.4 0.6 %copy-done.3 = s32[128]{0:T(128)S(1)} copy-done((s32[128]{0:T(128)S(1)}, s32[128]{0:T(128)}, u32[]{:S(2)}) %copy-start.3) | copy-done | bytes 536
  21.0 1.4 %all-to-all-done = s32[8,152,128]{2,1,0:T(8,128)S(1)} async-done(((s32[8,152,128]{2,1,0:T(8,128)}), s32[8,152,128]{2,1,0:T(8,128)S(1)}, u32[]{:S(2)}, u32[]{:S(2)}) %all-to-all-start) | async-done | bytes 622624 | tf_op jit(solution)/shard_map/all_to_all | solution.py:328
  22.4 15.6 %grid_blocks.1 = (bf16[392,2,128]{2,1,0:T(2,128)(2,1)}, f32[2,128,256]{2,1,0:T(8,128)S(1)}, bf16[2,128,256]{2,1,0:T(8,128)(2,1)S(1)}) custom-call(s32[1]{0:T(128)} %bitcast.8.refs_0_, s32[1216,128]{1,0:T(8,128)S(1)} %bitcast.18, f32[24,128]{1,0:T(8,128)S(1)} %copy.14.refs_2_, bf16[4,128,256]{2,1,0:T(8,128)(2,1)S(1)} %bitcast.19), custom_call_target="tpu_custom_call" | custom-call | tf_op jit(solution)/shard_map/grid_blocks/pallas_call | solution.py:338
  38.0 2.0 %collective-permute-start = (bf16[2,128,256]{2,1,0:T(8,128)(2,1)S(1)}, bf16[2,128,256]{2,1,0:T(8,128)(2,1)S(1)}, u32[]{:S(2)}, u32[]{:S(2)}) collective-permute-start(bf16[2,128,256]{2,1,0:T(8,128)(2,1)S(1)} %get-tuple-element.19), channel_id=1, source_target_pairs={{0,16},{2,18},{4,20},{6,22},{8,24},{10,26},{12,28},{14,30},{16,0},... | collective-permute-start | bytes 393224 | tf_op jit(solution)/shard_map/ppermute | solution.py:367
  40.1 3.5 %all-to-all-start.1 = ((bf16[392,2,128]{2,1,0:T(2,128)(2,1)}), bf16[392,2,128]{2,1,0:T(2,128)(2,1)S(1)}, u32[]{:S(2)}, u32[]{:S(2)}) async-start(bf16[392,2,128]{2,1,0:T(2,128)(2,1)} %get-tuple-element.17), calls=%async_computation.1 | async-start | bytes 401408 | tf_op jit(solution)/shard_map/all_to_all | solution.py:364
  43.6 0.4 collective-permute-done
  44.0 6.2 %all-gather.1 = bf16[4,128,256]{2,1,0:T(8,128)(2,1)S(1)} all-gather(bf16[2,128,256]{2,1,0:T(8,128)(2,1)S(1)} %add_convert_fusion), channel_id=3, replica_groups=mesh['tile'=16,'freq'=2] {'freq'}, dimensions={0}, use_global_device_ids=true | all-gather | bytes 393216 | tf_op jit(solution)/shard_map/all_gather | solution.py:368
  50.2 0.0 all-to-all-done.1.returned_ref
  50.2 1.5 %finish.1 = (f32[128,2,128]{2,1,0:T(2,128)}, f32[2,128,256]{2,1,0:T(8,128)}) custom-call(f32[2]{0:T(128)S(1)} %dynamic-slice_bitcast_fusion.row_ref, s32[128]{0:T(128)S(1)} %broadcast_add_fusion.slot_ref, bf16[392,2,128]{2,1,0:T(2,128)(2,1)S(1)} %all-to-all-done.1.returned_ref, bf16[2,2,128,256]{3,2,1,0:T(8,128)(2,1)S(1)} %bitcast.20), custom_call_target="tpu_custom_call" | custom-call | tf_op jit(solution)/shard_map/finish/pallas_call | solution.py:369
  (5 shorter events, 0.1 us)
Async XLA Ops:
  0.6 19.7 %copy-start = (f32[2,2]{1,0:T(2,128)S(1)}, f32[2,2]{1,0:T(2,128)}, u32[]{:S(2)}) copy-start(f32[2,2]{1,0:T(2,128)} %param.15) | copy-start | bytes 52
  4.5 18.0 %all-to-all-start = ((s32[8,152,128]{2,1,0:T(8,128)}), s32[8,152,128]{2,1,0:T(8,128)S(1)}, u32[]{:S(2)}, u32[]{:S(2)}) async-start(s32[8,152,128]{2,1,0:T(8,128)} %bitcast.21), calls=%async_computation | async-start | bytes 1245184 | tf_op jit(solution)/shard_map/all_to_all | solution.py:328
  9.7 0.7 %copy-start.2 = (bf16[16,8,8]{0,2,1:T(8,128)(2,1)S(1)}, bf16[16,8,8]{0,2,1:T(8,128)(2,1)}, u32[]{:S(2)}) copy-start(bf16[16,8,8]{0,2,1:T(8,128)(2,1)} %param.14) | copy-start | bytes 6148
  9.7 0.9 %copy-start.1 = (bf16[1,2,128,256]{3,2,1,0:T(8,128)(2,1)S(1)}, bf16[1,2,128,256]{3,2,1,0:T(8,128)(2,1)}, u32[]{:S(2)}) copy-start(bf16[1,2,128,256]{3,2,1,0:T(8,128)(2,1)} %param.13) | copy-start | bytes 393220
  20.4 0.7 %copy-start.3 = (s32[128]{0:T(128)S(1)}, s32[128]{0:T(128)}, u32[]{:S(2)}) copy-start(s32[128]{0:T(128)} %get-tuple-element.12) | copy-start | bytes 1540
  38.0 5.9 %collective-permute-start = (bf16[2,128,256]{2,1,0:T(8,128)(2,1)S(1)}, bf16[2,128,256]{2,1,0:T(8,128)(2,1)S(1)}, u32[]{:S(2)}, u32[]{:S(2)}) collective-permute-start(bf16[2,128,256]{2,1,0:T(8,128)(2,1)S(1)} %get-tuple-element.19), channel_id=1, source_target_pairs={{0,16},{2,18},{4,20},{6,22},{8,24},{10,26},{12,28},{14,30},{16,0},... | collective-permute-start | bytes 393224 | tf_op jit(solution)/shard_map/ppermute | solution.py:367
  40.1 10.1 %all-to-all-start.1 = ((bf16[392,2,128]{2,1,0:T(2,128)(2,1)}), bf16[392,2,128]{2,1,0:T(2,128)(2,1)S(1)}, u32[]{:S(2)}, u32[]{:S(2)}) async-start(bf16[392,2,128]{2,1,0:T(2,128)(2,1)} %get-tuple-element.17), calls=%async_computation.1 | async-start | bytes 401408 | tf_op jit(solution)/shard_map/all_to_all | solution.py:364

commit v12 on v11

--- a/solution.py
+++ b/solution.py
@@ -176,14 +176,14 @@
             found = about_ref[s, 1, t]
 
             def some(turn, carry):
-                for which in range(8):
-                    k = turn * 8 + which
+                for which in range(16):
+                    k = turn * 16 + which
                     place = k if t % 2 == 0 else capacity // 2 - 1 - k
                     code = about_ref[s, 0, jnp.maximum(first + place, 0)]
                     list_ref[filled + k] = code + (t << TILE_SHIFT)
                 return carry
 
-            lax.fori_loop(0, (found + 7) >> 3, some, 0)
+            lax.fori_loop(0, (found + 15) >> 4, some, 0)
             return filled + found
 
         lax.fori_loop(0, pairs, enlist, start + spare)
@@ -261,8 +261,8 @@
                         group == k, samples[part], zero
                     )
         grid_ref[chunk_tile(turn)] += lax.dot_general(
+            weighted_ref[...],
             row_ref[...],
-            weighted_ref[...],
             (((1,), (1,)), ((), ())),
             preferred_element_type=jnp.float32,
         )
@@ -279,8 +279,8 @@
     half = tiles // 2
     member = member_ref[0]
     for t in range(half):
-        own_ref[t] = grid_ref[member * half + t]
-        other_ref[t] = grid_ref[(1 - member) * half + t].astype(jnp.bfloat16)
+        own_ref[t] = grid_ref[member * half + t].T
+        other_ref[t] = grid_ref[(1 - member) * half + t].T.astype(jnp.bfloat16)
 
 
 def body(visibilities, uv_cell, sub_pixel, w_plane, block_tile, model_grid, kernel_table, coupling):
@@ -346,7 +346,7 @@
         out_specs=(VMEM, VMEM, VMEM),
         scratch_shapes=[
             pltpu.VMEM((2 * tiles_here, wide, side), jnp.bfloat16),
-            pltpu.VMEM((2 * tiles_here, side, wide), jnp.float32),
+            pltpu.VMEM((2 * tiles_here, wide, side), jnp.float32),
             pltpu.VMEM((pairs, 2, rows), jnp.int32),
             pltpu.SMEM((pairs, 2, rows), jnp.int32),
             pltpu.SMEM(

time: 52 us -> 51.5 us (level)
  Pallas kernels: 20.9 us -> 20.3 us
    pallas_call x1, Pallas kernels: 15.6 us -> 15 us  [body(): pl.pallas_call(lambda *refs: grid_kernel(pairs, capacity, *refs), out_sha...]
where the time goes in v12:
time: 51.5 us; the launch traced here: 51.1 us
  Pallas kernels  20.3 us (39%)
  blocking collectives  15.7 us (30%)
  starting transfers between devices  11 us (21%)
  waiting for transfers between devices  1.93 us (4%)
  local copies, waits for them, and re-layouts  1.55 us (3%)
  between operations  0.7 us (1%)
    pallas_call x1, Pallas kernels, body(): pl.pallas_call(lambda *refs: grid_kernel(pairs, capacity, *refs), out_sha...  15 us
    all_gather x1, blocking collectives, body(): lax.all_gather(model_grid[0], 'tile', axis=0, tiled=True, axis_index_grou...  9.71 us
    all_gather x1, blocking collectives, body(): lax.all_gather(grid_sum.astype(jnp.bfloat16)[None], 'freq', axis=0, tiled...  5.97 us
    all_to_all x1, starting transfers between devices, body(): lax.all_to_all(sent, 'tile', split_axis=0, concat_axis=0, tiled=True, axi...  5.27 us
    pallas_call x1, Pallas kernels, body(): pl.pallas_call(lambda *refs: pack_kernel(pairs, capacity, tiles_here, pla...  3.81 us
    all_to_all x1, starting transfers between devices, body(): lax.all_to_all(residual, 'tile', split_axis=0, concat_axis=0, tiled=True,...  3.39 us
    ppermute x1, starting transfers between devices, body(): grid_sum = own + lax.ppermute(other, 'tile', swap).astype(jnp.float32)  2.29 us
    pallas_call x1, Pallas kernels, body(): pl.pallas_call(finish_kernel, out_shape=(jax.ShapeDtypeStruct((blocks, 2,...  1.52 us
  transfers between devices with their start and end apart: 3, of which 2 were waited for; matrix products, arithmetic and copies ran while one was open for 0% of the time, Pallas kernels for 0%

profile of v12, /device:TPU:0, one launch (start us, length us, event | category | flops | bytes accessed | tf_op | source)
XLA Modules:
  0.0 51.1 jit_solution(8299277530794698469)
XLA Ops:
  0.6 0.0 copy-start
  0.6 3.8 %pack_blocks.1 = (s32[1216,128]{1,0:T(8,128)}, s32[128]{0:T(128)}) custom-call(s32[128]{0:T(128)} %bitcast.26, s32[128]{0:T(128)} %bitcast.27, f32[128,2,128]{2,1,0:T(2,128)} %bitcast.22, s32[128,2,128]{2,1,0:T(2,128)} %bitcast.23, s32[128,2,128]{2,1,0:T(2,128)} %bitcast.24), custom_call_target="tpu_custom_call" | custom-call | tf_op jit(solution)/shard_map/pack_blocks/pallas_call | solution.py:305
  4.5 5.3 %all-to-all-start = ((s32[8,152,128]{2,1,0:T(8,128)}), s32[8,152,128]{2,1,0:T(8,128)S(1)}, u32[]{:S(2)}, u32[]{:S(2)}) async-start(s32[8,152,128]{2,1,0:T(8,128)} %bitcast.21), calls=%async_computation | async-start | bytes 1245184 | tf_op jit(solution)/shard_map/all_to_all | solution.py:328
  9.7 0.0 copy-start.2
  9.7 0.0 copy-start.1
  9.8 0.7 %copy-done.2 = bf16[16,8,8]{0,2,1:T(8,128)(2,1)S(1)} copy-done((bf16[16,8,8]{0,2,1:T(8,128)(2,1)S(1)}, bf16[16,8,8]{0,2,1:T(8,128)(2,1)}, u32[]{:S(2)}) %copy-start.2) | copy-done | bytes 2072
  10.5 0.1 copy.14.refs_2_
  10.5 0.1 copy-done.1
  10.7 9.7 %all-gather = bf16[1,4,128,256]{3,2,0,1:T(8,128)(2,1)S(1)} all-gather(bf16[1,2,128,256]{3,2,0,1:T(8,128)(2,1)S(1)} %bitcast.25), channel_id=2, replica_groups={{0,16},{2,18},{4,20},{6,22},{8,24},{10,26},{12,28},{14,30},{1,17},{3,19..., dimensions={1}, use_global_device_ids=true | all-gather | bytes 393216 | tf_op jit(solution)/shard_map/all_gather | solution.py:298
  20.4 0.0 copy-done
  20.4 0.0 copy-start.3
  20.4 0.6 %copy-done.3 = s32[128]{0:T(128)S(1)} copy-done((s32[128]{0:T(128)S(1)}, s32[128]{0:T(128)}, u32[]{:S(2)}) %copy-start.3) | copy-done | bytes 536
  21.0 1.4 %all-to-all-done = s32[8,152,128]{2,1,0:T(8,128)S(1)} async-done(((s32[8,152,128]{2,1,0:T(8,128)}), s32[8,152,128]{2,1,0:T(8,128)S(1)}, u32[]{:S(2)}, u32[]{:S(2)}) %all-to-all-start) | async-done | bytes 622624 | tf_op jit(solution)/shard_map/all_to_all | solution.py:328
  22.4 15.0 %grid_blocks.1 = (bf16[392,2,128]{2,1,0:T(2,128)(2,1)}, f32[2,128,256]{2,1,0:T(8,128)S(1)}, bf16[2,128,256]{2,1,0:T(8,128)(2,1)S(1)}) custom-call(s32[1]{0:T(128)} %bitcast.8.refs_0_, s32[1216,128]{1,0:T(8,128)S(1)} %bitcast.18, f32[24,128]{1,0:T(8,128)S(1)} %copy.14.refs_2_, bf16[4,128,256]{2,1,0:T(8,128)(2,1)S(1)} %bitcast.19), custom_call_target="tpu_custom_call" | custom-call | tf_op jit(solution)/shard_map/grid_blocks/pallas_call | solution.py:338
  37.4 2.3 %collective-permute-start = (bf16[2,128,256]{2,1,0:T(8,128)(2,1)S(1)}, bf16[2,128,256]{2,1,0:T(8,128)(2,1)S(1)}, u32[]{:S(2)}, u32[]{:S(2)}) collective-permute-start(bf16[2,128,256]{2,1,0:T(8,128)(2,1)S(1)} %get-tuple-element.19), channel_id=1, source_target_pairs={{0,16},{2,18},{4,20},{6,22},{8,24},{10,26},{12,28},{14,30},{16,0},... | collective-permute-start | bytes 393224 | tf_op jit(solution)/shard_map/ppermute | solution.py:367
  39.7 3.4 %all-to-all-start.1 = ((bf16[392,2,128]{2,1,0:T(2,128)(2,1)}), bf16[392,2,128]{2,1,0:T(2,128)(2,1)S(1)}, u32[]{:S(2)}, u32[]{:S(2)}) async-start(bf16[392,2,128]{2,1,0:T(2,128)(2,1)} %get-tuple-element.17), calls=%async_computation.1 | async-start | bytes 401408 | tf_op jit(solution)/shard_map/all_to_all | solution.py:364
  43.1 0.5 %collective-permute-done = bf16[2,128,256]{2,1,0:T(8,128)(2,1)S(1)} collective-permute-done((bf16[2,128,256]{2,1,0:T(8,128)(2,1)S(1)}, bf16[2,128,256]{2,1,0:T(8,128)(2,1)S(1)}, u32[]{:S(2)}, u32[]{:S(2)}) %collective-permute-start) | collective-permute-done | bytes 131104 | tf_op jit(solution)/shard_map/ppermute | solution.py:367
  43.7 6.0 %all-gather.1 = bf16[4,128,256]{2,1,0:T(8,128)(2,1)S(1)} all-gather(bf16[2,128,256]{2,1,0:T(8,128)(2,1)S(1)} %add_convert_fusion), channel_id=3, replica_groups=mesh['tile'=16,'freq'=2] {'freq'}, dimensions={0}, use_global_device_ids=true | all-gather | bytes 393216 | tf_op jit(solution)/shard_map/all_gather | solution.py:368
  49.6 0.0 all-to-all-done.1.returned_ref
  49.6 1.5 %finish.1 = (f32[128,2,128]{2,1,0:T(2,128)}, f32[2,128,256]{2,1,0:T(8,128)}) custom-call(f32[2]{0:T(128)S(1)} %dynamic-slice_bitcast_fusion.row_ref, s32[128]{0:T(128)S(1)} %broadcast_add_fusion.slot_ref, bf16[392,2,128]{2,1,0:T(2,128)(2,1)S(1)} %all-to-all-done.1.returned_ref, bf16[2,2,128,256]{3,2,1,0:T(8,128)(2,1)S(1)} %bitcast.20), custom_call_target="tpu_custom_call" | custom-call | tf_op jit(solution)/shard_map/finish/pallas_call | solution.py:369
  (5 shorter events, 0.1 us)
Async XLA Ops:
  0.6 19.7 %copy-start = (f32[2,2]{1,0:T(2,128)S(1)}, f32[2,2]{1,0:T(2,128)}, u32[]{:S(2)}) copy-start(f32[2,2]{1,0:T(2,128)} %param.15) | copy-start | bytes 52
  4.5 18.0 %all-to-all-start = ((s32[8,152,128]{2,1,0:T(8,128)}), s32[8,152,128]{2,1,0:T(8,128)S(1)}, u32[]{:S(2)}, u32[]{:S(2)}) async-start(s32[8,152,128]{2,1,0:T(8,128)} %bitcast.21), calls=%async_computation | async-start | bytes 1245184 | tf_op jit(solution)/shard_map/all_to_all | solution.py:328
  9.7 0.7 %copy-start.2 = (bf16[16,8,8]{0,2,1:T(8,128)(2,1)S(1)}, bf16[16,8,8]{0,2,1:T(8,128)(2,1)}, u32[]{:S(2)}) copy-start(bf16[16,8,8]{0,2,1:T(8,128)(2,1)} %param.14) | copy-start | bytes 6148
  9.7 0.9 %copy-start.1 = (bf16[1,2,128,256]{3,2,1,0:T(8,128)(2,1)S(1)}, bf16[1,2,128,256]{3,2,1,0:T(8,128)(2,1)}, u32[]{:S(2)}) copy-start(bf16[1,2,128,256]{3,2,1,0:T(8,128)(2,1)} %param.13) | copy-start | bytes 393220
  20.4 0.7 %copy-start.3 = (s32[128]{0:T(128)S(1)}, s32[128]{0:T(128)}, u32[]{:S(2)}) copy-start(s32[128]{0:T(128)} %get-tuple-element.12) | copy-start | bytes 1540
  37.4 6.2 %collective-permute-start = (bf16[2,128,256]{2,1,0:T(8,128)(2,1)S(1)}, bf16[2,128,256]{2,1,0:T(8,128)(2,1)S(1)}, u32[]{:S(2)}, u32[]{:S(2)}) collective-permute-start(bf16[2,128,256]{2,1,0:T(8,128)(2,1)S(1)} %get-tuple-element.19), channel_id=1, source_target_pairs={{0,16},{2,18},{4,20},{6,22},{8,24},{10,26},{12,28},{14,30},{16,0},... | collective-permute-start | bytes 393224 | tf_op jit(solution)/shard_map/ppermute | solution.py:367
  39.7 9.9 %all-to-all-start.1 = ((bf16[392,2,128]{2,1,0:T(2,128)(2,1)}), bf16[392,2,128]{2,1,0:T(2,128)(2,1)S(1)}, u32[]{:S(2)}, u32[]{:S(2)}) async-start(bf16[392,2,128]{2,1,0:T(2,128)(2,1)} %get-tuple-element.17), calls=%async_computation.1 | async-start | bytes 401408 | tf_op jit(solution)/shard_map/all_to_all | solution.py:364

commit v13 on v12

--- a/solution.py
+++ b/solution.py
@@ -116,9 +116,11 @@
 
 
 def finish_kernel(row_ref, slot_ref, returned_ref, grid_ref, residual_ref, coupled_ref):
-    coupled_ref[...] = sum(
-        row_ref[g] * grid_ref[g].astype(jnp.float32) for g in range(grid_ref.shape[0])
-    )
+    planes, tiles_here = grid_ref.shape[:2]
+    for t in range(tiles_here):
+        coupled_ref[t] = sum(
+            row_ref[g] * grid_ref[g, t].astype(jnp.float32) for g in range(planes)
+        ).T
 
     def step(turn, carry):
         for which in range(8):
@@ -143,7 +145,7 @@
 
 def grid_kernel(pairs, capacity, member_ref, got_ref, table_ref, model_ref, residual_ref, own_ref,
                 other_ref, turned_ref, grid_ref, code_ref, about_ref, list_ref, sem, *buffers):
-    row_refs, partial_refs, weighted_refs = buffers[:4], buffers[4:8], buffers[8:]
+    row_refs, picked_refs = buffers[:4], buffers[4:]
     tiles, side, wide = model_ref.shape
     groups = side // 16
     zero_row = table_ref.shape[0] - 8
@@ -221,9 +223,9 @@
         return (list_ref[turn * UNROLL] >> TILE_SHIFT) & 15
 
     def front(turn, which):
-        row_ref, partial_ref = row_refs[which % len(row_refs)], partial_refs[which % len(partial_refs)]
-        for u in range(UNROLL):
-            _, _, parts = read(turn * UNROLL + u)
+        row_ref, picked_ref = row_refs[which % len(row_refs)], picked_refs[which % len(picked_refs)]
+        blocks = [read(turn * UNROLL + u) for u in range(UNROLL)]
+        for u, (_, _, parts) in enumerate(blocks):
             taps, group = parts(16)
             taps = taps.astype(jnp.bfloat16)
             group = group.astype(jnp.float32).astype(jnp.bfloat16)
@@ -231,37 +233,38 @@
                 row_ref[16 * k : 16 * k + 16, 128 * u : 128 * u + 128] = jnp.where(
                     group == k, taps, zero
                 )
-        partial_ref[...] = jnp.dot(
+        partial = jnp.dot(
             turned_ref[chunk_tile(turn)], row_ref[...], preferred_element_type=jnp.float32
         )
+        for u, (_, _, parts) in enumerate(blocks):
+            columns = slice(128 * u, 128 * u + 128)
+            taps, group = parts(0)
+            for part in range(2):
+                picked = jnp.zeros((16, 128), jnp.float32)
+                for k in range(groups):
+                    low = part * side + 16 * k
+                    picked = jnp.where(group == k, partial[low : low + 16, columns], picked)
+                picked_ref[part, :, columns] = picked * taps
 
     def back(turn, which):
-        row_ref, partial_ref = row_refs[which % len(row_refs)], partial_refs[which % len(partial_refs)]
-        weighted_ref = weighted_refs[which % len(weighted_refs)]
+        row_ref, picked_ref = row_refs[which % len(row_refs)], picked_refs[which % len(picked_refs)]
+        weighted = []
         for u in range(UNROLL):
             slot, sample, parts = read(turn * UNROLL + u)
             columns = slice(128 * u, 128 * u + 128)
             taps, group = parts(0)
-            residuals, samples = [], []
+            group = group.astype(jnp.float32).astype(jnp.bfloat16)
+            residuals, pieces = [], []
             for part in range(2):
-                picked = jnp.zeros((16, 128), jnp.float32)
-                for k in range(groups):
-                    low = part * side + 16 * k
-                    picked = jnp.where(group == k, partial_ref[low : low + 16, columns], picked)
-                model = jnp.sum(picked * taps, axis=0, keepdims=True)
+                model = jnp.sum(picked_ref[part, :, columns], axis=0, keepdims=True)
                 residual = sample(part) - model
                 residuals.append(residual)
-                samples.append((residual * taps).astype(jnp.bfloat16))
+                value = (residual * taps).astype(jnp.bfloat16)
+                pieces += [jnp.where(group == k, value, zero) for k in range(groups)]
             residual_ref[slot] = jnp.concatenate(residuals, axis=0).astype(jnp.bfloat16)
-            group = group.astype(jnp.float32).astype(jnp.bfloat16)
-            for part in range(2):
-                for k in range(groups):
-                    low = part * side + 16 * k
-                    weighted_ref[low : low + 16, columns] = jnp.where(
-                        group == k, samples[part], zero
-                    )
+            weighted.append(jnp.concatenate(pieces, axis=0))
         grid_ref[chunk_tile(turn)] += lax.dot_general(
-            weighted_ref[...],
+            jnp.concatenate(weighted, axis=1),
             row_ref[...],
             (((1,), (1,)), ((), ())),
             preferred_element_type=jnp.float32,
@@ -279,8 +282,8 @@
     half = tiles // 2
     member = member_ref[0]
     for t in range(half):
-        own_ref[t] = grid_ref[member * half + t].T
-        other_ref[t] = grid_ref[(1 - member) * half + t].T.astype(jnp.bfloat16)
+        own_ref[t] = grid_ref[member * half + t]
+        other_ref[t] = grid_ref[(1 - member) * half + t].astype(jnp.bfloat16)
 
 
 def body(visibilities, uv_cell, sub_pixel, w_plane, block_tile, model_grid, kernel_table, coupling):
@@ -339,8 +342,8 @@
         lambda *refs: grid_kernel(pairs, capacity, *refs),
         out_shape=(
             jax.ShapeDtypeStruct((slots, 2, rows), jnp.bfloat16),
-            jax.ShapeDtypeStruct((tiles_here, side, wide), jnp.float32),
-            jax.ShapeDtypeStruct((tiles_here, side, wide), jnp.bfloat16),
+            jax.ShapeDtypeStruct((tiles_here, wide, side), jnp.float32),
+            jax.ShapeDtypeStruct((tiles_here, wide, side), jnp.bfloat16),
         ),
         in_specs=[SMEM, VMEM, VMEM, VMEM],
         out_specs=(VMEM, VMEM, VMEM),
@@ -354,8 +357,7 @@
             ),
             pltpu.SemaphoreType.DMA,
             *[pltpu.VMEM((side, UNROLL * rows), jnp.bfloat16)] * 4,
-            *[pltpu.VMEM((wide, UNROLL * rows), jnp.float32)] * 4,
-            *[pltpu.VMEM((wide, UNROLL * rows), jnp.bfloat16)] * 2,
+            *[pltpu.VMEM((2, 16, UNROLL * rows), jnp.float32)] * 4,
         ],
         compiler_params=PARAMS,
         name="grid_blocks",

time: 51.5 us -> 51.4 us (level)
  Pallas kernels: 20.3 us -> 19.6 us
    pallas_call x1, Pallas kernels: 15 us -> 14.1 us  [body(): pl.pallas_call(lambda *refs: grid_kernel(pairs, capacity, *refs), out_sha...]
  transfers between devices with their start and end apart: 3 -> 3, of which waited for: 2 -> 1; matrix products, arithmetic and copies ran while one was open for 0% -> 0% of each run, Pallas kernels for 0% -> 0%
where the time goes in v13:
time: 51.4 us; the launch traced here: 50.6 us
  Pallas kernels  19.6 us (38%)
  blocking collectives  16.1 us (31%)
  starting transfers between devices  11.1 us (22%)
  local copies, waits for them, and re-layouts  1.55 us (3%)
  waiting for transfers between devices  1.46 us (3%)
  between operations  0.7 us (1%)
    pallas_call x1, Pallas kernels, body(): pl.pallas_call(lambda *refs: grid_kernel(pairs, capacity, *refs), out_sha...  14.1 us
    all_gather x1, blocking collectives, body(): lax.all_gather(model_grid[0], 'tile', axis=0, tiled=True, axis_index_grou...  9.71 us
    all_gather x1, blocking collectives, body(): lax.all_gather(grid_sum.astype(jnp.bfloat16)[None], 'freq', axis=0, tiled...  6.44 us
    all_to_all x1, starting transfers between devices, body(): lax.all_to_all(sent, 'tile', split_axis=0, concat_axis=0, tiled=True, axi...  5.27 us
    pallas_call x1, Pallas kernels, body(): pl.pallas_call(lambda *refs: pack_kernel(pairs, capacity, tiles_here, pla...  3.81 us
    all_to_all x1, starting transfers between devices, body(): lax.all_to_all(residual, 'tile', split_axis=0, concat_axis=0, tiled=True,...  3.39 us
    ppermute x1, starting transfers between devices, body(): grid_sum = own + lax.ppermute(other, 'tile', swap).astype(jnp.float32)  2.48 us
    pallas_call x1, Pallas kernels, body(): pl.pallas_call(finish_kernel, out_shape=(jax.ShapeDtypeStruct((blocks, 2,...  1.6 us
  transfers between devices with their start and end apart: 3, of which 1 were waited for; matrix products, arithmetic and copies ran while one was open for 0% of the time, Pallas kernels for 0%

profile of v13, /device:TPU:0, one launch (start us, length us, event | category | flops | bytes accessed | tf_op | source)
XLA Modules:
  0.0 50.6 jit_solution(606216098082166464)
XLA Ops:
  0.6 0.0 copy-start
  0.6 3.8 %pack_blocks.1 = (s32[1216,128]{1,0:T(8,128)}, s32[128]{0:T(128)}) custom-call(s32[128]{0:T(128)} %bitcast.26, s32[128]{0:T(128)} %bitcast.27, f32[128,2,128]{2,1,0:T(2,128)} %bitcast.22, s32[128,2,128]{2,1,0:T(2,128)} %bitcast.23, s32[128,2,128]{2,1,0:T(2,128)} %bitcast.24), custom_call_target="tpu_custom_call" | custom-call | tf_op jit(solution)/shard_map/pack_blocks/pallas_call | solution.py:308
  4.5 5.3 %all-to-all-start = ((s32[8,152,128]{2,1,0:T(8,128)}), s32[8,152,128]{2,1,0:T(8,128)S(1)}, u32[]{:S(2)}, u32[]{:S(2)}) async-start(s32[8,152,128]{2,1,0:T(8,128)} %bitcast.21), calls=%async_computation | async-start | bytes 1245184 | tf_op jit(solution)/shard_map/all_to_all | solution.py:331
  9.7 0.0 copy-start.2
  9.7 0.0 copy-start.1
  9.8 0.7 %copy-done.2 = bf16[16,8,8]{0,2,1:T(8,128)(2,1)S(1)} copy-done((bf16[16,8,8]{0,2,1:T(8,128)(2,1)S(1)}, bf16[16,8,8]{0,2,1:T(8,128)(2,1)}, u32[]{:S(2)}) %copy-start.2) | copy-done | bytes 2072
  10.5 0.1 copy.14.refs_2_
  10.5 0.1 copy-done.1
  10.7 9.7 %all-gather = bf16[1,4,128,256]{3,2,0,1:T(8,128)(2,1)S(1)} all-gather(bf16[1,2,128,256]{3,2,0,1:T(8,128)(2,1)S(1)} %bitcast.25), channel_id=2, replica_groups={{0,16},{2,18},{4,20},{6,22},{8,24},{10,26},{12,28},{14,30},{1,17},{3,19..., dimensions={1}, use_global_device_ids=true | all-gather | bytes 393216 | tf_op jit(solution)/shard_map/all_gather | solution.py:301
  20.4 0.0 copy-done
  20.4 0.0 copy-start.3
  20.4 0.6 %copy-done.3 = s32[128]{0:T(128)S(1)} copy-done((s32[128]{0:T(128)S(1)}, s32[128]{0:T(128)}, u32[]{:S(2)}) %copy-start.3) | copy-done | bytes 536
  21.0 1.4 %all-to-all-done = s32[8,152,128]{2,1,0:T(8,128)S(1)} async-done(((s32[8,152,128]{2,1,0:T(8,128)}), s32[8,152,128]{2,1,0:T(8,128)S(1)}, u32[]{:S(2)}, u32[]{:S(2)}) %all-to-all-start) | async-done | bytes 622624 | tf_op jit(solution)/shard_map/all_to_all | solution.py:331
  22.4 14.1 %grid_blocks.1 = (bf16[392,2,128]{2,1,0:T(2,128)(2,1)}, f32[2,256,128]{2,1,0:T(8,128)S(1)}, bf16[2,256,128]{2,1,0:T(8,128)(2,1)S(1)}) custom-call(s32[1]{0:T(128)} %bitcast.8.refs_0_, s32[1216,128]{1,0:T(8,128)S(1)} %bitcast.18, f32[24,128]{1,0:T(8,128)S(1)} %copy.14.refs_2_, bf16[4,128,256]{2,1,0:T(8,128)(2,1)S(1)} %bitcast.19), custom_call_target="tpu_custom_call" | custom-call | tf_op jit(solution)/shard_map/grid_blocks/pallas_call | solution.py:341
  36.6 2.5 %collective-permute-start = (bf16[2,256,128]{2,1,0:T(8,128)(2,1)S(1)}, bf16[2,256,128]{2,1,0:T(8,128)(2,1)S(1)}, u32[]{:S(2)}, u32[]{:S(2)}) collective-permute-start(bf16[2,256,128]{2,1,0:T(8,128)(2,1)S(1)} %get-tuple-element.19), channel_id=1, source_target_pairs={{0,16},{2,18},{4,20},{6,22},{8,24},{10,26},{12,28},{14,30},{16,0},... | collective-permute-start | bytes 393224 | tf_op jit(solution)/shard_map/ppermute | solution.py:369
  39.1 3.4 %all-to-all-start.1 = ((bf16[392,2,128]{2,1,0:T(2,128)(2,1)}), bf16[392,2,128]{2,1,0:T(2,128)(2,1)S(1)}, u32[]{:S(2)}, u32[]{:S(2)}) async-start(bf16[392,2,128]{2,1,0:T(2,128)(2,1)} %get-tuple-element.17), calls=%async_computation.1 | async-start | bytes 401408 | tf_op jit(solution)/shard_map/all_to_all | solution.py:366
  42.5 0.0 collective-permute-done
  42.6 6.4 %all-gather.1 = bf16[4,256,128]{2,1,0:T(8,128)(2,1)S(1)} all-gather(bf16[2,256,128]{2,1,0:T(8,128)(2,1)S(1)} %add_convert_fusion), channel_id=3, replica_groups=mesh['tile'=16,'freq'=2] {'freq'}, dimensions={0}, use_global_device_ids=true | all-gather | bytes 393216 | tf_op jit(solution)/shard_map/all_gather | solution.py:370
  49.0 0.0 all-to-all-done.1.returned_ref
  49.0 1.6 %finish.1 = (f32[128,2,128]{2,1,0:T(2,128)}, f32[2,128,256]{2,1,0:T(8,128)}) custom-call(f32[2]{0:T(128)S(1)} %dynamic-slice_bitcast_fusion.row_ref, s32[128]{0:T(128)S(1)} %broadcast_add_fusion.slot_ref, bf16[392,2,128]{2,1,0:T(2,128)(2,1)S(1)} %all-to-all-done.1.returned_ref, bf16[2,2,256,128]{3,2,1,0:T(8,128)(2,1)S(1)} %bitcast.20), custom_call_target="tpu_custom_call" | custom-call | tf_op jit(solution)/shard_map/finish/pallas_call | solution.py:371
  (5 shorter events, 0.1 us)
Async XLA Ops:
  0.6 19.7 %copy-start = (f32[2,2]{1,0:T(2,128)S(1)}, f32[2,2]{1,0:T(2,128)}, u32[]{:S(2)}) copy-start(f32[2,2]{1,0:T(2,128)} %param.15) | copy-start | bytes 52
  4.5 18.0 %all-to-all-start = ((s32[8,152,128]{2,1,0:T(8,128)}), s32[8,152,128]{2,1,0:T(8,128)S(1)}, u32[]{:S(2)}, u32[]{:S(2)}) async-start(s32[8,152,128]{2,1,0:T(8,128)} %bitcast.21), calls=%async_computation | async-start | bytes 1245184 | tf_op jit(solution)/shard_map/all_to_all | solution.py:331
  9.7 0.7 %copy-start.2 = (bf16[16,8,8]{0,2,1:T(8,128)(2,1)S(1)}, bf16[16,8,8]{0,2,1:T(8,128)(2,1)}, u32[]{:S(2)}) copy-start(bf16[16,8,8]{0,2,1:T(8,128)(2,1)} %param.14) | copy-start | bytes 6148
  9.7 0.9 %copy-start.1 = (bf16[1,2,128,256]{3,2,1,0:T(8,128)(2,1)S(1)}, bf16[1,2,128,256]{3,2,1,0:T(8,128)(2,1)}, u32[]{:S(2)}) copy-start(bf16[1,2,128,256]{3,2,1,0:T(8,128)(2,1)} %param.13) | copy-start | bytes 393220
  20.4 0.7 %copy-start.3 = (s32[128]{0:T(128)S(1)}, s32[128]{0:T(128)}, u32[]{:S(2)}) copy-start(s32[128]{0:T(128)} %get-tuple-element.12) | copy-start | bytes 1540
  36.6 5.9 %collective-permute-start = (bf16[2,256,128]{2,1,0:T(8,128)(2,1)S(1)}, bf16[2,256,128]{2,1,0:T(8,128)(2,1)S(1)}, u32[]{:S(2)}, u32[]{:S(2)}) collective-permute-start(bf16[2,256,128]{2,1,0:T(8,128)(2,1)S(1)} %get-tuple-element.19), channel_id=1, source_target_pairs={{0,16},{2,18},{4,20},{6,22},{8,24},{10,26},{12,28},{14,30},{16,0},... | collective-permute-start | bytes 393224 | tf_op jit(solution)/shard_map/ppermute | solution.py:369
  39.1 9.9 %all-to-all-start.1 = ((bf16[392,2,128]{2,1,0:T(2,128)(2,1)}), bf16[392,2,128]{2,1,0:T(2,128)(2,1)S(1)}, u32[]{:S(2)}, u32[]{:S(2)}) async-start(bf16[392,2,128]{2,1,0:T(2,128)(2,1)} %get-tuple-element.17), calls=%async_computation.1 | async-start | bytes 401408 | tf_op jit(solution)/shard_map/all_to_all | solution.py:366

commit v14 on v13

--- a/solution.py
+++ b/solution.py
@@ -6,8 +6,9 @@
 from jax.sharding import PartitionSpec as P
 
 UNROLL = 2
-CHUNKS = 8
+CHUNKS = 15
 AHEAD = 2
+BUFFERS = 5
 VMEM = pl.BlockSpec(memory_space=pltpu.VMEM)
 SMEM = pl.BlockSpec(memory_space=pltpu.SMEM)
 HBM = pl.BlockSpec(memory_space=pltpu.HBM)
@@ -145,7 +146,7 @@
 
 def grid_kernel(pairs, capacity, member_ref, got_ref, table_ref, model_ref, residual_ref, own_ref,
                 other_ref, turned_ref, grid_ref, code_ref, about_ref, list_ref, sem, *buffers):
-    row_refs, picked_refs = buffers[:4], buffers[4:]
+    row_refs, picked_refs = buffers[:BUFFERS], buffers[BUFFERS:]
     tiles, side, wide = model_ref.shape
     groups = side // 16
     zero_row = table_ref.shape[0] - 8
@@ -298,13 +299,8 @@
     swap = [(t, (t + pairs) % owners) for t in range(owners)]
     halves = [list(range(pairs)), list(range(pairs, owners))]
 
-    model = lax.all_gather(
-        model_grid[0],
-        "tile",
-        axis=0,
-        tiled=True,
-        axis_index_groups=[[t, t + pairs] for t in range(pairs)],
-    )
+    model_own = model_grid[0]
+    model_other = lax.ppermute(model_own, "tile", swap)
     sent, slot = pl.pallas_call(
         lambda *refs: pack_kernel(pairs, capacity, tiles_here, planes, *refs),
         out_shape=(
@@ -328,12 +324,18 @@
         compiler_params=WHOLE_PARAMS,
         name="pack_blocks",
     )(w_plane[0], block_tile[0], visibilities[0], uv_cell[0], sub_pixel[0])
+    sent, model_other = lax.optimization_barrier((sent, model_other))
     got = lax.all_to_all(
         sent, "tile", split_axis=0, concat_axis=0, tiled=True, axis_index_groups=halves
     )
     own_row = lax.dynamic_index_in_dim(coupling, lax.axis_index("freq"), 0, keepdims=False)
     slot, own_row, got = lax.optimization_barrier(
         (slot + lax.div(lax.axis_index("tile"), owners), own_row, got)
+    )
+    model = jnp.where(
+        member == 0,
+        jnp.concatenate([model_own, model_other]),
+        jnp.concatenate([model_other, model_own]),
     )
     table = jnp.pad(
         kernel_table.astype(jnp.float32), ((0, 8), (0, 0), (0, 16 - support))
@@ -356,8 +358,8 @@
                 (slots + capacity + (2 * tiles_here + CHUNKS + AHEAD) * UNROLL,), jnp.int32
             ),
             pltpu.SemaphoreType.DMA,
-            *[pltpu.VMEM((side, UNROLL * rows), jnp.bfloat16)] * 4,
-            *[pltpu.VMEM((2, 16, UNROLL * rows), jnp.float32)] * 4,
+            *[pltpu.VMEM((side, UNROLL * rows), jnp.bfloat16)] * BUFFERS,
+            *[pltpu.VMEM((2, 16, UNROLL * rows), jnp.float32)] * BUFFERS,
         ],
         compiler_params=PARAMS,
         name="grid_blocks",

time: 51.4 us -> 53.1 us (1.033)
  waiting for transfers between devices: 1.46 us -> 12.8 us
  blocking collectives: 16.1 us -> 5.64 us
  starting transfers between devices: 11.1 us -> 13.9 us
  Pallas kernels: 19.6 us -> 18.1 us
    all_gather x1 -> x0, blocking collectives: 9.71 us -> none  [body(): lax.all_gather(model_grid[0], 'tile', axis=0, tiled=True, axis_index_grou...]
    all_to_all x1, waiting for transfers between devices: 1.41 us -> 8.28 us  [body(): lax.all_to_all(sent, 'tile', split_axis=0, concat_axis=0, tiled=True, axi...]
    ppermute x0 -> x1, starting transfers between devices: none -> 4.1 us  [body(): model_other = lax.ppermute(model_own, 'tile', swap)]
    ppermute x0 -> x1, waiting for transfers between devices: none -> 2.82 us  [body(): model_other = lax.ppermute(model_own, 'tile', swap)]
    all_to_all x1, starting transfers between devices: 5.27 us -> 3.54 us  [body(): lax.all_to_all(sent, 'tile', split_axis=0, concat_axis=0, tiled=True, axi...]
    ppermute x1, waiting for transfers between devices: 0.05 us -> 1.65 us  [body(): grid_sum = own + lax.ppermute(other, 'tile', swap).astype(jnp.float32)]
    pallas_call x1, Pallas kernels: 14.1 us -> 12.8 us  [body(): pl.pallas_call(lambda *refs: grid_kernel(pairs, capacity, *refs), out_sha...]
    all_gather x1, blocking collectives: 6.44 us -> 5.64 us  [body(): lax.all_gather(grid_sum.astype(jnp.bfloat16)[None], 'freq', axis=0, tiled...]
  transfers between devices with their start and end apart: 3 -> 4, of which waited for: 1 -> 3; matrix products, arithmetic and copies ran while one was open for 0% -> 0% of each run, Pallas kernels for 0% -> 7%
where the time goes in v14:
time: 53.1 us; the launch traced here: 52.7 us
  Pallas kernels  18.1 us (34%)
  starting transfers between devices  13.9 us (26%)
  waiting for transfers between devices  12.8 us (24%)
  blocking collectives  5.64 us (11%)
  local copies, waits for them, and re-layouts  1.43 us (3%)
  between operations  0.75 us (1%)
    pallas_call x1, Pallas kernels, body(): pl.pallas_call(lambda *refs: grid_kernel(pairs, capacity, *refs), out_sha...  12.8 us
    all_to_all x1, waiting for transfers between devices, body(): lax.all_to_all(sent, 'tile', split_axis=0, concat_axis=0, tiled=True, axi...  8.28 us
    all_gather x1, blocking collectives, body(): lax.all_gather(grid_sum.astype(jnp.bfloat16)[None], 'freq', axis=0, tiled...  5.64 us
    ppermute x1, starting transfers between devices, body(): model_other = lax.ppermute(model_own, 'tile', swap)  4.1 us
    pallas_call x1, Pallas kernels, body(): pl.pallas_call(lambda *refs: pack_kernel(pairs, capacity, tiles_here, pla...  3.69 us
    all_to_all x1, starting transfers between devices, body(): lax.all_to_all(sent, 'tile', split_axis=0, concat_axis=0, tiled=True, axi...  3.54 us
    all_to_all x1, starting transfers between devices, body(): lax.all_to_all(residual, 'tile', split_axis=0, concat_axis=0, tiled=True,...  3.39 us
    ppermute x1, starting transfers between devices, body(): grid_sum = own + lax.ppermute(other, 'tile', swap).astype(jnp.float32)  2.89 us
  transfers between devices with their start and end apart: 4, of which 3 were waited for; matrix products, arithmetic and copies ran while one was open for 0% of the time, Pallas kernels for 7%

profile of v14, /device:TPU:0, one launch (start us, length us, event | category | flops | bytes accessed | tf_op | source)
XLA Modules:
  0.0 52.7 jit_solution(1195836158789519115)
XLA Ops:
  0.6 0.0 copy-start
  0.6 4.1 %collective-permute-start = (bf16[2,128,256]{2,1,0:T(8,128)(2,1)}, bf16[2,128,256]{2,1,0:T(8,128)(2,1)S(1)}, u32[]{:S(2)}, u32[]{:S(2)}) collective-permute-start(bf16[2,128,256]{2,1,0:T(8,128)(2,1)} %bitcast.23), channel_id=1, source_target_pairs={{0,16},{2,18},{4,20},{6,22},{8,24},{10,26},{12,28},{14,30},{16,0},... | collective-permute-start | bytes 393224 | tf_op jit(solution)/shard_map/ppermute | solution.py:303
  4.7 3.7 %pack_blocks.1 = (s32[1216,128]{1,0:T(8,128)}, s32[128]{0:T(128)}) custom-call(s32[128]{0:T(128)} %bitcast.25, s32[128]{0:T(128)} %bitcast.26, f32[128,2,128]{2,1,0:T(2,128)} %bitcast.20, s32[128,2,128]{2,1,0:T(2,128)} %bitcast.21, s32[128,2,128]{2,1,0:T(2,128)} %bitcast.22), custom_call_target="tpu_custom_call" | custom-call | tf_op jit(solution)/shard_map/pack_blocks/pallas_call | solution.py:304
  8.4 2.8 %collective-permute-done = bf16[2,128,256]{2,1,0:T(8,128)(2,1)S(1)} collective-permute-done((bf16[2,128,256]{2,1,0:T(8,128)(2,1)}, bf16[2,128,256]{2,1,0:T(8,128)(2,1)S(1)}, u32[]{:S(2)}, u32[]{:S(2)}) %collective-permute-start) | collective-permute-done | bytes 131104 | tf_op jit(solution)/shard_map/ppermute | solution.py:303
  11.3 3.5 %all-to-all-start = ((s32[8,152,128]{2,1,0:T(8,128)}), s32[8,152,128]{2,1,0:T(8,128)S(1)}, u32[]{:S(2)}, u32[]{:S(2)}) async-start(s32[8,152,128]{2,1,0:T(8,128)} %bitcast.19), calls=%async_computation | async-start | bytes 1245184 | tf_op jit(solution)/shard_map/all_to_all | solution.py:328
  14.8 0.0 copy-start.2
  14.8 0.0 copy-start.1
  14.9 0.7 %copy-done.2 = bf16[16,8,8]{0,2,1:T(8,128)(2,1)S(1)} copy-done((bf16[16,8,8]{0,2,1:T(8,128)(2,1)S(1)}, bf16[16,8,8]{0,2,1:T(8,128)(2,1)}, u32[]{:S(2)}) %copy-start.2) | copy-done | bytes 2072
  15.6 0.1 copy.13.refs_2_
  15.6 0.0 copy-done
  15.7 0.0 copy-start.3
  15.7 0.6 %copy-done.3 = s32[128]{0:T(128)S(1)} copy-done((s32[128]{0:T(128)S(1)}, s32[128]{0:T(128)}, u32[]{:S(2)}) %copy-start.3) | copy-done | bytes 536
  16.3 0.0 copy-done.1
  16.4 8.3 %all-to-all-done = s32[8,152,128]{2,1,0:T(8,128)S(1)} async-done(((s32[8,152,128]{2,1,0:T(8,128)}), s32[8,152,128]{2,1,0:T(8,128)S(1)}, u32[]{:S(2)}, u32[]{:S(2)}) %all-to-all-start) | async-done | bytes 622624 | tf_op jit(solution)/shard_map/all_to_all | solution.py:328
  24.6 12.8 %grid_blocks.1 = (bf16[392,2,128]{2,1,0:T(2,128)(2,1)}, f32[2,256,128]{2,1,0:T(8,128)S(1)}, bf16[2,256,128]{2,1,0:T(8,128)(2,1)S(1)}) custom-call(s32[1]{0:T(128)} %bitcast.9.refs_0_, s32[1216,128]{1,0:T(8,128)S(1)} %bitcast.17, f32[24,128]{1,0:T(8,128)S(1)} %copy.13.refs_2_, bf16[4,128,256]{2,1,0:T(8,128)(2,1)S(1)} %maximum_select_fusion.refs_3_), custom_call_target="tpu_custom_call" | custom-call | tf_op jit(solution)/shard_map/grid_blocks/pallas_call | solution.py:343
  37.4 2.9 %collective-permute-start.1 = (bf16[2,256,128]{2,1,0:T(8,128)(2,1)S(1)}, bf16[2,256,128]{2,1,0:T(8,128)(2,1)S(1)}, u32[]{:S(2)}, u32[]{:S(2)}) collective-permute-start(bf16[2,256,128]{2,1,0:T(8,128)(2,1)S(1)} %get-tuple-element.23), channel_id=1, source_target_pairs={{0,16},{2,18},{4,20},{6,22},{8,24},{10,26},{12,28},{14,30},{16,0},... | collective-permute-start | bytes 393224 | tf_op jit(solution)/shard_map/ppermute | solution.py:371
  40.3 3.4 %all-to-all-start.1 = ((bf16[392,2,128]{2,1,0:T(2,128)(2,1)}), bf16[392,2,128]{2,1,0:T(2,128)(2,1)S(1)}, u32[]{:S(2)}, u32[]{:S(2)}) async-start(bf16[392,2,128]{2,1,0:T(2,128)(2,1)} %get-tuple-element.21), calls=%async_computation.1 | async-start | bytes 401408 | tf_op jit(solution)/shard_map/all_to_all | solution.py:368
  43.7 1.7 %collective-permute-done.1 = bf16[2,256,128]{2,1,0:T(8,128)(2,1)S(1)} collective-permute-done((bf16[2,256,128]{2,1,0:T(8,128)(2,1)S(1)}, bf16[2,256,128]{2,1,0:T(8,128)(2,1)S(1)}, u32[]{:S(2)}, u32[]{:S(2)}) %collective-permute-start.1) | collective-permute-done | bytes 131104 | tf_op jit(solution)/shard_map/ppermute | solution.py:371
  45.4 5.6 %all-gather = bf16[4,256,128]{2,1,0:T(8,128)(2,1)S(1)} all-gather(bf16[2,256,128]{2,1,0:T(8,128)(2,1)S(1)} %add_convert_fusion), channel_id=2, replica_groups=mesh['tile'=16,'freq'=2] {'freq'}, dimensions={0}, use_global_device_ids=true | all-gather | bytes 393216 | tf_op jit(solution)/shard_map/all_gather | solution.py:372
  51.1 0.0 all-to-all-done.1.returned_ref
  51.1 1.6 %finish.1 = (f32[128,2,128]{2,1,0:T(2,128)}, f32[2,128,256]{2,1,0:T(8,128)}) custom-call(f32[2]{0:T(128)S(1)} %dynamic-slice_bitcast_fusion.row_ref, s32[128]{0:T(128)S(1)} %broadcast_add_fusion.slot_ref, bf16[392,2,128]{2,1,0:T(2,128)(2,1)S(1)} %all-to-all-done.1.returned_ref, bf16[2,2,256,128]{3,2,1,0:T(8,128)(2,1)S(1)} %bitcast.18), custom_call_target="tpu_custom_call" | custom-call | tf_op jit(solution)/shard_map/finish/pallas_call | solution.py:373
  (6 shorter events, 0.1 us)
Async XLA Ops:
  0.6 15.0 %copy-start = (f32[2,2]{1,0:T(2,128)S(1)}, f32[2,2]{1,0:T(2,128)}, u32[]{:S(2)}) copy-start(f32[2,2]{1,0:T(2,128)} %param.15) | copy-start | bytes 52
  0.6 10.6 %collective-permute-start = (bf16[2,128,256]{2,1,0:T(8,128)(2,1)}, bf16[2,128,256]{2,1,0:T(8,128)(2,1)S(1)}, u32[]{:S(2)}, u32[]{:S(2)}) collective-permute-start(bf16[2,128,256]{2,1,0:T(8,128)(2,1)} %bitcast.23), channel_id=1, source_target_pairs={{0,16},{2,18},{4,20},{6,22},{8,24},{10,26},{12,28},{14,30},{16,0},... | collective-permute-start | bytes 393224 | tf_op jit(solution)/shard_map/ppermute | solution.py:303
  11.3 13.4 %all-to-all-start = ((s32[8,152,128]{2,1,0:T(8,128)}), s32[8,152,128]{2,1,0:T(8,128)S(1)}, u32[]{:S(2)}, u32[]{:S(2)}) async-start(s32[8,152,128]{2,1,0:T(8,128)} %bitcast.19), calls=%async_computation | async-start | bytes 1245184 | tf_op jit(solution)/shard_map/all_to_all | solution.py:328
  14.8 0.7 %copy-start.2 = (bf16[16,8,8]{0,2,1:T(8,128)(2,1)S(1)}, bf16[16,8,8]{0,2,1:T(8,128)(2,1)}, u32[]{:S(2)}) copy-start(bf16[16,8,8]{0,2,1:T(8,128)(2,1)} %param.14) | copy-start | bytes 6148
  14.8 1.5 %copy-start.1 = (bf16[1,2,128,256]{3,2,1,0:T(8,128)(2,1)S(1)}, bf16[1,2,128,256]{3,2,1,0:T(8,128)(2,1)}, u32[]{:S(2)}) copy-start(bf16[1,2,128,256]{3,2,1,0:T(8,128)(2,1)} %param.13) | copy-start | bytes 393220
  15.7 0.7 %copy-start.3 = (s32[128]{0:T(128)S(1)}, s32[128]{0:T(128)}, u32[]{:S(2)}) copy-start(s32[128]{0:T(128)} %get-tuple-element.14) | copy-start | bytes 1540
  37.4 7.9 %collective-permute-start.1 = (bf16[2,256,128]{2,1,0:T(8,128)(2,1)S(1)}, bf16[2,256,128]{2,1,0:T(8,128)(2,1)S(1)}, u32[]{:S(2)}, u32[]{:S(2)}) collective-permute-start(bf16[2,256,128]{2,1,0:T(8,128)(2,1)S(1)} %get-tuple-element.23), channel_id=1, source_target_pairs={{0,16},{2,18},{4,20},{6,22},{8,24},{10,26},{12,28},{14,30},{16,0},... | collective-permute-start | bytes 393224 | tf_op jit(solution)/shard_map/ppermute | solution.py:371
  40.3 10.7 %all-to-all-start.1 = ((bf16[392,2,128]{2,1,0:T(2,128)(2,1)}), bf16[392,2,128]{2,1,0:T(2,128)(2,1)S(1)}, u32[]{:S(2)}, u32[]{:S(2)}) async-start(bf16[392,2,128]{2,1,0:T(2,128)(2,1)} %get-tuple-element.21), calls=%async_computation.1 | async-start | bytes 401408 | tf_op jit(solution)/shard_map/all_to_all | solution.py:368

commit v15 on v13

--- a/solution.py
+++ b/solution.py
@@ -6,8 +6,9 @@
 from jax.sharding import PartitionSpec as P
 
 UNROLL = 2
-CHUNKS = 8
+CHUNKS = 35
 AHEAD = 2
+BUFFERS = 5
 VMEM = pl.BlockSpec(memory_space=pltpu.VMEM)
 SMEM = pl.BlockSpec(memory_space=pltpu.SMEM)
 HBM = pl.BlockSpec(memory_space=pltpu.HBM)
@@ -145,7 +146,7 @@
 
 def grid_kernel(pairs, capacity, member_ref, got_ref, table_ref, model_ref, residual_ref, own_ref,
                 other_ref, turned_ref, grid_ref, code_ref, about_ref, list_ref, sem, *buffers):
-    row_refs, picked_refs = buffers[:4], buffers[4:]
+    row_refs, picked_refs = buffers[:BUFFERS], buffers[BUFFERS:]
     tiles, side, wide = model_ref.shape
     groups = side // 16
     zero_row = table_ref.shape[0] - 8
@@ -356,8 +357,8 @@
                 (slots + capacity + (2 * tiles_here + CHUNKS + AHEAD) * UNROLL,), jnp.int32
             ),
             pltpu.SemaphoreType.DMA,
-            *[pltpu.VMEM((side, UNROLL * rows), jnp.bfloat16)] * 4,
-            *[pltpu.VMEM((2, 16, UNROLL * rows), jnp.float32)] * 4,
+            *[pltpu.VMEM((side, UNROLL * rows), jnp.bfloat16)] * BUFFERS,
+            *[pltpu.VMEM((2, 16, UNROLL * rows), jnp.float32)] * BUFFERS,
         ],
         compiler_params=PARAMS,
         name="grid_blocks",

time: 51.4 us -> 48.4 us (0.942)
  Pallas kernels: 19.6 us -> 11.1 us
  starting transfers between devices: 11.1 us -> 16.4 us
    pallas_call x1, Pallas kernels: 14.1 us -> 5.72 us  [body(): pl.pallas_call(lambda *refs: grid_kernel(pairs, capacity, *refs), out_sha...]
    all_to_all x1, starting transfers between devices: 3.39 us -> 9.23 us  [body(): lax.all_to_all(residual, 'tile', split_axis=0, concat_axis=0, tiled=True,...]
    ppermute x1, starting transfers between devices: 2.48 us -> 1.92 us  [body(): grid_sum = own + lax.ppermute(other, 'tile', swap).astype(jnp.float32)]
where the time goes in v15:
time: 48.4 us; the launch traced here: 47.5 us
  starting transfers between devices  16.4 us (34%)
  blocking collectives  16.3 us (34%)
  Pallas kernels  11.1 us (23%)
  local copies, waits for them, and re-layouts  1.55 us (3%)
  waiting for transfers between devices  1.41 us (3%)
  between operations  0.7 us (1%)
    all_gather x1, blocking collectives, body(): lax.all_gather(model_grid[0], 'tile', axis=0, tiled=True, axis_index_grou...  9.71 us
    all_to_all x1, starting transfers between devices, body(): lax.all_to_all(residual, 'tile', split_axis=0, concat_axis=0, tiled=True,...  9.23 us
    all_gather x1, blocking collectives, body(): lax.all_gather(grid_sum.astype(jnp.bfloat16)[None], 'freq', axis=0, tiled...  6.58 us
    pallas_call x1, Pallas kernels, body(): pl.pallas_call(lambda *refs: grid_kernel(pairs, capacity, *refs), out_sha...  5.72 us
    all_to_all x1, starting transfers between devices, body(): lax.all_to_all(sent, 'tile', split_axis=0, concat_axis=0, tiled=True, axi...  5.27 us
    pallas_call x1, Pallas kernels, body(): pl.pallas_call(lambda *refs: pack_kernel(pairs, capacity, tiles_here, pla...  3.81 us
    ppermute x1, starting transfers between devices, body(): grid_sum = own + lax.ppermute(other, 'tile', swap).astype(jnp.float32)  1.92 us
    pallas_call x1, Pallas kernels, body(): pl.pallas_call(finish_kernel, out_shape=(jax.ShapeDtypeStruct((blocks, 2,...  1.6 us
  transfers between devices with their start and end apart: 3, of which 1 were waited for; matrix products, arithmetic and copies ran while one was open for 0% of the time, Pallas kernels for 0%

profile of v15, /device:TPU:0, one launch (start us, length us, event | category | flops | bytes accessed | tf_op | source)
XLA Modules:
  0.0 47.5 jit_solution(11935880280293494012)
XLA Ops:
  0.6 0.0 copy-start
  0.6 3.8 %pack_blocks.1 = (s32[1216,128]{1,0:T(8,128)}, s32[128]{0:T(128)}) custom-call(s32[128]{0:T(128)} %bitcast.26, s32[128]{0:T(128)} %bitcast.27, f32[128,2,128]{2,1,0:T(2,128)} %bitcast.22, s32[128,2,128]{2,1,0:T(2,128)} %bitcast.23, s32[128,2,128]{2,1,0:T(2,128)} %bitcast.24), custom_call_target="tpu_custom_call" | custom-call | tf_op jit(solution)/shard_map/pack_blocks/pallas_call | solution.py:309
  4.5 5.3 %all-to-all-start = ((s32[8,152,128]{2,1,0:T(8,128)}), s32[8,152,128]{2,1,0:T(8,128)S(1)}, u32[]{:S(2)}, u32[]{:S(2)}) async-start(s32[8,152,128]{2,1,0:T(8,128)} %bitcast.21), calls=%async_computation | async-start | bytes 1245184 | tf_op jit(solution)/shard_map/all_to_all | solution.py:332
  9.7 0.0 copy-start.2
  9.7 0.0 copy-start.1
  9.8 0.7 %copy-done.2 = bf16[16,8,8]{0,2,1:T(8,128)(2,1)S(1)} copy-done((bf16[16,8,8]{0,2,1:T(8,128)(2,1)S(1)}, bf16[16,8,8]{0,2,1:T(8,128)(2,1)}, u32[]{:S(2)}) %copy-start.2) | copy-done | bytes 2072
  10.5 0.1 copy.14.refs_2_
  10.5 0.1 copy-done.1
  10.7 9.7 %all-gather = bf16[1,4,128,256]{3,2,0,1:T(8,128)(2,1)S(1)} all-gather(bf16[1,2,128,256]{3,2,0,1:T(8,128)(2,1)S(1)} %bitcast.25), channel_id=2, replica_groups={{0,16},{2,18},{4,20},{6,22},{8,24},{10,26},{12,28},{14,30},{1,17},{3,19..., dimensions={1}, use_global_device_ids=true | all-gather | bytes 393216 | tf_op jit(solution)/shard_map/all_gather | solution.py:302
  20.4 0.0 copy-done
  20.4 0.0 copy-start.3
  20.4 0.6 %copy-done.3 = s32[128]{0:T(128)S(1)} copy-done((s32[128]{0:T(128)S(1)}, s32[128]{0:T(128)}, u32[]{:S(2)}) %copy-start.3) | copy-done | bytes 536
  21.0 1.4 %all-to-all-done = s32[8,152,128]{2,1,0:T(8,128)S(1)} async-done(((s32[8,152,128]{2,1,0:T(8,128)}), s32[8,152,128]{2,1,0:T(8,128)S(1)}, u32[]{:S(2)}, u32[]{:S(2)}) %all-to-all-start) | async-done | bytes 622624 | tf_op jit(solution)/shard_map/all_to_all | solution.py:332
  22.4 5.7 %grid_blocks.1 = (bf16[392,2,128]{2,1,0:T(2,128)(2,1)}, f32[2,256,128]{2,1,0:T(8,128)S(1)}, bf16[2,256,128]{2,1,0:T(8,128)(2,1)S(1)}) custom-call(s32[1]{0:T(128)} %bitcast.8.refs_0_, s32[1216,128]{1,0:T(8,128)S(1)} %bitcast.18, f32[24,128]{1,0:T(8,128)S(1)} %copy.14.refs_2_, bf16[4,128,256]{2,1,0:T(8,128)(2,1)S(1)} %bitcast.19), custom_call_target="tpu_custom_call" | custom-call | tf_op jit(solution)/shard_map/grid_blocks/pallas_call | solution.py:342
  28.2 1.9 %collective-permute-start = (bf16[2,256,128]{2,1,0:T(8,128)(2,1)S(1)}, bf16[2,256,128]{2,1,0:T(8,128)(2,1)S(1)}, u32[]{:S(2)}, u32[]{:S(2)}) collective-permute-start(bf16[2,256,128]{2,1,0:T(8,128)(2,1)S(1)} %get-tuple-element.19), channel_id=1, source_target_pairs={{0,16},{2,18},{4,20},{6,22},{8,24},{10,26},{12,28},{14,30},{16,0},... | collective-permute-start | bytes 393224 | tf_op jit(solution)/shard_map/ppermute | solution.py:370
  30.1 9.2 %all-to-all-start.1 = ((bf16[392,2,128]{2,1,0:T(2,128)(2,1)}), bf16[392,2,128]{2,1,0:T(2,128)(2,1)S(1)}, u32[]{:S(2)}, u32[]{:S(2)}) async-start(bf16[392,2,128]{2,1,0:T(2,128)(2,1)} %get-tuple-element.17), calls=%async_computation.1 | async-start | bytes 401408 | tf_op jit(solution)/shard_map/all_to_all | solution.py:367
  39.3 0.0 collective-permute-done
  39.4 6.6 %all-gather.1 = bf16[4,256,128]{2,1,0:T(8,128)(2,1)S(1)} all-gather(bf16[2,256,128]{2,1,0:T(8,128)(2,1)S(1)} %add_convert_fusion), channel_id=3, replica_groups=mesh['tile'=16,'freq'=2] {'freq'}, dimensions={0}, use_global_device_ids=true | all-gather | bytes 393216 | tf_op jit(solution)/shard_map/all_gather | solution.py:371
  45.9 0.0 all-to-all-done.1.returned_ref
  45.9 1.6 %finish.1 = (f32[128,2,128]{2,1,0:T(2,128)}, f32[2,128,256]{2,1,0:T(8,128)}) custom-call(f32[2]{0:T(128)S(1)} %dynamic-slice_bitcast_fusion.row_ref, s32[128]{0:T(128)S(1)} %broadcast_add_fusion.slot_ref, bf16[392,2,128]{2,1,0:T(2,128)(2,1)S(1)} %all-to-all-done.1.returned_ref, bf16[2,2,256,128]{3,2,1,0:T(8,128)(2,1)S(1)} %bitcast.20), custom_call_target="tpu_custom_call" | custom-call | tf_op jit(solution)/shard_map/finish/pallas_call | solution.py:372
  (5 shorter events, 0.1 us)
Async XLA Ops:
  0.6 19.7 %copy-start = (f32[2,2]{1,0:T(2,128)S(1)}, f32[2,2]{1,0:T(2,128)}, u32[]{:S(2)}) copy-start(f32[2,2]{1,0:T(2,128)} %param.15) | copy-start | bytes 52
  4.5 18.0 %all-to-all-start = ((s32[8,152,128]{2,1,0:T(8,128)}), s32[8,152,128]{2,1,0:T(8,128)S(1)}, u32[]{:S(2)}, u32[]{:S(2)}) async-start(s32[8,152,128]{2,1,0:T(8,128)} %bitcast.21), calls=%async_computation | async-start | bytes 1245184 | tf_op jit(solution)/shard_map/all_to_all | solution.py:332
  9.7 0.7 %copy-start.2 = (bf16[16,8,8]{0,2,1:T(8,128)(2,1)S(1)}, bf16[16,8,8]{0,2,1:T(8,128)(2,1)}, u32[]{:S(2)}) copy-start(bf16[16,8,8]{0,2,1:T(8,128)(2,1)} %param.14) | copy-start | bytes 6148
  9.7 0.9 %copy-start.1 = (bf16[1,2,128,256]{3,2,1,0:T(8,128)(2,1)S(1)}, bf16[1,2,128,256]{3,2,1,0:T(8,128)(2,1)}, u32[]{:S(2)}) copy-start(bf16[1,2,128,256]{3,2,1,0:T(8,128)(2,1)} %param.13) | copy-start | bytes 393220
  20.4 0.7 %copy-start.3 = (s32[128]{0:T(128)S(1)}, s32[128]{0:T(128)}, u32[]{:S(2)}) copy-start(s32[128]{0:T(128)} %get-tuple-element.12) | copy-start | bytes 1540
  28.2 11.2 %collective-permute-start = (bf16[2,256,128]{2,1,0:T(8,128)(2,1)S(1)}, bf16[2,256,128]{2,1,0:T(8,128)(2,1)S(1)}, u32[]{:S(2)}, u32[]{:S(2)}) collective-permute-start(bf16[2,256,128]{2,1,0:T(8,128)(2,1)S(1)} %get-tuple-element.19), channel_id=1, source_target_pairs={{0,16},{2,18},{4,20},{6,22},{8,24},{10,26},{12,28},{14,30},{16,0},... | collective-permute-start | bytes 393224 | tf_op jit(solution)/shard_map/ppermute | solution.py:370
  30.1 15.9 %all-to-all-start.1 = ((bf16[392,2,128]{2,1,0:T(2,128)(2,1)}), bf16[392,2,128]{2,1,0:T(2,128)(2,1)S(1)}, u32[]{:S(2)}, u32[]{:S(2)}) async-start(bf16[392,2,128]{2,1,0:T(2,128)(2,1)} %get-tuple-element.17), calls=%async_computation.1 | async-start | bytes 401408 | tf_op jit(solution)/shard_map/all_to_all | solution.py:367

commit v16 on v15

--- a/solution.py
+++ b/solution.py
@@ -7,7 +7,7 @@
 
 UNROLL = 2
 CHUNKS = 35
-AHEAD = 2
+AHEAD = 3
 BUFFERS = 5
 VMEM = pl.BlockSpec(memory_space=pltpu.VMEM)
 SMEM = pl.BlockSpec(memory_space=pltpu.SMEM)
@@ -146,7 +146,9 @@
 
 def grid_kernel(pairs, capacity, member_ref, got_ref, table_ref, model_ref, residual_ref, own_ref,
                 other_ref, turned_ref, grid_ref, code_ref, about_ref, list_ref, sem, *buffers):
-    row_refs, picked_refs = buffers[:BUFFERS], buffers[BUFFERS:]
+    row_refs, picked_refs, taps_refs, group_refs = (
+        buffers[i * BUFFERS : (i + 1) * BUFFERS] for i in range(4)
+    )
     tiles, side, wide = model_ref.shape
     groups = side // 16
     zero_row = table_ref.shape[0] - 8
@@ -224,7 +226,8 @@
         return (list_ref[turn * UNROLL] >> TILE_SHIFT) & 15
 
     def front(turn, which):
-        row_ref, picked_ref = row_refs[which % len(row_refs)], picked_refs[which % len(picked_refs)]
+        row_ref, picked_ref = row_refs[which % BUFFERS], picked_refs[which % BUFFERS]
+        taps_ref, group_ref = taps_refs[which % BUFFERS], group_refs[which % BUFFERS]
         blocks = [read(turn * UNROLL + u) for u in range(UNROLL)]
         for u, (_, _, parts) in enumerate(blocks):
             taps, group = parts(16)
@@ -246,15 +249,17 @@
                     low = part * side + 16 * k
                     picked = jnp.where(group == k, partial[low : low + 16, columns], picked)
                 picked_ref[part, :, columns] = picked * taps
+            taps_ref[:, columns] = taps
+            group_ref[:, columns] = group.astype(jnp.float32).astype(jnp.bfloat16)
 
     def back(turn, which):
-        row_ref, picked_ref = row_refs[which % len(row_refs)], picked_refs[which % len(picked_refs)]
+        row_ref, picked_ref = row_refs[which % BUFFERS], picked_refs[which % BUFFERS]
+        taps_ref, group_ref = taps_refs[which % BUFFERS], group_refs[which % BUFFERS]
         weighted = []
         for u in range(UNROLL):
-            slot, sample, parts = read(turn * UNROLL + u)
+            slot, sample, _ = read(turn * UNROLL + u)
             columns = slice(128 * u, 128 * u + 128)
-            taps, group = parts(0)
-            group = group.astype(jnp.float32).astype(jnp.bfloat16)
+            taps, group = taps_ref[:, columns], group_ref[:, columns]
             residuals, pieces = [], []
             for part in range(2):
                 model = jnp.sum(picked_ref[part, :, columns], axis=0, keepdims=True)
@@ -359,6 +364,8 @@
             pltpu.SemaphoreType.DMA,
             *[pltpu.VMEM((side, UNROLL * rows), jnp.bfloat16)] * BUFFERS,
             *[pltpu.VMEM((2, 16, UNROLL * rows), jnp.float32)] * BUFFERS,
+            *[pltpu.VMEM((16, UNROLL * rows), jnp.float32)] * BUFFERS,
+            *[pltpu.VMEM((16, UNROLL * rows), jnp.bfloat16)] * BUFFERS,
         ],
         compiler_params=PARAMS,
         name="grid_blocks",

time: 48.4 us -> 49.5 us (1.023)
  Pallas kernels: 11.1 us -> 18.3 us
  starting transfers between devices: 16.4 us -> 10.8 us
    pallas_call x1, Pallas kernels: 5.72 us -> 12.8 us  [body(): pl.pallas_call(lambda *refs: grid_kernel(pairs, capacity, *refs), out_sha...]
    all_to_all x1, starting transfers between devices: 9.23 us -> 3.49 us  [body(): lax.all_to_all(residual, 'tile', split_axis=0, concat_axis=0, tiled=True,...]
  transfers between devices with their start and end apart: 3 -> 3, of which waited for: 1 -> 2; matrix products, arithmetic and copies ran while one was open for 0% -> 0% of each run, Pallas kernels for 0% -> 0%
where the time goes in v16:
time: 49.5 us; the launch traced here: 49.1 us
  Pallas kernels  18.3 us (37%)
  blocking collectives  15.9 us (32%)
  starting transfers between devices  10.8 us (22%)
  waiting for transfers between devices  1.78 us (4%)
  local copies, waits for them, and re-layouts  1.55 us (3%)
  between operations  0.7 us (1%)
    pallas_call x1, Pallas kernels, body(): pl.pallas_call(lambda *refs: grid_kernel(pairs, capacity, *refs), out_sha...  12.8 us
    all_gather x1, blocking collectives, body(): lax.all_gather(model_grid[0], 'tile', axis=0, tiled=True, axis_index_grou...  9.71 us
    all_gather x1, blocking collectives, body(): lax.all_gather(grid_sum.astype(jnp.bfloat16)[None], 'freq', axis=0, tiled...  6.22 us
    all_to_all x1, starting transfers between devices, body(): lax.all_to_all(sent, 'tile', split_axis=0, concat_axis=0, tiled=True, axi...  5.27 us
    pallas_call x1, Pallas kernels, body(): pl.pallas_call(lambda *refs: pack_kernel(pairs, capacity, tiles_here, pla...  3.81 us
    all_to_all x1, starting transfers between devices, body(): lax.all_to_all(residual, 'tile', split_axis=0, concat_axis=0, tiled=True,...  3.49 us
    ppermute x1, starting transfers between devices, body(): grid_sum = own + lax.ppermute(other, 'tile', swap).astype(jnp.float32)  2.07 us
    pallas_call x1, Pallas kernels, body(): pl.pallas_call(finish_kernel, out_shape=(jax.ShapeDtypeStruct((blocks, 2,...  1.6 us
  transfers between devices with their start and end apart: 3, of which 2 were waited for; matrix products, arithmetic and copies ran while one was open for 0% of the time, Pallas kernels for 0%

profile of v16, /device:TPU:0, one launch (start us, length us, event | category | flops | bytes accessed | tf_op | source)
XLA Modules:
  0.0 49.1 jit_solution(17081312651444691311)
XLA Ops:
  0.6 0.0 copy-start
  0.6 3.8 %pack_blocks.1 = (s32[1216,128]{1,0:T(8,128)}, s32[128]{0:T(128)}) custom-call(s32[128]{0:T(128)} %bitcast.26, s32[128]{0:T(128)} %bitcast.27, f32[128,2,128]{2,1,0:T(2,128)} %bitcast.22, s32[128,2,128]{2,1,0:T(2,128)} %bitcast.23, s32[128,2,128]{2,1,0:T(2,128)} %bitcast.24), custom_call_target="tpu_custom_call" | custom-call | tf_op jit(solution)/shard_map/pack_blocks/pallas_call | solution.py:314
  4.5 5.3 %all-to-all-start = ((s32[8,152,128]{2,1,0:T(8,128)}), s32[8,152,128]{2,1,0:T(8,128)S(1)}, u32[]{:S(2)}, u32[]{:S(2)}) async-start(s32[8,152,128]{2,1,0:T(8,128)} %bitcast.21), calls=%async_computation | async-start | bytes 1245184 | tf_op jit(solution)/shard_map/all_to_all | solution.py:337
  9.7 0.0 copy-start.2
  9.7 0.0 copy-start.1
  9.8 0.7 %copy-done.2 = bf16[16,8,8]{0,2,1:T(8,128)(2,1)S(1)} copy-done((bf16[16,8,8]{0,2,1:T(8,128)(2,1)S(1)}, bf16[16,8,8]{0,2,1:T(8,128)(2,1)}, u32[]{:S(2)}) %copy-start.2) | copy-done | bytes 2072
  10.5 0.1 copy.14.refs_2_
  10.5 0.1 copy-done.1
  10.7 9.7 %all-gather = bf16[1,4,128,256]{3,2,0,1:T(8,128)(2,1)S(1)} all-gather(bf16[1,2,128,256]{3,2,0,1:T(8,128)(2,1)S(1)} %bitcast.25), channel_id=2, replica_groups={{0,16},{2,18},{4,20},{6,22},{8,24},{10,26},{12,28},{14,30},{1,17},{3,19..., dimensions={1}, use_global_device_ids=true | all-gather | bytes 393216 | tf_op jit(solution)/shard_map/all_gather | solution.py:307
  20.4 0.0 copy-done
  20.4 0.0 copy-start.3
  20.4 0.6 %copy-done.3 = s32[128]{0:T(128)S(1)} copy-done((s32[128]{0:T(128)S(1)}, s32[128]{0:T(128)}, u32[]{:S(2)}) %copy-start.3) | copy-done | bytes 536
  21.0 1.4 %all-to-all-done = s32[8,152,128]{2,1,0:T(8,128)S(1)} async-done(((s32[8,152,128]{2,1,0:T(8,128)}), s32[8,152,128]{2,1,0:T(8,128)S(1)}, u32[]{:S(2)}, u32[]{:S(2)}) %all-to-all-start) | async-done | bytes 622624 | tf_op jit(solution)/shard_map/all_to_all | solution.py:337
  22.4 12.8 %grid_blocks.1 = (bf16[392,2,128]{2,1,0:T(2,128)(2,1)}, f32[2,256,128]{2,1,0:T(8,128)S(1)}, bf16[2,256,128]{2,1,0:T(8,128)(2,1)S(1)}) custom-call(s32[1]{0:T(128)} %bitcast.8.refs_0_, s32[1216,128]{1,0:T(8,128)S(1)} %bitcast.18, f32[24,128]{1,0:T(8,128)S(1)} %copy.14.refs_2_, bf16[4,128,256]{2,1,0:T(8,128)(2,1)S(1)} %bitcast.19), custom_call_target="tpu_custom_call" | custom-call | tf_op jit(solution)/shard_map/grid_blocks/pallas_call | solution.py:347
  35.3 2.1 %collective-permute-start = (bf16[2,256,128]{2,1,0:T(8,128)(2,1)S(1)}, bf16[2,256,128]{2,1,0:T(8,128)(2,1)S(1)}, u32[]{:S(2)}, u32[]{:S(2)}) collective-permute-start(bf16[2,256,128]{2,1,0:T(8,128)(2,1)S(1)} %get-tuple-element.19), channel_id=1, source_target_pairs={{0,16},{2,18},{4,20},{6,22},{8,24},{10,26},{12,28},{14,30},{16,0},... | collective-permute-start | bytes 393224 | tf_op jit(solution)/shard_map/ppermute | solution.py:377
  37.4 3.5 %all-to-all-start.1 = ((bf16[392,2,128]{2,1,0:T(2,128)(2,1)}), bf16[392,2,128]{2,1,0:T(2,128)(2,1)S(1)}, u32[]{:S(2)}, u32[]{:S(2)}) async-start(bf16[392,2,128]{2,1,0:T(2,128)(2,1)} %get-tuple-element.17), calls=%async_computation.1 | async-start | bytes 401408 | tf_op jit(solution)/shard_map/all_to_all | solution.py:374
  40.9 0.4 collective-permute-done
  41.3 6.2 %all-gather.1 = bf16[4,256,128]{2,1,0:T(8,128)(2,1)S(1)} all-gather(bf16[2,256,128]{2,1,0:T(8,128)(2,1)S(1)} %add_convert_fusion), channel_id=3, replica_groups=mesh['tile'=16,'freq'=2] {'freq'}, dimensions={0}, use_global_device_ids=true | all-gather | bytes 393216 | tf_op jit(solution)/shard_map/all_gather | solution.py:378
  47.5 0.0 all-to-all-done.1.returned_ref
  47.5 1.6 %finish.1 = (f32[128,2,128]{2,1,0:T(2,128)}, f32[2,128,256]{2,1,0:T(8,128)}) custom-call(f32[2]{0:T(128)S(1)} %dynamic-slice_bitcast_fusion.row_ref, s32[128]{0:T(128)S(1)} %broadcast_add_fusion.slot_ref, bf16[392,2,128]{2,1,0:T(2,128)(2,1)S(1)} %all-to-all-done.1.returned_ref, bf16[2,2,256,128]{3,2,1,0:T(8,128)(2,1)S(1)} %bitcast.20), custom_call_target="tpu_custom_call" | custom-call | tf_op jit(solution)/shard_map/finish/pallas_call | solution.py:379
  (5 shorter events, 0.1 us)
Async XLA Ops:
  0.6 19.7 %copy-start = (f32[2,2]{1,0:T(2,128)S(1)}, f32[2,2]{1,0:T(2,128)}, u32[]{:S(2)}) copy-start(f32[2,2]{1,0:T(2,128)} %param.15) | copy-start | bytes 52
  4.5 18.0 %all-to-all-start = ((s32[8,152,128]{2,1,0:T(8,128)}), s32[8,152,128]{2,1,0:T(8,128)S(1)}, u32[]{:S(2)}, u32[]{:S(2)}) async-start(s32[8,152,128]{2,1,0:T(8,128)} %bitcast.21), calls=%async_computation | async-start | bytes 1245184 | tf_op jit(solution)/shard_map/all_to_all | solution.py:337
  9.7 0.7 %copy-start.2 = (bf16[16,8,8]{0,2,1:T(8,128)(2,1)S(1)}, bf16[16,8,8]{0,2,1:T(8,128)(2,1)}, u32[]{:S(2)}) copy-start(bf16[16,8,8]{0,2,1:T(8,128)(2,1)} %param.14) | copy-start | bytes 6148
  9.7 0.9 %copy-start.1 = (bf16[1,2,128,256]{3,2,1,0:T(8,128)(2,1)S(1)}, bf16[1,2,128,256]{3,2,1,0:T(8,128)(2,1)}, u32[]{:S(2)}) copy-start(bf16[1,2,128,256]{3,2,1,0:T(8,128)(2,1)} %param.13) | copy-start | bytes 393220
  20.4 0.7 %copy-start.3 = (s32[128]{0:T(128)S(1)}, s32[128]{0:T(128)}, u32[]{:S(2)}) copy-start(s32[128]{0:T(128)} %get-tuple-element.12) | copy-start | bytes 1540
  35.3 5.9 %collective-permute-start = (bf16[2,256,128]{2,1,0:T(8,128)(2,1)S(1)}, bf16[2,256,128]{2,1,0:T(8,128)(2,1)S(1)}, u32[]{:S(2)}, u32[]{:S(2)}) collective-permute-start(bf16[2,256,128]{2,1,0:T(8,128)(2,1)S(1)} %get-tuple-element.19), channel_id=1, source_target_pairs={{0,16},{2,18},{4,20},{6,22},{8,24},{10,26},{12,28},{14,30},{16,0},... | collective-permute-start | bytes 393224 | tf_op jit(solution)/shard_map/ppermute | solution.py:377
  37.4 10.1 %all-to-all-start.1 = ((bf16[392,2,128]{2,1,0:T(2,128)(2,1)}), bf16[392,2,128]{2,1,0:T(2,128)(2,1)S(1)}, u32[]{:S(2)}, u32[]{:S(2)}) async-start(bf16[392,2,128]{2,1,0:T(2,128)(2,1)} %get-tuple-element.17), calls=%async_computation.1 | async-start | bytes 401408 | tf_op jit(solution)/shard_map/all_to_all | solution.py:374

commit v17 on v15

--- a/solution.py
+++ b/solution.py
@@ -5,10 +5,10 @@
 from jax.experimental.pallas import tpu as pltpu
 from jax.sharding import PartitionSpec as P
 
-UNROLL = 2
-CHUNKS = 35
-AHEAD = 2
-BUFFERS = 5
+UNROLL = 4
+CHUNKS = 18
+AHEAD = 1
+BUFFERS = 6
 VMEM = pl.BlockSpec(memory_space=pltpu.VMEM)
 SMEM = pl.BlockSpec(memory_space=pltpu.SMEM)
 HBM = pl.BlockSpec(memory_space=pltpu.HBM)

time: 48.4 us -> 49.1 us (1.014)
  Pallas kernels: 11.1 us -> 11.6 us
where the time goes in v17:
time: 49.1 us; the launch traced here: 48.5 us
  starting transfers between devices  16.8 us (34%)
  blocking collectives  16.4 us (33%)
  Pallas kernels  11.6 us (24%)
  local copies, waits for them, and re-layouts  1.55 us (3%)
  waiting for transfers between devices  1.41 us (3%)
  between operations  0.7 us (1%)
    all_gather x1, blocking collectives, body(): lax.all_gather(model_grid[0], 'tile', axis=0, tiled=True, axis_index_grou...  9.71 us
    all_to_all x1, starting transfers between devices, body(): lax.all_to_all(residual, 'tile', split_axis=0, concat_axis=0, tiled=True,...  9.46 us
    all_gather x1, blocking collectives, body(): lax.all_gather(grid_sum.astype(jnp.bfloat16)[None], 'freq', axis=0, tiled...  6.66 us
    pallas_call x1, Pallas kernels, body(): pl.pallas_call(lambda *refs: grid_kernel(pairs, capacity, *refs), out_sha...  6.16 us
    all_to_all x1, starting transfers between devices, body(): lax.all_to_all(sent, 'tile', split_axis=0, concat_axis=0, tiled=True, axi...  5.27 us
    pallas_call x1, Pallas kernels, body(): pl.pallas_call(lambda *refs: pack_kernel(pairs, capacity, tiles_here, pla...  3.81 us
    ppermute x1, starting transfers between devices, body(): grid_sum = own + lax.ppermute(other, 'tile', swap).astype(jnp.float32)  2.08 us
    pallas_call x1, Pallas kernels, body(): pl.pallas_call(finish_kernel, out_shape=(jax.ShapeDtypeStruct((blocks, 2,...  1.6 us
  transfers between devices with their start and end apart: 3, of which 1 were waited for; matrix products, arithmetic and copies ran while one was open for 0% of the time, Pallas kernels for 0%

profile of v17, /device:TPU:0, one launch (start us, length us, event | category | flops | bytes accessed | tf_op | source)
XLA Modules:
  0.0 48.5 jit_solution(12896889824693252882)
XLA Ops:
  0.6 0.0 copy-start
  0.6 3.8 %pack_blocks.1 = (s32[1216,128]{1,0:T(8,128)}, s32[128]{0:T(128)}) custom-call(s32[128]{0:T(128)} %bitcast.26, s32[128]{0:T(128)} %bitcast.27, f32[128,2,128]{2,1,0:T(2,128)} %bitcast.22, s32[128,2,128]{2,1,0:T(2,128)} %bitcast.23, s32[128,2,128]{2,1,0:T(2,128)} %bitcast.24), custom_call_target="tpu_custom_call" | custom-call | tf_op jit(solution)/shard_map/pack_blocks/pallas_call | solution.py:309
  4.5 5.3 %all-to-all-start = ((s32[8,152,128]{2,1,0:T(8,128)}), s32[8,152,128]{2,1,0:T(8,128)S(1)}, u32[]{:S(2)}, u32[]{:S(2)}) async-start(s32[8,152,128]{2,1,0:T(8,128)} %bitcast.21), calls=%async_computation | async-start | bytes 1245184 | tf_op jit(solution)/shard_map/all_to_all | solution.py:332
  9.7 0.0 copy-start.2
  9.7 0.0 copy-start.1
  9.8 0.7 %copy-done.2 = bf16[16,8,8]{0,2,1:T(8,128)(2,1)S(1)} copy-done((bf16[16,8,8]{0,2,1:T(8,128)(2,1)S(1)}, bf16[16,8,8]{0,2,1:T(8,128)(2,1)}, u32[]{:S(2)}) %copy-start.2) | copy-done | bytes 2072
  10.5 0.1 copy.14.refs_2_
  10.5 0.1 copy-done.1
  10.7 9.7 %all-gather = bf16[1,4,128,256]{3,2,0,1:T(8,128)(2,1)S(1)} all-gather(bf16[1,2,128,256]{3,2,0,1:T(8,128)(2,1)S(1)} %bitcast.25), channel_id=2, replica_groups={{0,16},{2,18},{4,20},{6,22},{8,24},{10,26},{12,28},{14,30},{1,17},{3,19..., dimensions={1}, use_global_device_ids=true | all-gather | bytes 393216 | tf_op jit(solution)/shard_map/all_gather | solution.py:302
  20.4 0.0 copy-done
  20.4 0.0 copy-start.3
  20.4 0.6 %copy-done.3 = s32[128]{0:T(128)S(1)} copy-done((s32[128]{0:T(128)S(1)}, s32[128]{0:T(128)}, u32[]{:S(2)}) %copy-start.3) | copy-done | bytes 536
  21.0 1.4 %all-to-all-done = s32[8,152,128]{2,1,0:T(8,128)S(1)} async-done(((s32[8,152,128]{2,1,0:T(8,128)}), s32[8,152,128]{2,1,0:T(8,128)S(1)}, u32[]{:S(2)}, u32[]{:S(2)}) %all-to-all-start) | async-done | bytes 622624 | tf_op jit(solution)/shard_map/all_to_all | solution.py:332
  22.4 6.2 %grid_blocks.1 = (bf16[392,2,128]{2,1,0:T(2,128)(2,1)}, f32[2,256,128]{2,1,0:T(8,128)S(1)}, bf16[2,256,128]{2,1,0:T(8,128)(2,1)S(1)}) custom-call(s32[1]{0:T(128)} %bitcast.8.refs_0_, s32[1216,128]{1,0:T(8,128)S(1)} %bitcast.18, f32[24,128]{1,0:T(8,128)S(1)} %copy.14.refs_2_, bf16[4,128,256]{2,1,0:T(8,128)(2,1)S(1)} %bitcast.19), custom_call_target="tpu_custom_call" | custom-call | tf_op jit(solution)/shard_map/grid_blocks/pallas_call | solution.py:342
  28.6 2.1 %collective-permute-start = (bf16[2,256,128]{2,1,0:T(8,128)(2,1)S(1)}, bf16[2,256,128]{2,1,0:T(8,128)(2,1)S(1)}, u32[]{:S(2)}, u32[]{:S(2)}) collective-permute-start(bf16[2,256,128]{2,1,0:T(8,128)(2,1)S(1)} %get-tuple-element.19), channel_id=1, source_target_pairs={{0,16},{2,18},{4,20},{6,22},{8,24},{10,26},{12,28},{14,30},{16,0},... | collective-permute-start | bytes 393224 | tf_op jit(solution)/shard_map/ppermute | solution.py:370
  30.7 9.5 %all-to-all-start.1 = ((bf16[392,2,128]{2,1,0:T(2,128)(2,1)}), bf16[392,2,128]{2,1,0:T(2,128)(2,1)S(1)}, u32[]{:S(2)}, u32[]{:S(2)}) async-start(bf16[392,2,128]{2,1,0:T(2,128)(2,1)} %get-tuple-element.17), calls=%async_computation.1 | async-start | bytes 401408 | tf_op jit(solution)/shard_map/all_to_all | solution.py:367
  40.1 0.0 collective-permute-done
  40.2 6.7 %all-gather.1 = bf16[4,256,128]{2,1,0:T(8,128)(2,1)S(1)} all-gather(bf16[2,256,128]{2,1,0:T(8,128)(2,1)S(1)} %add_convert_fusion), channel_id=3, replica_groups=mesh['tile'=16,'freq'=2] {'freq'}, dimensions={0}, use_global_device_ids=true | all-gather | bytes 393216 | tf_op jit(solution)/shard_map/all_gather | solution.py:371
  46.8 0.0 all-to-all-done.1.returned_ref
  46.9 1.6 %finish.1 = (f32[128,2,128]{2,1,0:T(2,128)}, f32[2,128,256]{2,1,0:T(8,128)}) custom-call(f32[2]{0:T(128)S(1)} %dynamic-slice_bitcast_fusion.row_ref, s32[128]{0:T(128)S(1)} %broadcast_add_fusion.slot_ref, bf16[392,2,128]{2,1,0:T(2,128)(2,1)S(1)} %all-to-all-done.1.returned_ref, bf16[2,2,256,128]{3,2,1,0:T(8,128)(2,1)S(1)} %bitcast.20), custom_call_target="tpu_custom_call" | custom-call | tf_op jit(solution)/shard_map/finish/pallas_call | solution.py:372
  (5 shorter events, 0.1 us)
Async XLA Ops:
  0.6 19.7 %copy-start = (f32[2,2]{1,0:T(2,128)S(1)}, f32[2,2]{1,0:T(2,128)}, u32[]{:S(2)}) copy-start(f32[2,2]{1,0:T(2,128)} %param.15) | copy-start | bytes 52
  4.5 18.0 %all-to-all-start = ((s32[8,152,128]{2,1,0:T(8,128)}), s32[8,152,128]{2,1,0:T(8,128)S(1)}, u32[]{:S(2)}, u32[]{:S(2)}) async-start(s32[8,152,128]{2,1,0:T(8,128)} %bitcast.21), calls=%async_computation | async-start | bytes 1245184 | tf_op jit(solution)/shard_map/all_to_all | solution.py:332
  9.7 0.7 %copy-start.2 = (bf16[16,8,8]{0,2,1:T(8,128)(2,1)S(1)}, bf16[16,8,8]{0,2,1:T(8,128)(2,1)}, u32[]{:S(2)}) copy-start(bf16[16,8,8]{0,2,1:T(8,128)(2,1)} %param.14) | copy-start | bytes 6148
  9.7 0.9 %copy-start.1 = (bf16[1,2,128,256]{3,2,1,0:T(8,128)(2,1)S(1)}, bf16[1,2,128,256]{3,2,1,0:T(8,128)(2,1)}, u32[]{:S(2)}) copy-start(bf16[1,2,128,256]{3,2,1,0:T(8,128)(2,1)} %param.13) | copy-start | bytes 393220
  20.4 0.7 %copy-start.3 = (s32[128]{0:T(128)S(1)}, s32[128]{0:T(128)}, u32[]{:S(2)}) copy-start(s32[128]{0:T(128)} %get-tuple-element.12) | copy-start | bytes 1540
  28.6 11.5 %collective-permute-start = (bf16[2,256,128]{2,1,0:T(8,128)(2,1)S(1)}, bf16[2,256,128]{2,1,0:T(8,128)(2,1)S(1)}, u32[]{:S(2)}, u32[]{:S(2)}) collective-permute-start(bf16[2,256,128]{2,1,0:T(8,128)(2,1)S(1)} %get-tuple-element.19), channel_id=1, source_target_pairs={{0,16},{2,18},{4,20},{6,22},{8,24},{10,26},{12,28},{14,30},{16,0},... | collective-permute-start | bytes 393224 | tf_op jit(solution)/shard_map/ppermute | solution.py:370
  30.7 16.2 %all-to-all-start.1 = ((bf16[392,2,128]{2,1,0:T(2,128)(2,1)}), bf16[392,2,128]{2,1,0:T(2,128)(2,1)S(1)}, u32[]{:S(2)}, u32[]{:S(2)}) async-start(bf16[392,2,128]{2,1,0:T(2,128)(2,1)} %get-tuple-element.17), calls=%async_computation.1 | async-start | bytes 401408 | tf_op jit(solution)/shard_map/all_to_all | solution.py:367

commit v18 on v15

--- a/solution.py
+++ b/solution.py
@@ -7,7 +7,7 @@
 
 UNROLL = 2
 CHUNKS = 35
-AHEAD = 2
+AHEAD = 1
 BUFFERS = 5
 VMEM = pl.BlockSpec(memory_space=pltpu.VMEM)
 SMEM = pl.BlockSpec(memory_space=pltpu.SMEM)
@@ -40,7 +40,7 @@
 
 
 def pack_kernel(pairs, capacity, tiles_here, planes, plane_hbm, tile_hbm, vis_hbm, cell_hbm, sub_hbm,
-                sent_ref, slot_ref, plane_ref, tile_ref, vis_ref, cell_ref, sub_ref, about_ref, turned_ref,
+                sent_ref, slot_ref, row_ref, plane_ref, tile_ref, vis_ref, cell_ref, sub_ref, about_ref, turned_ref,
                 count_ref, load_sem, about_sem):
     blocks = tile_ref.shape[0]
     stride = rows_per_source(capacity)
@@ -75,6 +75,7 @@
         count_ref[key] = rank + 1
         place = first_slot(local, rank, capacity)
         slot_ref[b] = pair * (capacity + 1) + place
+        row_ref[b] = pair * stride + 3 * place
         about_ref[pair, 0, place] = plane_ref[b] << PLANE_SHIFT
 
     def each(work):
@@ -98,8 +99,7 @@
     inverse = (FULL * SCALE) / largest
 
     def move(b):
-        slot = slot_ref[b]
-        row = 3 * slot + scalar_div(slot, capacity + 1) * (stride - 3 * (capacity + 1))
+        row = row_ref[b]
         value = jnp.clip(jnp.round(vis_ref[b] * inverse), -FULL, FULL).astype(jnp.int32)
         for i, pair in enumerate([value, cell_ref[b], sub_ref[b]]):
             sent_ref[pl.ds(row + i, 1), :] = two_halves(pair[0:1], pair[1:2])
@@ -315,6 +315,7 @@
         in_specs=[HBM] * 5,
         out_specs=(VMEM, SMEM),
         scratch_shapes=[
+            pltpu.SMEM((blocks,), jnp.int32),
             pltpu.SMEM((blocks,), jnp.int32),
             pltpu.SMEM((blocks,), jnp.int32),
             pltpu.VMEM((blocks, 2, rows), jnp.float32),

time: 48.4 us -> 48.9 us (1.010)
  Pallas kernels: 11.1 us -> 17.7 us
  starting transfers between devices: 16.4 us -> 10.8 us
  blocking collectives: 16.3 us -> 15.6 us
  waiting for transfers between devices: 1.41 us -> 1.99 us
    pallas_call x1, Pallas kernels: 5.72 us -> 12.2 us  [body(): pl.pallas_call(lambda *refs: grid_kernel(pairs, capacity, *refs), out_sha...]
    all_to_all x1, starting transfers between devices: 9.23 us -> 3.39 us  [body(): lax.all_to_all(residual, 'tile', split_axis=0, concat_axis=0, tiled=True,...]
    all_gather x1, blocking collectives: 6.58 us -> 5.91 us  [body(): lax.all_gather(grid_sum.astype(jnp.bfloat16)[None], 'freq', axis=0, tiled...]
    ppermute x1, waiting for transfers between devices: 0.01 us -> 0.58 us  [body(): grid_sum = own + lax.ppermute(other, 'tile', swap).astype(jnp.float32)]
  transfers between devices with their start and end apart: 3 -> 3, of which waited for: 1 -> 2; matrix products, arithmetic and copies ran while one was open for 0% -> 0% of each run, Pallas kernels for 0% -> 0%
where the time goes in v18:
time: 48.9 us; the launch traced here: 48.4 us
  Pallas kernels  17.7 us (36%)
  blocking collectives  15.6 us (32%)
  starting transfers between devices  10.8 us (22%)
  waiting for transfers between devices  1.99 us (4%)
  local copies, waits for them, and re-layouts  1.55 us (3%)
  between operations  0.7 us (1%)
    pallas_call x1, Pallas kernels, body(): pl.pallas_call(lambda *refs: grid_kernel(pairs, capacity, *refs), out_sha...  12.2 us
    all_gather x1, blocking collectives, body(): lax.all_gather(model_grid[0], 'tile', axis=0, tiled=True, axis_index_grou...  9.71 us
    all_gather x1, blocking collectives, body(): lax.all_gather(grid_sum.astype(jnp.bfloat16)[None], 'freq', axis=0, tiled...  5.91 us
    all_to_all x1, starting transfers between devices, body(): lax.all_to_all(sent, 'tile', split_axis=0, concat_axis=0, tiled=True, axi...  5.27 us
    pallas_call x1, Pallas kernels, body(): pl.pallas_call(lambda *refs: pack_kernel(pairs, capacity, tiles_here, pla...  3.98 us
    all_to_all x1, starting transfers between devices, body(): lax.all_to_all(residual, 'tile', split_axis=0, concat_axis=0, tiled=True,...  3.39 us
    ppermute x1, starting transfers between devices, body(): grid_sum = own + lax.ppermute(other, 'tile', swap).astype(jnp.float32)  2.12 us
    pallas_call x1, Pallas kernels, body(): pl.pallas_call(finish_kernel, out_shape=(jax.ShapeDtypeStruct((blocks, 2,...  1.6 us
  transfers between devices with their start and end apart: 3, of which 2 were waited for; matrix products, arithmetic and copies ran while one was open for 0% of the time, Pallas kernels for 0%

profile of v18, /device:TPU:0, one launch (start us, length us, event | category | flops | bytes accessed | tf_op | source)
XLA Modules:
  0.0 48.4 jit_solution(539649301866301082)
XLA Ops:
  0.6 0.0 copy-start
  0.6 4.0 %pack_blocks.1 = (s32[1216,128]{1,0:T(8,128)}, s32[128]{0:T(128)}) custom-call(s32[128]{0:T(128)} %bitcast.26, s32[128]{0:T(128)} %bitcast.27, f32[128,2,128]{2,1,0:T(2,128)} %bitcast.22, s32[128,2,128]{2,1,0:T(2,128)} %bitcast.23, s32[128,2,128]{2,1,0:T(2,128)} %bitcast.24), custom_call_target="tpu_custom_call" | custom-call | tf_op jit(solution)/shard_map/pack_blocks/pallas_call | solution.py:309
  4.6 5.3 %all-to-all-start = ((s32[8,152,128]{2,1,0:T(8,128)}), s32[8,152,128]{2,1,0:T(8,128)S(1)}, u32[]{:S(2)}, u32[]{:S(2)}) async-start(s32[8,152,128]{2,1,0:T(8,128)} %bitcast.21), calls=%async_computation | async-start | bytes 1245184 | tf_op jit(solution)/shard_map/all_to_all | solution.py:333
  9.9 0.0 copy-start.2
  9.9 0.0 copy-start.1
  9.9 0.7 %copy-done.2 = bf16[16,8,8]{0,2,1:T(8,128)(2,1)S(1)} copy-done((bf16[16,8,8]{0,2,1:T(8,128)(2,1)S(1)}, bf16[16,8,8]{0,2,1:T(8,128)(2,1)}, u32[]{:S(2)}) %copy-start.2) | copy-done | bytes 2072
  10.6 0.1 copy.14.refs_2_
  10.7 0.1 copy-done.1
  10.8 9.7 %all-gather = bf16[1,4,128,256]{3,2,0,1:T(8,128)(2,1)S(1)} all-gather(bf16[1,2,128,256]{3,2,0,1:T(8,128)(2,1)S(1)} %bitcast.25), channel_id=2, replica_groups={{0,16},{2,18},{4,20},{6,22},{8,24},{10,26},{12,28},{14,30},{1,17},{3,19..., dimensions={1}, use_global_device_ids=true | all-gather | bytes 393216 | tf_op jit(solution)/shard_map/all_gather | solution.py:302
  20.5 0.0 copy-done
  20.5 0.0 copy-start.3
  20.5 0.6 %copy-done.3 = s32[128]{0:T(128)S(1)} copy-done((s32[128]{0:T(128)S(1)}, s32[128]{0:T(128)}, u32[]{:S(2)}) %copy-start.3) | copy-done | bytes 536
  21.2 1.4 %all-to-all-done = s32[8,152,128]{2,1,0:T(8,128)S(1)} async-done(((s32[8,152,128]{2,1,0:T(8,128)}), s32[8,152,128]{2,1,0:T(8,128)S(1)}, u32[]{:S(2)}, u32[]{:S(2)}) %all-to-all-start) | async-done | bytes 622624 | tf_op jit(solution)/shard_map/all_to_all | solution.py:333
  22.6 12.2 %grid_blocks.1 = (bf16[392,2,128]{2,1,0:T(2,128)(2,1)}, f32[2,256,128]{2,1,0:T(8,128)S(1)}, bf16[2,256,128]{2,1,0:T(8,128)(2,1)S(1)}) custom-call(s32[1]{0:T(128)} %bitcast.8.refs_0_, s32[1216,128]{1,0:T(8,128)S(1)} %bitcast.18, f32[24,128]{1,0:T(8,128)S(1)} %copy.14.refs_2_, bf16[4,128,256]{2,1,0:T(8,128)(2,1)S(1)} %bitcast.19), custom_call_target="tpu_custom_call" | custom-call | tf_op jit(solution)/shard_map/grid_blocks/pallas_call | solution.py:343
  34.8 2.1 %collective-permute-start = (bf16[2,256,128]{2,1,0:T(8,128)(2,1)S(1)}, bf16[2,256,128]{2,1,0:T(8,128)(2,1)S(1)}, u32[]{:S(2)}, u32[]{:S(2)}) collective-permute-start(bf16[2,256,128]{2,1,0:T(8,128)(2,1)S(1)} %get-tuple-element.19), channel_id=1, source_target_pairs={{0,16},{2,18},{4,20},{6,22},{8,24},{10,26},{12,28},{14,30},{16,0},... | collective-permute-start | bytes 393224 | tf_op jit(solution)/shard_map/ppermute | solution.py:371
  36.9 3.4 %all-to-all-start.1 = ((bf16[392,2,128]{2,1,0:T(2,128)(2,1)}), bf16[392,2,128]{2,1,0:T(2,128)(2,1)S(1)}, u32[]{:S(2)}, u32[]{:S(2)}) async-start(bf16[392,2,128]{2,1,0:T(2,128)(2,1)} %get-tuple-element.17), calls=%async_computation.1 | async-start | bytes 401408 | tf_op jit(solution)/shard_map/all_to_all | solution.py:368
  40.3 0.6 %collective-permute-done = bf16[2,256,128]{2,1,0:T(8,128)(2,1)S(1)} collective-permute-done((bf16[2,256,128]{2,1,0:T(8,128)(2,1)S(1)}, bf16[2,256,128]{2,1,0:T(8,128)(2,1)S(1)}, u32[]{:S(2)}, u32[]{:S(2)}) %collective-permute-start) | collective-permute-done | bytes 131104 | tf_op jit(solution)/shard_map/ppermute | solution.py:371
  40.9 5.9 %all-gather.1 = bf16[4,256,128]{2,1,0:T(8,128)(2,1)S(1)} all-gather(bf16[2,256,128]{2,1,0:T(8,128)(2,1)S(1)} %add_convert_fusion), channel_id=3, replica_groups=mesh['tile'=16,'freq'=2] {'freq'}, dimensions={0}, use_global_device_ids=true | all-gather | bytes 393216 | tf_op jit(solution)/shard_map/all_gather | solution.py:372
  46.8 0.0 all-to-all-done.1.returned_ref
  46.8 1.6 %finish.1 = (f32[128,2,128]{2,1,0:T(2,128)}, f32[2,128,256]{2,1,0:T(8,128)}) custom-call(f32[2]{0:T(128)S(1)} %dynamic-slice_bitcast_fusion.row_ref, s32[128]{0:T(128)S(1)} %broadcast_add_fusion.slot_ref, bf16[392,2,128]{2,1,0:T(2,128)(2,1)S(1)} %all-to-all-done.1.returned_ref, bf16[2,2,256,128]{3,2,1,0:T(8,128)(2,1)S(1)} %bitcast.20), custom_call_target="tpu_custom_call" | custom-call | tf_op jit(solution)/shard_map/finish/pallas_call | solution.py:373
  (5 shorter events, 0.1 us)
Async XLA Ops:
  0.6 19.9 %copy-start = (f32[2,2]{1,0:T(2,128)S(1)}, f32[2,2]{1,0:T(2,128)}, u32[]{:S(2)}) copy-start(f32[2,2]{1,0:T(2,128)} %param.15) | copy-start | bytes 52
  4.6 18.0 %all-to-all-start = ((s32[8,152,128]{2,1,0:T(8,128)}), s32[8,152,128]{2,1,0:T(8,128)S(1)}, u32[]{:S(2)}, u32[]{:S(2)}) async-start(s32[8,152,128]{2,1,0:T(8,128)} %bitcast.21), calls=%async_computation | async-start | bytes 1245184 | tf_op jit(solution)/shard_map/all_to_all | solution.py:333
  9.9 0.7 %copy-start.2 = (bf16[16,8,8]{0,2,1:T(8,128)(2,1)S(1)}, bf16[16,8,8]{0,2,1:T(8,128)(2,1)}, u32[]{:S(2)}) copy-start(bf16[16,8,8]{0,2,1:T(8,128)(2,1)} %param.14) | copy-start | bytes 6148
  9.9 0.9 %copy-start.1 = (bf16[1,2,128,256]{3,2,1,0:T(8,128)(2,1)S(1)}, bf16[1,2,128,256]{3,2,1,0:T(8,128)(2,1)}, u32[]{:S(2)}) copy-start(bf16[1,2,128,256]{3,2,1,0:T(8,128)(2,1)} %param.13) | copy-start | bytes 393220
  20.5 0.7 %copy-start.3 = (s32[128]{0:T(128)S(1)}, s32[128]{0:T(128)}, u32[]{:S(2)}) copy-start(s32[128]{0:T(128)} %get-tuple-element.12) | copy-start | bytes 1540
  34.8 6.1 %collective-permute-start = (bf16[2,256,128]{2,1,0:T(8,128)(2,1)S(1)}, bf16[2,256,128]{2,1,0:T(8,128)(2,1)S(1)}, u32[]{:S(2)}, u32[]{:S(2)}) collective-permute-start(bf16[2,256,128]{2,1,0:T(8,128)(2,1)S(1)} %get-tuple-element.19), channel_id=1, source_target_pairs={{0,16},{2,18},{4,20},{6,22},{8,24},{10,26},{12,28},{14,30},{16,0},... | collective-permute-start | bytes 393224 | tf_op jit(solution)/shard_map/ppermute | solution.py:371
  36.9 9.9 %all-to-all-start.1 = ((bf16[392,2,128]{2,1,0:T(2,128)(2,1)}), bf16[392,2,128]{2,1,0:T(2,128)(2,1)S(1)}, u32[]{:S(2)}, u32[]{:S(2)}) async-start(bf16[392,2,128]{2,1,0:T(2,128)(2,1)} %get-tuple-element.17), calls=%async_computation.1 | async-start | bytes 401408 | tf_op jit(solution)/shard_map/all_to_all | solution.py:368

commit v19 on v18

--- a/solution.py
+++ b/solution.py
@@ -7,7 +7,7 @@
 
 UNROLL = 2
 CHUNKS = 35
-AHEAD = 1
+AHEAD = 2
 BUFFERS = 5
 VMEM = pl.BlockSpec(memory_space=pltpu.VMEM)
 SMEM = pl.BlockSpec(memory_space=pltpu.SMEM)
@@ -39,11 +39,13 @@
     return (high << 16) | (low & 0xFFFF)
 
 
-def pack_kernel(pairs, capacity, tiles_here, planes, plane_hbm, tile_hbm, vis_hbm, cell_hbm, sub_hbm,
-                sent_ref, slot_ref, row_ref, plane_ref, tile_ref, vis_ref, cell_ref, sub_ref, about_ref, turned_ref,
-                count_ref, load_sem, about_sem):
+def pack_kernel(pairs, capacity, tiles_here, plane_hbm, tile_hbm, vis_hbm, cell_hbm, sub_hbm,
+                sent_ref, slot_ref, row_ref, plane_ref, tile_ref, vis_ref, cell_ref, sub_ref, code_ref,
+                count_ref, load_sem):
     blocks = tile_ref.shape[0]
     stride = rows_per_source(capacity)
+    tiles = 2 * tiles_here
+    lane = lax.broadcasted_iota(jnp.int32, (1, 128), 1)
     loads = [
         pltpu.make_async_copy(source, target, load_sem.at[i])
         for i, (source, target) in enumerate(
@@ -58,10 +60,9 @@
     ]
     for copy in loads:
         copy.start()
-    for d in range(pairs):
-        for t in range(2 * tiles_here):
-            count_ref[d * 2 * tiles_here + t] = 0
-    for copy in loads[:2]:
+    for key in range(pairs * tiles):
+        count_ref[key] = 0
+    for copy in loads:
         copy.wait()
 
     def assign(b):
@@ -70,50 +71,51 @@
         high = (owner >= pairs).astype(jnp.int32)
         pair = owner - high * pairs
         local = tile - (owner - high) * tiles_here
-        key = pair * (2 * tiles_here) + local
+        key = pair * tiles + local
         rank = count_ref[key]
         count_ref[key] = rank + 1
         place = first_slot(local, rank, capacity)
         slot_ref[b] = pair * (capacity + 1) + place
         row_ref[b] = pair * stride + 3 * place
-        about_ref[pair, 0, place] = plane_ref[b] << PLANE_SHIFT
-
-    def each(work):
-        def step(turn, carry):
-            for which in range(8):
-                work(turn * 8 + which)
-            return carry
-
-        lax.fori_loop(0, blocks // 8, step, 0)
-
-    each(assign)
-    for d in range(pairs):
-        for t in range(2 * tiles_here):
-            about_ref[d, 1, t] = count_ref[d * 2 * tiles_here + t]
-    turn_about = pltpu.make_async_copy(about_ref, turned_ref, about_sem)
-    turn_about.start()
-    for copy in loads[2:]:
-        copy.wait()
-    largest = jnp.max(jnp.max(jnp.abs(vis_ref[...]), axis=0), keepdims=True)
+        codes = code_ref[pl.ds(pair, 1), :]
+        code_ref[pl.ds(pair, 1), :] = jnp.where(lane == place, plane_ref[b] << PLANE_SHIFT, codes)
+
+    largest = jnp.max(jnp.max(jnp.abs(vis_ref[...]), axis=0, keepdims=True), axis=1, keepdims=True)
     largest = jnp.maximum(jnp.ceil(largest * SCALE), 1.0)
     inverse = (FULL * SCALE) / largest
 
-    def move(b):
-        row = row_ref[b]
-        value = jnp.clip(jnp.round(vis_ref[b] * inverse), -FULL, FULL).astype(jnp.int32)
-        for i, pair in enumerate([value, cell_ref[b], sub_ref[b]]):
-            sent_ref[pl.ds(row + i, 1), :] = two_halves(pair[0:1], pair[1:2])
-
-    each(move)
-    turn_about.wait()
-    lane = lax.broadcasted_iota(jnp.int32, (1, 128), 1)
+    def move(four):
+        rows = pl.ds(pl.multiple_of(8 * four, 8), 8)
+        value = jnp.clip(jnp.round(vis_ref[rows, :] * inverse), -FULL, FULL).astype(jnp.int32)
+        words = [
+            two_halves(parts, pltpu.roll(parts, 7, 0))
+            for parts in [value, cell_ref[rows, :], sub_ref[rows, :]]
+        ]
+        for u in range(4):
+            row = row_ref[4 * four + u]
+            for i, word in enumerate(words):
+                sent_ref[pl.ds(row + i, 1), :] = word[2 * u : 2 * u + 1]
+
+    def step(turn, carry):
+        for which in range(8):
+            assign(8 * turn + 8 + which)
+        move(2 * turn)
+        move(2 * turn + 1)
+        return carry
+
+    for which in range(8):
+        assign(which)
+    lax.fori_loop(0, blocks // 8 - 1, step, 0)
+    move(blocks // 4 - 2)
+    move(blocks // 4 - 1)
     for d in range(pairs):
+        counts = jnp.broadcast_to(largest.astype(jnp.int32), (1, 128))
+        for t in range(tiles):
+            counts = jnp.where(lane == t, count_ref[d * tiles + t], counts)
         row = d * stride + 3 * capacity
-        sent_ref[row : row + 1, :] = turned_ref[d, 0:1, :]
+        sent_ref[row : row + 1, :] = code_ref[d : d + 1, :]
         sent_ref[row + 1 : row + 2, :] = jnp.zeros((1, 128), jnp.int32)
-        sent_ref[row + 2 : row + 3, :] = jnp.where(
-            lane < 2 * tiles_here, turned_ref[d, 1:2, :], largest.astype(jnp.int32)
-        )
+        sent_ref[row + 2 : row + 3, :] = counts
 
 
 def finish_kernel(row_ref, slot_ref, returned_ref, grid_ref, residual_ref, coupled_ref):
@@ -307,7 +309,7 @@
         axis_index_groups=[[t, t + pairs] for t in range(pairs)],
     )
     sent, slot = pl.pallas_call(
-        lambda *refs: pack_kernel(pairs, capacity, tiles_here, planes, *refs),
+        lambda *refs: pack_kernel(pairs, capacity, tiles_here, *refs),
         out_shape=(
             jax.ShapeDtypeStruct((pairs * rows_per_source(capacity), rows), jnp.int32),
             jax.ShapeDtypeStruct((blocks,), jnp.int32),
@@ -318,18 +320,20 @@
             pltpu.SMEM((blocks,), jnp.int32),
             pltpu.SMEM((blocks,), jnp.int32),
             pltpu.SMEM((blocks,), jnp.int32),
-            pltpu.VMEM((blocks, 2, rows), jnp.float32),
-            pltpu.VMEM((blocks, 2, rows), jnp.int32),
-            pltpu.VMEM((blocks, 2, rows), jnp.int32),
-            pltpu.SMEM((pairs, 2, rows), jnp.int32),
-            pltpu.VMEM((pairs, 2, rows), jnp.int32),
+            pltpu.VMEM((2 * blocks, rows), jnp.float32),
+            pltpu.VMEM((2 * blocks, rows), jnp.int32),
+            pltpu.VMEM((2 * blocks, rows), jnp.int32),
+            pltpu.VMEM((pairs, rows), jnp.int32),
             pltpu.SMEM((pairs * 2 * tiles_here,), jnp.int32),
             pltpu.SemaphoreType.DMA((5,)),
-            pltpu.SemaphoreType.DMA,
         ],
         compiler_params=WHOLE_PARAMS,
         name="pack_blocks",
-    )(w_plane[0], block_tile[0], visibilities[0], uv_cell[0], sub_pixel[0])
+    )(
+        w_plane[0],
+        block_tile[0],
+        *[array.reshape(2 * blocks, rows) for array in (visibilities, uv_cell, sub_pixel)],
+    )
     got = lax.all_to_all(
         sent, "tile", split_axis=0, concat_axis=0, tiled=True, axis_index_groups=halves
     )

time: 48.9 us -> 47.9 us (0.980)
  Pallas kernels: 17.7 us -> 17 us
    pallas_call x1, Pallas kernels: 3.98 us -> 3.4 us  [body(): pl.pallas_call(lambda *refs: pack_kernel(pairs, capacity, tiles_here, *re...]
where the time goes in v19:
time: 47.9 us; the launch traced here: 47.4 us
  Pallas kernels  17 us (35%)
  blocking collectives  15.6 us (33%)
  starting transfers between devices  10.6 us (22%)
  waiting for transfers between devices  2.02 us (4%)
  local copies, waits for them, and re-layouts  1.55 us (3%)
  between operations  0.7 us (1%)
    pallas_call x1, Pallas kernels, body(): pl.pallas_call(lambda *refs: grid_kernel(pairs, capacity, *refs), out_sha...  12 us
    all_gather x1, blocking collectives, body(): lax.all_gather(model_grid[0], 'tile', axis=0, tiled=True, axis_index_grou...  9.71 us
    all_gather x1, blocking collectives, body(): lax.all_gather(grid_sum.astype(jnp.bfloat16)[None], 'freq', axis=0, tiled...  5.87 us
    all_to_all x1, starting transfers between devices, body(): lax.all_to_all(sent, 'tile', split_axis=0, concat_axis=0, tiled=True, axi...  5.27 us
    pallas_call x1, Pallas kernels, body(): pl.pallas_call(lambda *refs: pack_kernel(pairs, capacity, tiles_here, *re...  3.4 us
    all_to_all x1, starting transfers between devices, body(): lax.all_to_all(residual, 'tile', split_axis=0, concat_axis=0, tiled=True,...  3.39 us
    ppermute x1, starting transfers between devices, body(): grid_sum = own + lax.ppermute(other, 'tile', swap).astype(jnp.float32)  1.92 us
    pallas_call x1, Pallas kernels, body(): pl.pallas_call(finish_kernel, out_shape=(jax.ShapeDtypeStruct((blocks, 2,...  1.6 us
  transfers between devices with their start and end apart: 3, of which 2 were waited for; matrix products, arithmetic and copies ran while one was open for 0% of the time, Pallas kernels for 0%

profile of v19, /device:TPU:0, one launch (start us, length us, event | category | flops | bytes accessed | tf_op | source)
XLA Modules:
  0.0 47.4 jit_solution(5939853009041001170)
XLA Ops:
  0.6 0.0 copy-start
  0.6 3.4 %pack_blocks.1 = (s32[1216,128]{1,0:T(8,128)}, s32[128]{0:T(128)}) custom-call(s32[128]{0:T(128)} %bitcast.26, s32[128]{0:T(128)} %bitcast.27, f32[256,128]{1,0:T(8,128)} %bitcast.22, s32[256,128]{1,0:T(8,128)} %bitcast.23, s32[256,128]{1,0:T(8,128)} %bitcast.24), custom_call_target="tpu_custom_call" | custom-call | tf_op jit(solution)/shard_map/pack_blocks/pallas_call | solution.py:311
  4.0 5.3 %all-to-all-start = ((s32[8,152,128]{2,1,0:T(8,128)}), s32[8,152,128]{2,1,0:T(8,128)S(1)}, u32[]{:S(2)}, u32[]{:S(2)}) async-start(s32[8,152,128]{2,1,0:T(8,128)} %bitcast.21), calls=%async_computation | async-start | bytes 1245184 | tf_op jit(solution)/shard_map/all_to_all | solution.py:337
  9.3 0.0 copy-start.2
  9.3 0.0 copy-start.1
  9.3 0.7 %copy-done.2 = bf16[16,8,8]{0,2,1:T(8,128)(2,1)S(1)} copy-done((bf16[16,8,8]{0,2,1:T(8,128)(2,1)S(1)}, bf16[16,8,8]{0,2,1:T(8,128)(2,1)}, u32[]{:S(2)}) %copy-start.2) | copy-done | bytes 2072
  10.1 0.1 copy.14.refs_2_
  10.1 0.1 copy-done.1
  10.2 9.7 %all-gather = bf16[1,4,128,256]{3,2,0,1:T(8,128)(2,1)S(1)} all-gather(bf16[1,2,128,256]{3,2,0,1:T(8,128)(2,1)S(1)} %bitcast.25), channel_id=2, replica_groups={{0,16},{2,18},{4,20},{6,22},{8,24},{10,26},{12,28},{14,30},{1,17},{3,19..., dimensions={1}, use_global_device_ids=true | all-gather | bytes 393216 | tf_op jit(solution)/shard_map/all_gather | solution.py:304
  19.9 0.0 copy-done
  20.0 0.0 copy-start.3
  20.0 0.6 %copy-done.3 = s32[128]{0:T(128)S(1)} copy-done((s32[128]{0:T(128)S(1)}, s32[128]{0:T(128)}, u32[]{:S(2)}) %copy-start.3) | copy-done | bytes 536
  20.6 1.4 %all-to-all-done = s32[8,152,128]{2,1,0:T(8,128)S(1)} async-done(((s32[8,152,128]{2,1,0:T(8,128)}), s32[8,152,128]{2,1,0:T(8,128)S(1)}, u32[]{:S(2)}, u32[]{:S(2)}) %all-to-all-start) | async-done | bytes 622624 | tf_op jit(solution)/shard_map/all_to_all | solution.py:337
  22.0 12.0 %grid_blocks.1 = (bf16[392,2,128]{2,1,0:T(2,128)(2,1)}, f32[2,256,128]{2,1,0:T(8,128)S(1)}, bf16[2,256,128]{2,1,0:T(8,128)(2,1)S(1)}) custom-call(s32[1]{0:T(128)} %bitcast.8.refs_0_, s32[1216,128]{1,0:T(8,128)S(1)} %bitcast.18, f32[24,128]{1,0:T(8,128)S(1)} %copy.14.refs_2_, bf16[4,128,256]{2,1,0:T(8,128)(2,1)S(1)} %bitcast.19), custom_call_target="tpu_custom_call" | custom-call | tf_op jit(solution)/shard_map/grid_blocks/pallas_call | solution.py:347
  34.0 1.9 %collective-permute-start = (bf16[2,256,128]{2,1,0:T(8,128)(2,1)S(1)}, bf16[2,256,128]{2,1,0:T(8,128)(2,1)S(1)}, u32[]{:S(2)}, u32[]{:S(2)}) collective-permute-start(bf16[2,256,128]{2,1,0:T(8,128)(2,1)S(1)} %get-tuple-element.19), channel_id=1, source_target_pairs={{0,16},{2,18},{4,20},{6,22},{8,24},{10,26},{12,28},{14,30},{16,0},... | collective-permute-start | bytes 393224 | tf_op jit(solution)/shard_map/ppermute | solution.py:375
  35.9 3.4 %all-to-all-start.1 = ((bf16[392,2,128]{2,1,0:T(2,128)(2,1)}), bf16[392,2,128]{2,1,0:T(2,128)(2,1)S(1)}, u32[]{:S(2)}, u32[]{:S(2)}) async-start(bf16[392,2,128]{2,1,0:T(2,128)(2,1)} %get-tuple-element.17), calls=%async_computation.1 | async-start | bytes 401408 | tf_op jit(solution)/shard_map/all_to_all | solution.py:372
  39.3 0.6 %collective-permute-done = bf16[2,256,128]{2,1,0:T(8,128)(2,1)S(1)} collective-permute-done((bf16[2,256,128]{2,1,0:T(8,128)(2,1)S(1)}, bf16[2,256,128]{2,1,0:T(8,128)(2,1)S(1)}, u32[]{:S(2)}, u32[]{:S(2)}) %collective-permute-start) | collective-permute-done | bytes 131104 | tf_op jit(solution)/shard_map/ppermute | solution.py:375
  40.0 5.9 %all-gather.1 = bf16[4,256,128]{2,1,0:T(8,128)(2,1)S(1)} all-gather(bf16[2,256,128]{2,1,0:T(8,128)(2,1)S(1)} %add_convert_fusion), channel_id=3, replica_groups=mesh['tile'=16,'freq'=2] {'freq'}, dimensions={0}, use_global_device_ids=true | all-gather | bytes 393216 | tf_op jit(solution)/shard_map/all_gather | solution.py:376
  45.8 0.0 all-to-all-done.1.returned_ref
  45.8 1.6 %finish.1 = (f32[128,2,128]{2,1,0:T(2,128)}, f32[2,128,256]{2,1,0:T(8,128)}) custom-call(f32[2]{0:T(128)S(1)} %dynamic-slice_bitcast_fusion.row_ref, s32[128]{0:T(128)S(1)} %broadcast_add_fusion.slot_ref, bf16[392,2,128]{2,1,0:T(2,128)(2,1)S(1)} %all-to-all-done.1.returned_ref, bf16[2,2,256,128]{3,2,1,0:T(8,128)(2,1)S(1)} %bitcast.20), custom_call_target="tpu_custom_call" | custom-call | tf_op jit(solution)/shard_map/finish/pallas_call | solution.py:377
  (5 shorter events, 0.1 us)
Async XLA Ops:
  0.6 19.3 %copy-start = (f32[2,2]{1,0:T(2,128)S(1)}, f32[2,2]{1,0:T(2,128)}, u32[]{:S(2)}) copy-start(f32[2,2]{1,0:T(2,128)} %param.15) | copy-start | bytes 52
  4.0 18.0 %all-to-all-start = ((s32[8,152,128]{2,1,0:T(8,128)}), s32[8,152,128]{2,1,0:T(8,128)S(1)}, u32[]{:S(2)}, u32[]{:S(2)}) async-start(s32[8,152,128]{2,1,0:T(8,128)} %bitcast.21), calls=%async_computation | async-start | bytes 1245184 | tf_op jit(solution)/shard_map/all_to_all | solution.py:337
  9.3 0.7 %copy-start.2 = (bf16[16,8,8]{0,2,1:T(8,128)(2,1)S(1)}, bf16[16,8,8]{0,2,1:T(8,128)(2,1)}, u32[]{:S(2)}) copy-start(bf16[16,8,8]{0,2,1:T(8,128)(2,1)} %param.14) | copy-start | bytes 6148
  9.3 0.9 %copy-start.1 = (bf16[1,2,128,256]{3,2,1,0:T(8,128)(2,1)S(1)}, bf16[1,2,128,256]{3,2,1,0:T(8,128)(2,1)}, u32[]{:S(2)}) copy-start(bf16[1,2,128,256]{3,2,1,0:T(8,128)(2,1)} %param.13) | copy-start | bytes 393220
  20.0 0.7 %copy-start.3 = (s32[128]{0:T(128)S(1)}, s32[128]{0:T(128)}, u32[]{:S(2)}) copy-start(s32[128]{0:T(128)} %get-tuple-element.12) | copy-start | bytes 1540
  34.0 5.9 %collective-permute-start = (bf16[2,256,128]{2,1,0:T(8,128)(2,1)S(1)}, bf16[2,256,128]{2,1,0:T(8,128)(2,1)S(1)}, u32[]{:S(2)}, u32[]{:S(2)}) collective-permute-start(bf16[2,256,128]{2,1,0:T(8,128)(2,1)S(1)} %get-tuple-element.19), channel_id=1, source_target_pairs={{0,16},{2,18},{4,20},{6,22},{8,24},{10,26},{12,28},{14,30},{16,0},... | collective-permute-start | bytes 393224 | tf_op jit(solution)/shard_map/ppermute | solution.py:375
  35.9 9.9 %all-to-all-start.1 = ((bf16[392,2,128]{2,1,0:T(2,128)(2,1)}), bf16[392,2,128]{2,1,0:T(2,128)(2,1)S(1)}, u32[]{:S(2)}, u32[]{:S(2)}) async-start(bf16[392,2,128]{2,1,0:T(2,128)(2,1)} %get-tuple-element.17), calls=%async_computation.1 | async-start | bytes 401408 | tf_op jit(solution)/shard_map/all_to_all | solution.py:372
